TPU v7x, 32 devices: a whole 2x2x4 slice. The times are simulated.
32 devices in a mesh: grp: 2 (over x), band: 16 (over z, y, core).
Axes of the slice: x: 2, y: 2, z: 4, core: 2. Of those that a mesh axis runs over, the one named last changes fastest.
Arguments:
- node_lat: bfloat16 [8192, 256], P(('grp', 'band')), parts along dimension 0, may hold values from -6 to 6
- edge_lat: bfloat16 [163840, 256], P(('grp', 'band')), parts along dimension 0, may hold values from -6 to 6
- node_cot: bfloat16 [8192, 256], P(('grp', 'band')), parts along dimension 0, may hold values from -6 to 6
- edge_cot: bfloat16 [163840, 256], P(('grp', 'band')), parts along dimension 0, may hold values from -6 to 6
- w_edge_in: bfloat16 [768, 256], replicated, may hold values from -0.21875 to 0.21875
- w_edge_out: bfloat16 [256, 256], replicated, may hold values from -0.375 to 0.375
- gain_edge: float32 [256], replicated, may hold values from 0.25 to 1.75
- w_node_in: bfloat16 [512, 256], replicated, may hold values from -0.25 to 0.25
- w_node_out: bfloat16 [256, 256], replicated, may hold values from -0.375 to 0.375
- gain_node: float32 [256], replicated, may hold values from 0.25 to 1.75
- fetch_idx: int32 [16, 16, 32], P('band'), may hold values from 0 to 255
- edge_slot: int32 [81920], P('band'), may hold values from 0 to 511
- edge_recv: int32 [81920], P('band'), may hold values from 0 to 255
- block_fill: int32 [16, 40], P('band'), may hold values from 1 to 128, 3840 in all within a row
Outputs:
- node_grad: float32 [8192, 256], P(('grp', 'band')), parts along dimension 0
- edge_grad: bfloat16 [163840, 256], P(('grp', 'band')), parts along dimension 0
- w_edge_in_grad: float32 [1536, 256], P('grp'), parts along dimension 0
- w_edge_out_grad: float32 [512, 256], P('grp'), parts along dimension 0
- gain_edge_grad: float32 [512], P('grp'), parts along dimension 0
- w_node_in_grad: float32 [1024, 256], P('grp'), parts along dimension 0
- w_node_out_grad: float32 [512, 256], P('grp'), parts along dimension 0
- gain_node_grad: float32 [512], P('grp'), parts along dimension 0
There are 2 independent parts, one for each index of `grp`. A program takes and returns all parts, laid end to end along the dimension named above; an argument that names none is the same for every part. Nothing has to cross between parts.
Inputs may be any that keep to these rules, and one draw needn't show every extreme that they name: `fetch_idx`: entries of one list may repeat; every entry of every list is a real node. `block_fill`: the blocks of one patch hold 3840 live edges together, and some block is full.
All inputs are finite; a program needn't handle non-finite values.
Results may differ from a plain program's by a relative error of at most 0.0075.
Values may be sent and summed in bfloat16 or wider, within the bound.
No kernel may reach another device: no remote copies, remote signals or barrier semaphores. Data moves between devices by JAX's collectives and lax.ppermute only.
A program may use at most 192 MiB of HBM per device.

v0:
```python
import jax
import jax.numpy as jnp
from jax import lax
from jax.sharding import PartitionSpec as P

epsilon = 1e-05


def swish(values):
    return values * jax.nn.sigmoid(values)


def swish_slope(values):
    logistic = jax.nn.sigmoid(values)
    return logistic * (1.0 + values * (1.0 - logistic))


def normalize(values):
    centred = values - jnp.mean(values, axis=-1, keepdims=True)
    scale_inv = lax.rsqrt(jnp.mean(centred * centred, axis=-1, keepdims=True) + epsilon)
    return (centred * scale_inv, scale_inv)


def normalize_back(incoming, normed, scale_inv, gain_vec):
    scaled = incoming * gain_vec
    return scale_inv * (
        scaled
        - jnp.mean(scaled, axis=-1, keepdims=True)
        - normed * jnp.mean(scaled * normed, axis=-1, keepdims=True)
    )


def matmul(lhs_mat, rhs_mat):
    return jnp.dot(lhs_mat, rhs_mat, preferred_element_type=jnp.float32)


def patch_backward(
    node_own,
    senders,
    edge_own,
    recv_rows,
    valid,
    node_cotan,
    edge_cotan,
    w_edge_in,
    w_edge_out,
    gain_edge,
    w_node_in,
    w_node_out,
    gain_node,
):
    latent = node_own.shape[1]
    node_count = node_own.shape[0]
    receivers = node_own[recv_rows]
    stacked = jnp.concatenate([edge_own, senders, receivers], axis=1)
    pre_edge = matmul(stacked, w_edge_in)
    hidden_edge = swish(pre_edge).astype(jnp.bfloat16)
    out_edge = matmul(hidden_edge, w_edge_out)
    normed_edge, inv_edge = normalize(out_edge)
    valid_col = valid[:, None]
    update = normed_edge * gain_edge * valid_col
    summed = jax.ops.segment_sum(update, recv_rows, num_segments=node_count).astype(jnp.bfloat16)
    node_input = jnp.concatenate([node_own, summed], axis=1)
    pre_node = matmul(node_input, w_node_in)
    hidden_node = swish(pre_node).astype(jnp.bfloat16)
    out_node = matmul(hidden_node, w_node_out)
    normed_node, inv_node = normalize(out_node)
    node_base = node_cotan.astype(jnp.float32)
    gain_node_grad = jnp.sum(node_base * normed_node, axis=0)
    grad_out_node = normalize_back(node_base, normed_node, inv_node, gain_node).astype(jnp.bfloat16)
    w_node_out_grad = matmul(hidden_node.T, grad_out_node)
    grad_pre_node = (matmul(grad_out_node, w_node_out.T) * swish_slope(pre_node)).astype(
        jnp.bfloat16
    )
    w_node_in_grad = matmul(node_input.T, grad_pre_node)
    grad_node_input = matmul(grad_pre_node, w_node_in.T)
    grad_summed = grad_node_input[:, latent:]
    edge_base = edge_cotan.astype(jnp.float32)
    grad_update = edge_base + grad_summed[recv_rows]
    gain_edge_grad = jnp.sum(grad_update * normed_edge * valid_col, axis=0)
    grad_out_edge = (
        normalize_back(grad_update, normed_edge, inv_edge, gain_edge) * valid_col
    ).astype(jnp.bfloat16)
    w_edge_out_grad = matmul(hidden_edge.T, grad_out_edge)
    grad_pre_edge = (matmul(grad_out_edge, w_edge_out.T) * swish_slope(pre_edge)).astype(
        jnp.bfloat16
    )
    w_edge_in_grad = matmul(stacked.T, grad_pre_edge)
    grad_stacked = matmul(grad_pre_edge, w_edge_in.T)
    edge_result = (edge_base + grad_stacked[:, :latent]).astype(jnp.bfloat16)
    node_local = (
        node_base
        + grad_node_input[:, :latent]
        + jax.ops.segment_sum(grad_stacked[:, 2 * latent :], recv_rows, num_segments=node_count)
    )
    weight_terms = (
        w_edge_in_grad,
        w_edge_out_grad,
        gain_edge_grad,
        w_node_in_grad,
        w_node_out_grad,
        gain_node_grad,
    )
    return (edge_result, node_local, grad_stacked[:, latent : 2 * latent], weight_terms)


def per_device(
    node_lat,
    edge_lat,
    node_cot,
    edge_cot,
    w_edge_in,
    w_edge_out,
    gain_edge,
    w_node_in,
    w_node_out,
    gain_node,
    fetch_idx,
    edge_slot,
    edge_recv,
    block_fill,
):
    band_count = lax.axis_size("band")
    node_count = node_lat.shape[0]
    latent = node_lat.shape[1]
    capacity = fetch_idx.shape[2]
    wanted = fetch_idx[0]
    asked = lax.all_to_all(wanted, "band", split_axis=0, concat_axis=0, tiled=True)
    gathered = lax.all_gather(node_lat, "band", axis=0, tiled=True)
    offsets = (jnp.arange(band_count, dtype=jnp.int32) * node_count)[:, None]
    fetched = gathered[(wanted + offsets).reshape(-1)]
    senders = fetched[edge_slot]
    valid = (
        (jnp.arange(128, dtype=jnp.int32)[None, :] < block_fill[0][:, None])
        .reshape(-1)
        .astype(jnp.float32)
    )
    edge_result, node_local, grad_send, weight_terms = patch_backward(
        node_lat,
        senders,
        edge_lat,
        edge_recv,
        valid,
        node_cot,
        edge_cot,
        w_edge_in,
        w_edge_out,
        gain_edge,
        w_node_in,
        w_node_out,
        gain_node,
    )
    slot_grads = jax.ops.segment_sum(
        grad_send, edge_slot, num_segments=band_count * capacity
    ).reshape(band_count, capacity, latent)
    returned = lax.all_to_all(
        slot_grads.astype(jnp.bfloat16), "band", split_axis=0, concat_axis=0, tiled=True
    ).astype(slot_grads.dtype)
    node_grad = node_local + jax.ops.segment_sum(
        returned.reshape(-1, latent), asked.reshape(-1), num_segments=node_count
    )
    summed_terms = lax.psum(
        (
            weight_terms[0],
            weight_terms[1],
            weight_terms[2],
            weight_terms[3],
            weight_terms[4],
            weight_terms[5],
        ),
        "band",
    )
    return (
        node_grad,
        edge_result,
        summed_terms[0],
        summed_terms[1],
        summed_terms[2],
        summed_terms[3],
        summed_terms[4],
        summed_terms[5],
    )


def solution(mesh):
    in_specs = (
        P(("grp", "band"), None),
        P(("grp", "band"), None),
        P(("grp", "band"), None),
        P(("grp", "band"), None),
        P(),
        P(),
        P(),
        P(),
        P(),
        P(),
        P("band", None, None),
        P("band"),
        P("band"),
        P("band", None),
    )
    out_specs = (
        P(("grp", "band"), None),
        P(("grp", "band"), None),
        P("grp", None),
        P("grp", None),
        P("grp"),
        P("grp", None),
        P("grp", None),
        P("grp"),
    )
    return jax.shard_map(
        per_device, mesh=mesh, in_specs=in_specs, out_specs=out_specs, check_vma=False
    )
```

profile of v0, /device:TPU:0, one launch (start us, length us, event | category | flops | bytes accessed | tf_op | source)
XLA Modules:
  0.0 350.7 jit_solution(8553826969501899956)
XLA Ops:
  7.9 7.4 %all-to-all-start = ((s32[16,1,32]{2,1,0:T(1,128)}), s32[16,1,32]{2,1,0:T(1,128)S(1)}, u32[]{:S(2)}, u32[]{:S(2)}) async-start(s32[16,1,32]{2,1,0:T(1,128)} %bitcast.36), calls=%async_computation | async-start | bytes 16384 | tf_op jit(solution)/shard_map/all_to_all | solution.py:128
  19.7 3.6 %constant_dynamic-update-slice_fusion.2 = bf16[5120,768]{1,0:T(8,128)(2,1)} fusion(bf16[5120,256]{1,0:T(8,128)(2,1)} %param.15), kind=kLoop, calls=%fused_computation.65 | loop fusion | bytes 5242880
  23.3 18.2 %gather_fusion.2 = bf16[5120,256]{1,0:T(8,128)(2,1)S(1)} fusion(bf16[256,256]{1,0:T(8,128)(2,1)S(1)} %copy-done.1, s32[5120]{0:T(1024)S(1)} %fusion.24), kind=kCustom, calls=%fused_computation.2 | custom fusion | bytes 5263360 | tf_op jit(solution)/shard_map/gather | solution.py:54
  41.7 4.5 %copy.42 = bf16[5120,256]{0,1:T(8,128)(2,1)} copy(bf16[5120,256]{1,0:T(8,128)(2,1)} %param.17) | data formatting | bytes 5242880 | tf_op args[3]
  47.5 6.9 %all-gather.2.cloned.1.call-done = bf16[4096,256]{1,0:T(8,128)(2,1)} async-done(((bf16[256,256]{1,0:T(8,128)(2,1)}), bf16[4096,256]{1,0:T(8,128)(2,1)}) %all-gather.2.cloned.1.call-update) | async-done | bytes 2097168 | tf_op jit(solution)/shard_map/all_gather | solution.py:129
  54.3 3.4 gather_fusion
  57.7 22.8 %gather_fusion.1 = bf16[5120,256]{1,0:T(8,128)(2,1)} fusion(bf16[512,256]{1,0:T(8,128)(2,1)S(1)} %gather_fusion, s32[5120]{0:T(1024)} %fusion.23), kind=kCustom, calls=%fused_computation.1 | custom fusion | bytes 5263360 | tf_op jit(solution)/shard_map/gather | solution.py:132
  80.6 3.5 constant_dynamic-update-slice_fusion.1
  85.8 7.8 %multiply_convert_fusion.1 = (bf16[5120,256]{1,0:T(8,128)(2,1)S(1)}, f32[5120,256]{1,0:T(8,128)}) fusion(bf16[5120,768]{1,0:T(8,128)(2,1)} %constant_dynamic-update-slice_fusion, bf16[768,256]{1,0:T(8,128)(2,1)S(1)} %copy-done), kind=kOutput, calls=%fused_computation.22 | convolution fusion | flops 2019819520 | bytes 16121856 | tf_op jit(solution)/shard_map/dot_general | solution.py:34
  100.7 5.9 %copy.40 = f32[5120,256]{1,0:T(8,128)} copy(f32[5120,256]{0,1:T(8,128)} %multiply_multiply_fusion) | data formatting | bytes 10485760 | tf_op jit(solution)/shard_map/mul | solution.py:61
  106.7 28.5 %scatter_custom_fusion = f32[256,256]{1,0:T(8,128)S(1)} fusion(s32[5120]{0:T(1024)} %param.26, f32[5120,256]{1,0:T(8,128)} %copy.40, f32[]{:T(128)} %constant.8.clone.1), kind=kCustom, calls=%fused_computation.50 | custom fusion | flops 1310720 | bytes 262656 | tf_op jit(solution)/shard_map/scatter-add | solution.py:62
  139.4 20.0 %gather_fusion.3 = f32[5120,256]{1,0:T(8,128)} fusion(f32[256,256]{1,0:T(8,128)S(1)} %get-tuple-element.44, s32[5120]{0:T(1024)S(1)} %copy-done.15), kind=kCustom, calls=%fused_computation.3 | custom fusion | bytes 10506240 | tf_op jit(solution)/shard_map/gather | solution.py:79
  159.4 6.0 %copy.43 = f32[5120,256]{0,1:T(8,128)} copy(f32[5120,256]{1,0:T(8,128)} %gather_fusion.3) | data formatting | bytes 10485760 | tf_op jit(solution)/shard_map/gather | solution.py:79
  165.4 6.3 %multiply_reduce_fusion = (f32[256]{0:T(256)S(1)}, f32[5120]{0:T(1024)S(1)}, f32[5120]{0:T(1024)S(1)}) fusion(f32[5120,256]{0,1:T(8,128)} %copy-done.2, f32[5120]{0:T(1024)S(1)} %copy-done.12, f32[5120]{0:T(1024)S(1)} %add_rsqrt_fusion, f32[5120]{0:T(1024)S(1)} %broadcast_multiply_fusion.2, f32[5120,256]{0,1:T(8,128)} %copy.43, bf16[5120,256]{0,1:T(8,128)(2,1)} %copy.42, ...), kind=kLoop, calls=%fused_computation.17 | loop fusion | flops 14407424 | bytes 13211648 | tf_op jit(solution)/shard_map/reduce_sum | solution.py:80
  185.3 5.5 %copy-done.3 = f32[5120,768]{1,0:T(8,128)} copy-done((f32[5120,768]{1,0:T(8,128)}, f32[5120,768]{1,0:T(8,128)S(1)}, u32[]{:S(2)}) %copy-start.3) | copy-done | bytes 15728664
  193.4 29.0 %scatter_custom_fusion.2 = f32[512,256]{1,0:T(8,128)S(1)} fusion(s32[5120]{0:T(1024)} %param.25, f32[5120,768]{1,0:T(8,128)} %copy-done.3, f32[]{:T(128)} %constant.8.clone.1), kind=kCustom, calls=%fused_computation.13 | custom fusion | flops 1310720 | bytes 5767680 | tf_op jit(solution)/shard_map/scatter-add | solution.py:153
  222.4 6.0 %copy.48 = f32[5120,256]{0,1:T(8,128)} copy(f32[5120,256]{1,0:T(8,128)} %slice.32) | data formatting | bytes 10485760
  229.2 3.5 %all-to-all-start.1 = ((bf16[16,32,256]{2,1,0:T(8,128)(2,1)}), bf16[16,32,256]{2,1,0:T(8,128)(2,1)S(1)}, u32[]{:S(2)}, u32[]{:S(2)}) async-start(bf16[16,32,256]{2,1,0:T(8,128)(2,1)} %bitcast.34), calls=%async_computation.1 | async-start | bytes 524288 | tf_op jit(solution)/shard_map/all_to_all | solution.py:156
  233.5 4.7 %fusion.1 = bf16[5120,256]{0,1:T(8,128)(2,1)} fusion(f32[5120,256]{0,1:T(8,128)} %copy.48, bf16[5120,256]{0,1:T(8,128)(2,1)S(1)} %copy-done.6), kind=kLoop, calls=%fused_computation.12 | loop fusion | flops 3932160 | bytes 10485760 | tf_op jit(solution)/shard_map/convert_element_type | solution.py:90
  238.2 4.4 %copy.46 = bf16[5120,256]{1,0:T(8,128)(2,1)} copy(bf16[5120,256]{0,1:T(8,128)(2,1)} %fusion.1) | data formatting | bytes 5242880
  242.9 28.8 %scatter_custom_fusion.1 = f32[256,256]{1,0:T(8,128)S(1)} fusion(f32[256,256]{1,0:T(8,128)S(1)} %copy.44, s32[5120]{0:T(1024)} %param.26, f32[5120,768]{1,0:T(8,128)} %copy-done.3), kind=kCustom, calls=%fused_computation.15 | custom fusion | flops 1310720 | bytes 5505024 | tf_op jit(solution)/shard_map/scatter-add | solution.py:94
  271.7 34.4 %all-reduce = (f32[256]{0:T(256)}, f32[256]{0:T(256)}) all-reduce(f32[256]{0:T(256)S(1)} %get-tuple-element.32, f32[256]{0:T(256)S(1)} %get-tuple-element.35), channel_id=1, replica_groups=mesh['grp'=2,'band'=16] {'band'}, use_global_device_ids=true, to_apply=%region_15.0 | all-reduce | flops 512 | bytes 4096 | tf_op jit(solution)/shard_map/psum | solution.py:162
  306.1 3.4 scatter_custom_fusion.3
  310.3 26.3 %all-reduce.4.cloned.1.call-done = (f32[768,256]{1,0:T(8,128)}, f32[256,256]{1,0:T(8,128)}, f32[512,256]{1,0:T(8,128)}, f32[256,256]{1,0:T(8,128)}) async-done(((f32[768,256]{1,0:T(8,128)}, f32[256,256]{1,0:T(8,128)}, f32[512,256]{1,0:T(8,128)}, f32[256,256]{1,0:T(8,128)}), (f32[768,256]{1,0:T(8,128)}, f32[256,256]{1,0:T(8,128)}, f32[512,256]{1,0:T(8,128)}, ...) | async-done | bytes 1835024 | tf_op jit(solution)/shard_map/psum | solution.py:162
  (112 shorter events, 45.3 us)
Async XLA Ops:
  7.2 78.7 %copy-start = (bf16[768,256]{1,0:T(8,128)(2,1)S(1)}, bf16[768,256]{1,0:T(8,128)(2,1)}, u32[]{:S(2)}) copy-start(bf16[768,256]{1,0:T(8,128)(2,1)} %param.18) | copy-start | bytes 1179652
  7.2 16.1 %copy-start.1 = (bf16[256,256]{1,0:T(8,128)(2,1)S(1)}, bf16[256,256]{1,0:T(8,128)(2,1)}, u32[]{:S(2)}) copy-start(bf16[256,256]{1,0:T(8,128)(2,1)} %param.14) | copy-start | bytes 393220
  7.2 47.1 %all-gather.2.cloned.1.call-start = ((), (), s32[]{:S(2)}) async-start(), calls=%async_computation.2 | async-start | bytes 2228224 | tf_op jit(solution)/shard_map/all_gather | solution.py:129
  7.9 38.3 %all-to-all-start = ((s32[16,1,32]{2,1,0:T(1,128)}), s32[16,1,32]{2,1,0:T(1,128)S(1)}, u32[]{:S(2)}, u32[]{:S(2)}) async-start(s32[16,1,32]{2,1,0:T(1,128)} %bitcast.36), calls=%async_computation | async-start | bytes 16384 | tf_op jit(solution)/shard_map/all_to_all | solution.py:128
  18.4 23.1 %copy-start.14 = (s32[5120]{0:T(1024)}, s32[5120]{0:T(1024)S(1)}, u32[]{:S(2)}) copy-start(s32[5120]{0:T(1024)S(1)} %fusion.24) | copy-start | bytes 61444
  23.3 18.2 %copy-start.17 = (bf16[256,256]{1,0:T(8,128)(2,1)S(1)}, bf16[256,256]{1,0:T(8,128)(2,1)}, u32[]{:S(2)}) copy-start(bf16[256,256]{1,0:T(8,128)(2,1)} %param.16) | copy-start | bytes 393220
  41.6 94.4 %copy-start.9 = (bf16[256,256]{0,1:T(8,128)(2,1)}, bf16[256,256]{0,1:T(8,128)(2,1)S(1)}, u32[]{:S(2)}) copy-start(bf16[256,256]{0,1:T(8,128)(2,1)S(1)} %copy.39) | copy-start | bytes 393220
  85.8 7.8 %copy-start.16 = (bf16[256,256]{1,0:T(8,128)(2,1)S(1)}, bf16[256,256]{1,0:T(8,128)(2,1)}, u32[]{:S(2)}) copy-start(bf16[256,256]{1,0:T(8,128)(2,1)} %param.19) | copy-start | bytes 393220
  100.7 34.5 %copy-start.13 = (bf16[512,256]{1,0:T(8,128)(2,1)S(1)}, bf16[512,256]{1,0:T(8,128)(2,1)}, u32[]{:S(2)}) copy-start(bf16[512,256]{1,0:T(8,128)(2,1)} %param.21) | copy-start | bytes 786436
  100.7 34.8 %copy-start.18 = (bf16[256,256]{1,0:T(8,128)(2,1)S(1)}, bf16[256,256]{1,0:T(8,128)(2,1)}, u32[]{:S(2)}) copy-start(bf16[256,256]{1,0:T(8,128)(2,1)} %param.22) | copy-start | bytes 393220
  100.7 35.1 %copy-start.20 = (f32[256]{0:T(256)S(1)}, f32[256]{0:T(256)}, u32[]{:S(2)}) copy-start(f32[256]{0:T(256)} %param.23) | copy-start | bytes 3076
  106.7 32.8 %copy-start.15 = (s32[5120]{0:T(1024)S(1)}, s32[5120]{0:T(1024)}, u32[]{:S(2)}) copy-start(s32[5120]{0:T(1024)} %copy-done.14) | copy-start | bytes 61444
  159.4 12.4 %slice-start = ((s8[5242880]{0:T(1024)(128)(4,1)}), s8[1048576]{0:T(1024)(128)(4,1)S(1)}, s32[]{:S(2)}) async-start(s8[5242880]{0:T(1024)(128)(4,1)} %bitcast.30), calls=%async_computation.4 | async-start | bytes 2097152
  165.4 6.4 %slice-start.1 = ((s8[5242880]{0:T(1024)(128)(4,1)}), s8[4194304]{0:T(1024)(128)(4,1)S(1)}, s32[]{:S(2)}) async-start(s8[5242880]{0:T(1024)(128)(4,1)} %bitcast.30), calls=%async_computation.5 | async-start | bytes 8388608
  165.4 7.6 %copy-start.4 = (f32[5120,256]{0,1:T(8,128)S(1)}, f32[5120,256]{0,1:T(8,128)}, u32[]{:S(2)}) copy-start(f32[5120,256]{0,1:T(8,128)} %copy.43) | copy-start | bytes 15728644
  165.4 8.3 %copy-start.5 = (bf16[5120,256]{0,1:T(8,128)(2,1)S(1)}, bf16[5120,256]{0,1:T(8,128)(2,1)}, u32[]{:S(2)}) copy-start(bf16[5120,256]{0,1:T(8,128)(2,1)} %copy.42) | copy-start | bytes 7864324
  165.4 11.9 %slice-start.4 = ((s8[5242880]{0:T(1024)(128)(4,1)}), s8[4194304]{0:T(1024)(128)(4,1)S(1)}, s32[]{:S(2)}) async-start(s8[5242880]{0:T(1024)(128)(4,1)} %bitcast.39), calls=%async_computation.8 | async-start | bytes 8388608
  175.7 4.2 %slice-start.2 = ((s8[7864320]{0:T(1024)(128)(4,1)}), s8[4194304]{0:T(1024)(128)(4,1)S(1)}, s32[]{:S(2)}) async-start(s8[7864320]{0:T(1024)(128)(4,1)} %bitcast.32), calls=%async_computation.6 | async-start | bytes 8388608
  185.3 5.5 %copy-start.3 = (f32[5120,768]{1,0:T(8,128)}, f32[5120,768]{1,0:T(8,128)S(1)}, u32[]{:S(2)}) copy-start(f32[5120,768]{1,0:T(8,128)S(1)} %fusion.31) | copy-start | bytes 47185924
  222.4 11.1 %copy-start.6 = (bf16[5120,256]{0,1:T(8,128)(2,1)S(1)}, bf16[5120,256]{0,1:T(8,128)(2,1)}, u32[]{:S(2)}) copy-start(bf16[5120,256]{0,1:T(8,128)(2,1)} %copy.42) | copy-start | bytes 7864324
  229.2 76.9 %all-to-all-start.1 = ((bf16[16,32,256]{2,1,0:T(8,128)(2,1)}), bf16[16,32,256]{2,1,0:T(8,128)(2,1)S(1)}, u32[]{:S(2)}, u32[]{:S(2)}) async-start(bf16[16,32,256]{2,1,0:T(8,128)(2,1)} %bitcast.34), calls=%async_computation.1 | async-start | bytes 524288 | tf_op jit(solution)/shard_map/all_to_all | solution.py:156
  232.7 103.9 %all-reduce.4.cloned.1.call-start = ((), (), s32[]{:S(2)}) async-start(), calls=%async_computation.3 | async-start | bytes 3670016 | tf_op jit(solution)/shard_map/psum | solution.py:162
  238.2 4.4 %copy-start.11 = (f32[256,256]{1,0:T(8,128)S(1)}, f32[256,256]{1,0:T(8,128)}, u32[]{:S(2)}) copy-start(f32[256,256]{1,0:T(8,128)} %get-tuple-element.45) | copy-start | bytes 786436
  238.2 4.6 %copy-start.10 = (bf16[256,256]{0,1:T(8,128)(2,1)S(1)}, bf16[256,256]{0,1:T(8,128)(2,1)}, u32[]{:S(2)}) copy-start(bf16[256,256]{0,1:T(8,128)(2,1)} %copy-done.9) | copy-start | bytes 393220
  (7 other events, 16.5 us)
Sparse Core Ops, SparseCore 0:
  10.2 44.0 all-gather.1
  238.0 98.5 all-reduce.3
where the time goes:
time: 352 us; the launch traced here: 351 us
  local copies, waits for them, and re-layouts  122 us (35%)
  other arithmetic  113 us (32%)
  waiting for transfers between devices  34.6 us (10%)
  blocking collectives  34.4 us (10%)
  matrix products  21.2 us (6%)
  between operations  14.5 us (4%)
  starting transfers between devices  11 us (3%)
    unnamed x65, local copies, waits for them, and re-layouts  39.3 us
    psum x1, blocking collectives, per_device(): lax.psum((weight_terms[0], weight_terms[1], weight_terms[2], weight_terms...  34.4 us
    scatter-add x1, other arithmetic, per_device(): jax.ops.segment_sum(grad_send, edge_slot, num_segments=band_count * capac...  29 us
    scatter-add x1, other arithmetic, patch_backward(): jax.ops.segment_sum(grad_stacked[:, 2 * latent:], recv_rows, num_segments...  28.8 us
    scatter-add x1, other arithmetic, patch_backward(): jax.ops.segment_sum(update, recv_rows, num_segments=node_count)  28.5 us
    psum x1, waiting for transfers between devices, per_device(): lax.psum((weight_terms[0], weight_terms[1], weight_terms[2], weight_terms...  26.3 us
    gather x2, local copies, waits for them, and re-layouts, patch_backward(): grad_update = edge_base + grad_summed[recv_rows]  25.9 us
    gather x1, local copies, waits for them, and re-layouts, per_device(): senders = fetched[edge_slot]  22.8 us
  transfers between devices with their start and end apart: 4, of which 2 were waited for; matrix products, arithmetic and copies ran while one was open for 21% of the time, Pallas kernels for 0%

commit v1 on v0

v1 whole, which is shorter than its diff:
```python
import functools

import jax
import jax.numpy as jnp
from jax import lax
from jax.experimental import pallas as pl
from jax.experimental.pallas import tpu as pltpu
from jax.sharding import PartitionSpec as P

epsilon = 1e-05
CHUNK = 512
VMEM_LIMIT = 60 * 2**20
BF = jnp.bfloat16
F32 = jnp.float32


def dot(lhs, rhs, lhs_dim, rhs_dim):
    return lax.dot_general(
        lhs, rhs, (((lhs_dim,), (rhs_dim,)), ((), ())), preferred_element_type=F32
    )


def swish_and_slope(values):
    logistic = jax.nn.sigmoid(values)
    hidden = values * logistic
    return hidden, logistic + hidden * (1.0 - logistic)


def onehot_rows(row_count, index_row):
    rows = lax.broadcasted_iota(jnp.int32, (row_count, index_row.shape[1]), 0)
    return (rows == index_row).astype(BF)


def vmem():
    return pl.BlockSpec(memory_space=pltpu.VMEM)


def whole(shape):
    return pl.BlockSpec(shape, lambda *_: (0,) * len(shape))


def serve_kernel(asked_ref, node_ref, rows_ref):
    picks = onehot_rows(node_ref.shape[0], asked_ref[...])
    rows_ref[...] = dot(picks, node_ref[...], 0, 0).astype(BF)


def serve(asked_row, node_lat):
    return pl.pallas_call(
        serve_kernel,
        out_shape=jax.ShapeDtypeStruct((asked_row.shape[1], node_lat.shape[1]), BF),
        in_specs=[vmem(), vmem()],
        out_specs=vmem(),
        name="serve_rows",
    )(asked_row, node_lat)


def prepare_kernel(
    edge_ref, cot_ref, recv_ref, slot_ref, node_ref, w_in_t_ref, part_ref, cot_t_ref, hot_ref, node_part
):
    latent = edge_ref.shape[1]
    nodes = node_ref.shape[0]
    slots = hot_ref.shape[1] - nodes

    @pl.when(pl.program_id(0) == 0)
    def _():
        node_part[...] = dot(w_in_t_ref[:, 2 * latent :], node_ref[...], 1, 1).astype(BF)

    recv_hot = onehot_rows(nodes, recv_ref[0])
    hot_ref[0, :nodes, :] = recv_hot
    hot_ref[0, nodes:, :] = onehot_rows(slots, slot_ref[0])
    part_ref[0] = (
        dot(w_in_t_ref[:, :latent], edge_ref[...], 1, 1) + dot(node_part[...], recv_hot, 1, 0)
    ).astype(BF)
    cot_t_ref[0] = cot_ref[...].T


def prepare(edge_lat, edge_cot, recv_rows, slot_rows, node_lat, w_edge_in_t, slots):
    edges, latent = edge_lat.shape
    hidden = w_edge_in_t.shape[0]
    nodes = node_lat.shape[0]
    chunks = edges // CHUNK
    rows = pl.BlockSpec((CHUNK, latent), lambda i: (i, 0))
    index = pl.BlockSpec((1, 1, CHUNK), lambda i: (i, 0, 0))

    def out(height):
        return pl.BlockSpec((1, height, CHUNK), lambda i: (i, 0, 0))

    return pl.pallas_call(
        prepare_kernel,
        grid=(chunks,),
        out_shape=[
            jax.ShapeDtypeStruct((chunks, hidden, CHUNK), BF),
            jax.ShapeDtypeStruct((chunks, latent, CHUNK), BF),
            jax.ShapeDtypeStruct((chunks, nodes + slots, CHUNK), BF),
        ],
        in_specs=[rows, rows, index, index, whole(node_lat.shape), whole(w_edge_in_t.shape)],
        out_specs=[out(hidden), out(latent), out(nodes + slots)],
        scratch_shapes=[pltpu.VMEM((hidden, nodes), BF)],
        compiler_params=pltpu.CompilerParams(vmem_limit_bytes=VMEM_LIMIT),
        cost_estimate=pl.CostEstimate(
            flops=4 * edges * latent * hidden, bytes_accessed=8 * edges * latent, transcendentals=0
        ),
        name="prepare_edges",
    )(edge_lat, edge_cot, recv_rows, slot_rows, node_lat, w_edge_in_t)


def layer_kernel(
    piece_rows,
    core_ref,
    part_hbm,
    cot_hbm,
    hot_hbm,
    edge_hbm,
    valid_ref,
    fetched_ref,
    node_ref,
    node_cot_ref,
    w_in_ref,
    w_in_t_ref,
    w_out_ref,
    w_out_t_ref,
    gain_edge_ref,
    w_node_in_ref,
    w_node_in_t_ref,
    w_node_out_ref,
    w_node_out_t_ref,
    gain_node_ref,
    grad_pre_hbm,
    node_local_ref,
    pack_ref,
    part,
    cot,
    hot,
    edge,
    hidden,
    slope,
    normed,
    scale,
    grad_pre,
    send_part,
    summed_acc,
    w_in_acc,
    w_out_acc,
    ends_acc,
    gain_acc,
    grad_summed,
    weight_pack,
    sems,
    out_sems,
):
    chunks, latent, width = part.shape
    nodes = node_ref.shape[0]
    slots = fetched_ref.shape[0]
    bands = pack_ref.shape[1] * 2
    cap = slots // bands

    def incoming(c):
        return (
            pltpu.make_async_copy(part_hbm.at[c], part.at[c], sems.at[0, c]),
            pltpu.make_async_copy(hot_hbm.at[c], hot.at[c], sems.at[1, c]),
        )

    def incoming_later(c):
        return (
            pltpu.make_async_copy(cot_hbm.at[c], cot.at[c], sems.at[2, c]),
            pltpu.make_async_copy(edge_hbm.at[c], edge.at[c], sems.at[3, c]),
        )

    for c in range(chunks):
        for copy in incoming(c):
            copy.start()
    for c in range(chunks):
        for copy in incoming_later(c):
            copy.start()

    send_part[...] = dot(w_in_t_ref[:, latent : 2 * latent], fetched_ref[...], 1, 1).astype(BF)
    summed_acc[...] = jnp.zeros_like(summed_acc)
    w_in_acc[...] = jnp.zeros_like(w_in_acc)
    w_out_acc[...] = jnp.zeros_like(w_out_acc)
    ends_acc[...] = jnp.zeros_like(ends_acc)
    gain_acc[...] = jnp.zeros_like(gain_acc)

    @pl.loop(0, chunks)
    def _(c):
        for copy in incoming(c):
            copy.wait()
        pre = part[c].astype(F32) + dot(send_part[...], hot[c, nodes:, :], 1, 0)
        hid, slo = swish_and_slope(pre)
        hid = hid.astype(BF)
        hidden[c] = hid
        slope[c] = slo.astype(BF)
        out = dot(w_out_t_ref[...], hid, 1, 0)
        centred = out - jnp.mean(out, axis=0, keepdims=True)
        inv = lax.rsqrt(jnp.mean(centred * centred, axis=0, keepdims=True) + epsilon)
        inv = inv * valid_ref[c]
        scale[c] = inv
        norm = (centred * inv).astype(BF)
        normed[c] = norm
        summed_acc[...] += dot(norm, hot[c, :nodes, :], 1, 1)

    node = node_ref[...]
    summed = (summed_acc[...] * gain_edge_ref[...]).astype(BF)
    pre_node = dot(w_node_in_t_ref[:, :latent], node, 1, 1) + dot(
        w_node_in_t_ref[:, latent:], summed, 1, 0
    )
    hid_node, slope_node = swish_and_slope(pre_node)
    hid_node = hid_node.astype(BF)
    out_node = dot(w_node_out_t_ref[...], hid_node, 1, 0)
    centred = out_node - jnp.mean(out_node, axis=0, keepdims=True)
    inv_node = lax.rsqrt(jnp.mean(centred * centred, axis=0, keepdims=True) + epsilon)
    norm_node = centred * inv_node
    node_base = node_cot_ref[...].astype(F32)
    cot_node = node_base.T
    product = cot_node * norm_node
    gain_node_grad = jnp.sum(product.T, axis=0, keepdims=True)
    dy = cot_node * gain_node_ref[...]
    grad_out_node = (
        inv_node
        * (
            dy
            - jnp.mean(dy, axis=0, keepdims=True)
            - norm_node * jnp.mean(dy * norm_node, axis=0, keepdims=True)
        )
    ).astype(BF)
    base = 4 * latent
    weight_pack[base + 2 * latent : base + 3 * latent, :] = dot(hid_node, grad_out_node, 1, 1)
    grad_pre_node = (dot(w_node_out_ref[...], grad_out_node, 1, 0) * slope_node).astype(BF)
    weight_pack[base : base + latent, :] = dot(node, grad_pre_node, 0, 1)
    weight_pack[base + latent : base + 2 * latent, :] = dot(summed, grad_pre_node, 1, 1)
    grad_summed[...] = dot(w_node_in_ref[latent:, :], grad_pre_node, 1, 0).astype(BF)
    node_local = node_base + dot(grad_pre_node, w_node_in_ref[:latent, :], 0, 1)

    @pl.loop(0, chunks)
    def _(c):
        for copy in incoming_later(c):
            copy.wait()
        grad_update = cot[c].astype(F32) + dot(grad_summed[...], hot[c, :nodes, :], 1, 0)
        norm = normed[c].astype(F32)
        product = grad_update * norm
        gain_acc[...] += product
        gain = gain_edge_ref[...]
        dy = grad_update * gain
        mean_dy = jnp.mean(dy, axis=0, keepdims=True)
        mean_product = jnp.mean(product * gain, axis=0, keepdims=True)
        grad_out = (scale[c] * (dy - mean_dy - norm * mean_product)).astype(BF)
        w_out_acc[...] += dot(hidden[c], grad_out, 1, 1)
        grad_hidden = dot(w_out_ref[...], grad_out, 1, 0)
        grad_in = (grad_hidden * slope[c].astype(F32)).astype(BF)
        grad_pre[c] = grad_in
        pltpu.make_async_copy(grad_pre.at[c], grad_pre_hbm.at[c], out_sems.at[c]).start()
        w_in_acc[...] += dot(grad_in, edge[c], 1, 0)
        ends_acc[...] += dot(grad_in, hot[c], 1, 1)

    recv_sum = ends_acc[:, :nodes].astype(BF)
    slot_sum = ends_acc[:, nodes:].astype(BF)
    node_local_ref[...] = node_local + dot(recv_sum, w_in_ref[2 * latent :, :], 0, 1)
    weight_pack[:latent, :] = w_in_acc[...].T
    weight_pack[latent : 2 * latent, :] = dot(fetched_ref[...], slot_sum, 0, 1)
    weight_pack[2 * latent : 3 * latent, :] = dot(node, recv_sum, 0, 1)
    weight_pack[3 * latent : 4 * latent, :] = w_out_acc[...]
    tail = base + 3 * latent
    weight_pack[tail:, :] = jnp.zeros_like(weight_pack[tail:, :])
    weight_pack[tail : tail + 1, :] = jnp.sum(gain_acc[...].T, axis=0, keepdims=True)
    weight_pack[tail + 1 : tail + 2, :] = gain_node_grad
    slot_grads = dot(slot_sum, w_in_ref[latent : 2 * latent, :], 0, 1).astype(BF)
    core = core_ref[0]
    for d in range(bands):
        side = core if d % 2 == 0 else 1 - core
        pack_ref[side, d // 2, :cap, :] = slot_grads[d * cap : (d + 1) * cap, :]
        pack_ref[side, d // 2, cap:, :] = weight_pack[
            d * piece_rows : (d + 1) * piece_rows, :
        ].astype(BF)
    for c in range(chunks):
        pltpu.make_async_copy(grad_pre.at[c], grad_pre_hbm.at[c], out_sems.at[c]).wait()


def layer(core, part, cot_t, hot, edge_lat, valid_rows, fetched, node_lat, node_cot, weights, bands):
    chunks, hidden, width = part.shape
    nodes, latent = node_lat.shape
    slots = fetched.shape[0]
    cap = slots // bands
    used = 7 * latent + 2
    piece_rows = -(-used // (bands * 16)) * 16
    edge_chunks = edge_lat.reshape(chunks, width, latent)
    hbm = pl.BlockSpec(memory_space=pl.ANY)
    return pl.pallas_call(
        functools.partial(layer_kernel, piece_rows),
        out_shape=[
            jax.ShapeDtypeStruct((chunks, hidden, width), BF),
            jax.ShapeDtypeStruct((nodes, latent), F32),
            jax.ShapeDtypeStruct((2, bands // 2, cap + piece_rows, latent), BF),
        ],
        in_specs=[pl.BlockSpec(memory_space=pltpu.SMEM)] + [hbm] * 4 + [vmem()] * 14,
        out_specs=[hbm, vmem(), vmem()],
        scratch_shapes=[
            pltpu.VMEM((chunks, hidden, width), BF),
            pltpu.VMEM((chunks, latent, width), BF),
            pltpu.VMEM((chunks, nodes + slots, width), BF),
            pltpu.VMEM((chunks, width, latent), BF),
            pltpu.VMEM((chunks, hidden, width), BF),
            pltpu.VMEM((chunks, hidden, width), BF),
            pltpu.VMEM((chunks, latent, width), BF),
            pltpu.VMEM((chunks, 1, width), F32),
            pltpu.VMEM((chunks, hidden, width), BF),
            pltpu.VMEM((hidden, slots), BF),
            pltpu.VMEM((latent, nodes), F32),
            pltpu.VMEM((hidden, latent), F32),
            pltpu.VMEM((hidden, latent), F32),
            pltpu.VMEM((hidden, nodes + slots), F32),
            pltpu.VMEM((latent, width), F32),
            pltpu.VMEM((latent, nodes), BF),
            pltpu.VMEM((piece_rows * bands, latent), F32),
            pltpu.SemaphoreType.DMA((4, chunks)),
            pltpu.SemaphoreType.DMA((chunks,)),
        ],
        compiler_params=pltpu.CompilerParams(vmem_limit_bytes=VMEM_LIMIT),
        name="layer_backward",
    )(core, part, cot_t, hot, edge_chunks, valid_rows, fetched, node_lat, node_cot, *weights)


def edge_kernel(grad_ref, cot_ref, w_in_ref, out_ref):
    latent = cot_ref.shape[1]
    back = dot(grad_ref[0], w_in_ref[:latent, :], 0, 1)
    out_ref[...] = (cot_ref[...].astype(F32) + back).astype(BF)


def edge_result(grad_pre, edge_cot, w_edge_in):
    chunks, hidden, width = grad_pre.shape
    latent = edge_cot.shape[1]
    rows = pl.BlockSpec((width, latent), lambda i: (i, 0))
    return pl.pallas_call(
        edge_kernel,
        grid=(chunks,),
        out_shape=jax.ShapeDtypeStruct(edge_cot.shape, BF),
        in_specs=[
            pl.BlockSpec((1, hidden, width), lambda i: (i, 0, 0)),
            rows,
            whole(w_edge_in.shape),
        ],
        out_specs=rows,
        compiler_params=pltpu.CompilerParams(vmem_limit_bytes=VMEM_LIMIT),
        cost_estimate=pl.CostEstimate(
            flops=2 * chunks * width * hidden * latent,
            bytes_accessed=6 * chunks * width * latent,
            transcendentals=0,
        ),
        name="edge_result",
    )(grad_pre, edge_cot, w_edge_in)


def join_kernel(cap, pack_ref, got_ref, out_ref):
    out_ref[:, :cap, :] = pack_ref[:, :cap, :]
    out_ref[:, cap : 2 * cap, :] = got_ref[:, :cap, :]
    out_ref[:, 2 * cap :, :] = (
        pack_ref[:, cap:, :].astype(F32) + got_ref[:, cap:, :].astype(F32)
    ).astype(BF)


def join(keep, got, cap):
    chips, height, latent = keep.shape
    return pl.pallas_call(
        functools.partial(join_kernel, cap),
        out_shape=jax.ShapeDtypeStruct((chips, height + cap, latent), BF),
        in_specs=[vmem(), vmem()],
        out_specs=vmem(),
        name="join_cores",
    )(keep, got)


def settle_kernel(cap, asked_ref, back_ref, local_ref, node_grad_ref, piece_ref):
    chips, height, latent = back_ref.shape
    rows = back_ref[:, : 2 * cap, :].reshape(chips * 2 * cap, latent)
    picks = onehot_rows(local_ref.shape[0], asked_ref[...])
    node_grad_ref[...] = local_ref[...] + dot(picks, rows, 1, 0)
    piece_ref[...] = jnp.sum(back_ref[:, 2 * cap :, :].astype(F32), axis=0).astype(BF)


def settle(asked_row, back, node_local, cap):
    chips, height, latent = back.shape
    return pl.pallas_call(
        functools.partial(settle_kernel, cap),
        out_shape=[
            jax.ShapeDtypeStruct(node_local.shape, F32),
            jax.ShapeDtypeStruct((height - 2 * cap, latent), BF),
        ],
        in_specs=[vmem()] * 3,
        out_specs=[vmem()] * 2,
        name="settle_sums",
    )(asked_row, back, node_local)


def per_device(
    node_lat,
    edge_lat,
    node_cot,
    edge_cot,
    w_edge_in,
    w_edge_out,
    gain_edge,
    w_node_in,
    w_node_out,
    gain_node,
    fetch_idx,
    edge_slot,
    edge_recv,
    block_fill,
):
    bands = lax.axis_size("band")
    chips = bands // 2
    me = lax.axis_index("band")
    core = me % 2
    latent = node_lat.shape[1]
    cap = fetch_idx.shape[2]
    slots = bands * cap
    chunks = edge_lat.shape[0] // CHUNK
    other_core = [(i, i ^ 1) for i in range(bands)]
    same_core = [[2 * i + c for i in range(chips)] for c in range(2)]

    asked = lax.all_to_all(fetch_idx[0], "band", split_axis=0, concat_axis=0, tiled=True)
    rows = serve(asked.reshape(1, slots), node_lat)
    fetched = lax.all_to_all(
        rows.reshape(bands, cap, latent), "band", split_axis=0, concat_axis=0, tiled=True
    ).reshape(slots, latent)

    valid = jnp.arange(128, dtype=jnp.int32)[None, :] < block_fill[0][:, None]
    valid = valid.reshape(chunks, 1, CHUNK)
    recv_rows = edge_recv.reshape(chunks, 1, CHUNK)
    slot_rows = edge_slot.reshape(chunks, 1, CHUNK)
    part, cot_t, hot = prepare(
        edge_lat, edge_cot, recv_rows, slot_rows, node_lat, w_edge_in.T, slots
    )
    weights = (
        w_edge_in,
        w_edge_in.T,
        w_edge_out,
        w_edge_out.T,
        gain_edge[:, None],
        w_node_in,
        w_node_in.T,
        w_node_out,
        w_node_out.T,
        gain_node[:, None],
    )
    grad_pre, node_local, pack = layer(
        core.reshape(1).astype(jnp.int32),
        part,
        cot_t,
        hot,
        edge_lat,
        valid.astype(F32),
        fetched,
        node_lat,
        node_cot,
        weights,
        bands,
    )
    got = lax.ppermute(pack[1], "band", other_core)
    joined = join(pack[0], got, cap)
    back = lax.all_to_all(
        joined, "band", split_axis=0, concat_axis=0, tiled=True, axis_index_groups=same_core
    )
    edge_grad = edge_result(grad_pre, edge_cot, w_edge_in)
    asked_pairs = asked.reshape(chips, 2, cap)
    asked_pairs = jnp.where(core == 0, asked_pairs, asked_pairs[:, ::-1, :])
    node_grad, piece = settle(asked_pairs.reshape(1, slots), back, node_local, cap)
    mine = lax.all_to_all(
        jnp.broadcast_to(piece[None], (chips,) + piece.shape),
        "band",
        split_axis=0,
        concat_axis=0,
        tiled=True,
        axis_index_groups=same_core,
    )
    theirs = lax.ppermute(mine, "band", other_core)
    both = jnp.where(
        core == 0, jnp.stack([mine, theirs], axis=1), jnp.stack([theirs, mine], axis=1)
    ).reshape(-1, latent)
    both = both.astype(F32)
    return (
        node_grad,
        edge_grad,
        both[: 3 * latent],
        both[3 * latent : 4 * latent],
        both[7 * latent],
        both[4 * latent : 6 * latent],
        both[6 * latent : 7 * latent],
        both[7 * latent + 1],
    )


def solution(mesh):
    in_specs = (
        P(("grp", "band"), None),
        P(("grp", "band"), None),
        P(("grp", "band"), None),
        P(("grp", "band"), None),
        P(),
        P(),
        P(),
        P(),
        P(),
        P(),
        P("band", None, None),
        P("band"),
        P("band"),
        P("band", None),
    )
    out_specs = (
        P(("grp", "band"), None),
        P(("grp", "band"), None),
        P("grp", None),
        P("grp", None),
        P("grp"),
        P("grp", None),
        P("grp", None),
        P("grp"),
    )
    return jax.shard_map(
        per_device, mesh=mesh, in_specs=in_specs, out_specs=out_specs, check_vma=False
    )
```

time: 352 us -> 139 us (0.39)
  other arithmetic: 113 us -> 2.76 us
  local copies, waits for them, and re-layouts: 122 us -> 20.7 us
  Pallas kernels: 0 us -> 50.5 us
  matrix products: 21.2 us -> 0 us
  between operations: 14.5 us -> 0.69 us
  waiting for transfers between devices: 34.6 us -> 21.6 us
    scatter-add x4 -> x0, other arithmetic: 89.7 us -> none  [the longest x1 29 us: per_device(): jax.ops.segment_sum(grad_send, edge_slot, num_segments=band_count * capac...]
    gather x5 -> x0, local copies, waits for them, and re-layouts: 70.4 us -> none  [the longest x2 25.9 us: patch_backward(): grad_update = edge_base + grad_summed[recv_rows]]
    pallas_call x0 -> x6, Pallas kernels: none -> 50.5 us  [the longest x1 24.5 us: layer(): pl.pallas_call(functools.partial(layer_kernel, piece_rows), out_shape=[ja...]
    psum x1 -> x0, blocking collectives: 34.4 us -> none  [per_device(): lax.psum((weight_terms[0], weight_terms[1], weight_terms[2], weight_terms...]
    all_to_all x0 -> x2, blocking collectives: none -> 31.8 us  [the longest x1 18.1 us: per_device(): lax.all_to_all(jnp.broadcast_to(piece[None], (chips,) + piece.shape), 'ba...]
    unnamed x65 -> x11, local copies, waits for them, and re-layouts: 39.3 us -> 9.96 us
    psum x1 -> x0, waiting for transfers between devices: 26.3 us -> none  [per_device(): lax.psum((weight_terms[0], weight_terms[1], weight_terms[2], weight_terms...]
    dot_general x12 -> x0, matrix products: 21.2 us -> none  [matmul(): return jnp.dot(lhs_mat, rhs_mat, preferred_element_type=jnp.float32)]
  transfers between devices with their start and end apart: 4 -> 4, of which waited for: 2 -> 2; matrix products, arithmetic and copies ran while one was open for 21% -> 9% of each run, Pallas kernels for 0% -> 14%
where the time goes in v1:
time: 139 us; the launch traced here: 138 us
  Pallas kernels  50.5 us (36%)
  blocking collectives  31.8 us (23%)
  waiting for transfers between devices  21.6 us (16%)
  local copies, waits for them, and re-layouts  20.7 us (15%)
  starting transfers between devices  9.68 us (7%)
  other arithmetic  2.76 us (2%)
    pallas_call x1, Pallas kernels, layer(): pl.pallas_call(functools.partial(layer_kernel, piece_rows), out_shape=[ja...  24.5 us
    all_to_all x1, waiting for transfers between devices, per_device(): lax.all_to_all(joined, 'band', split_axis=0, concat_axis=0, tiled=True, a...  19.8 us
    all_to_all x1, blocking collectives, per_device(): lax.all_to_all(jnp.broadcast_to(piece[None], (chips,) + piece.shape), 'ba...  18.1 us
    all_to_all x1, blocking collectives, per_device(): lax.all_to_all(fetch_idx[0], 'band', split_axis=0, concat_axis=0, tiled=T...  13.7 us
    pallas_call x1, Pallas kernels, prepare(): pl.pallas_call(prepare_kernel, grid=(chunks,), out_shape=[jax.ShapeDtypeS...  11.1 us
    unnamed x11, local copies, waits for them, and re-layouts  9.96 us
    pallas_call x1, Pallas kernels, edge_result(): pl.pallas_call(edge_kernel, grid=(chunks,), out_shape=jax.ShapeDtypeStruc...  8.52 us
    all_to_all x1, starting transfers between devices, per_device(): lax.all_to_all(joined, 'band', split_axis=0, concat_axis=0, tiled=True, a...  5.86 us
  transfers between devices with their start and end apart: 4, of which 2 were waited for; matrix products, arithmetic and copies ran while one was open for 9% of the time, Pallas kernels for 14%

profile of v1, /device:TPU:0, one launch (start us, length us, event | category | flops | bytes accessed | tf_op | source)
XLA Modules:
  0.0 137.7 jit_solution(4163800921553107309)
XLA Ops:
  0.6 13.7 %all_to_all.24 = s32[16,1,32]{2,1,0:T(1,128)S(1)} all-to-all(s32[16,1,32]{2,1,0:T(1,128)} %bitcast.55), channel_id=1, replica_groups=mesh['grp'=2,'band'=16] {'band'}, dimensions={0} | all-to-all | bytes 4096 | tf_op jit(solution)/shard_map/all_to_all | solution.py:419
  16.2 1.9 %serve_rows.1 = bf16[512,256]{1,0:T(8,128)(2,1)} custom-call(s32[1,512]{1,0:T(1,128)} %reshape.114.asked_ref, bf16[256,256]{1,0:T(8,128)(2,1)} %node_ref.5), custom_call_target="tpu_custom_call" | custom-call | tf_op jit(solution)/shard_map/serve_rows/pallas_call | solution.py:48
  18.1 3.5 %all-to-all-start.1 = ((bf16[16,32,256]{2,1,0:T(8,128)(2,1)}), bf16[16,32,256]{2,1,0:T(8,128)(2,1)S(1)}, u32[]{:S(2)}, u32[]{:S(2)}) async-start(bf16[16,32,256]{2,1,0:T(8,128)(2,1)} %bitcast.40), calls=%async_computation.1 | async-start | bytes 524288 | tf_op jit(solution)/shard_map/all_to_all | solution.py:421
  21.7 1.3 reduce.6
  23.1 1.5 %copy.36.gain_edge_ref = f32[256,1]{1,0:T(8,128)} copy(f32[256,1]{0,1:T(1,128)} %bitcast.56) | data formatting | bytes 2048 | tf_op jit(solution)/shard_map/broadcast_in_dim | solution.py:437
  24.5 1.5 %copy.37.gain_node_ref = f32[256,1]{1,0:T(8,128)} copy(f32[256,1]{0,1:T(1,128)} %bitcast.57) | data formatting | bytes 2048 | tf_op jit(solution)/shard_map/broadcast_in_dim | solution.py:442
  26.0 1.7 %copy.33 = bf16[256,256]{0,1:T(8,128)(2,1)} copy(bf16[256,256]{1,0:T(8,128)(2,1)} %w_out_ref.1) | data formatting | bytes 262144 | tf_op args[5]
  27.7 1.7 %copy.35 = bf16[256,256]{0,1:T(8,128)(2,1)} copy(bf16[256,256]{1,0:T(8,128)(2,1)} %w_node_out_ref.1) | data formatting | bytes 262144 | tf_op args[8]
  29.3 1.8 %copy.34 = bf16[512,256]{0,1:T(8,128)(2,1)} copy(bf16[512,256]{1,0:T(8,128)(2,1)} %w_node_in_ref.1) | data formatting | bytes 524288 | tf_op args[7]
  31.1 1.9 %copy.32 = bf16[768,256]{0,1:T(8,128)(2,1)} copy(bf16[768,256]{1,0:T(8,128)(2,1)} %w_in_ref.3) | data formatting | bytes 786432 | tf_op args[4]
  33.0 11.1 %prepare_edges.1 = (bf16[10,256,512]{2,1,0:T(8,128)(2,1)}, bf16[10,256,512]{2,1,0:T(8,128)(2,1)}, bf16[10,768,512]{2,1,0:T(8,128)(2,1)}) custom-call(bf16[5120,256]{1,0:T(8,128)(2,1)} %edge_ref.1, bf16[5120,256]{1,0:T(8,128)(2,1)} %cot_ref.3, s32[10,1,512]{2,1,0:T(1,128)} %bitcast.53, s32[10,1,512]{2,1,0:T(1,128)} %bitcast.54, bf16[256,256]{1,0:T(8,128)(2,1)} %node_ref.5, ...), custom_call_target="tpu_custom_call" | custom-call | flops 1342177280 | bytes 10485760 | tf_op jit(solution)/shard_map/prepare_edges/pallas_call | solution.py:88
  45.6 24.5 %layer_backward.1 = (bf16[10,256,512]{2,1,0:T(8,128)(2,1)}, f32[256,256]{1,0:T(8,128)}, bf16[2,8,160,256]{3,2,1,0:T(8,128)(2,1)}) custom-call(s32[1]{0:T(128)} %bitcast.2.core_ref, bf16[10,256,512]{2,1,0:T(8,128)(2,1)} %get-tuple-element.16.part_hbm, bf16[10,256,512]{2,1,0:T(8,128)(2,1)} %get-tuple-element.17.cot_hbm, ...), custom_call_target="tpu_custom_call" | custom-call | tf_op jit(solution)/shard_map/layer_backward/pallas_call | solution.py:286
  70.1 2.2 %slice_bitcast_fusion = (bf16[8,160,256]{2,1,0:T(8,128)(2,1)S(1)}, bf16[8,160,256]{2,1,0:T(8,128)(2,1)}) fusion(bf16[2,8,160,256]{3,2,1,0:T(8,128)(2,1)} %get-tuple-element.19), kind=kLoop, calls=%fused_computation.2 | loop fusion | bytes 2621440 | tf_op jit(solution)/shard_map/squeeze | solution.py:457
  72.5 1.8 %collective-permute-done.got_ref = bf16[8,160,256]{2,1,0:T(8,128)(2,1)S(1)} collective-permute-done((bf16[8,160,256]{2,1,0:T(8,128)(2,1)S(1)}, bf16[8,160,256]{2,1,0:T(8,128)(2,1)S(1)}, u32[]{:S(2)}, u32[]{:S(2)}) %collective-permute-start) | collective-permute-done | bytes 655392 | tf_op jit(solution)/shard_map/ppermute | solution.py:457
  75.2 2.3 %join_cores.1 = bf16[8,192,256]{2,1,0:T(8,128)(2,1)} custom-call(bf16[8,160,256]{2,1,0:T(8,128)(2,1)} %get-tuple-element.29.pack_ref, bf16[8,160,256]{2,1,0:T(8,128)(2,1)} %copy-done.2), custom_call_target="tpu_custom_call" | custom-call | tf_op jit(solution)/shard_map/join_cores/pallas_call | solution.py:361
  77.5 5.9 %all-to-all-start.2 = ((bf16[8,192,256]{2,1,0:T(8,128)(2,1)}), bf16[8,192,256]{2,1,0:T(8,128)(2,1)S(1)}, u32[]{:S(2)}, u32[]{:S(2)}) async-start(bf16[8,192,256]{2,1,0:T(8,128)(2,1)} %join_cores.1), calls=%async_computation.2 | async-start | bytes 1572864 | tf_op jit(solution)/shard_map/all_to_all | solution.py:459
  84.1 19.8 %all-to-all-done.2.back_ref = bf16[8,192,256]{2,1,0:T(8,128)(2,1)S(1)} async-done(((bf16[8,192,256]{2,1,0:T(8,128)(2,1)}), bf16[8,192,256]{2,1,0:T(8,128)(2,1)S(1)}, u32[]{:S(2)}, u32[]{:S(2)}) %all-to-all-start.2) | async-done | bytes 786464 | tf_op jit(solution)/shard_map/all_to_all | solution.py:459
  103.8 0.9 copy-done
  104.7 2.2 %settle_sums.1 = (f32[256,256]{1,0:T(8,128)}, bf16[128,256]{1,0:T(8,128)(2,1)}) custom-call(s32[1,512]{1,0:T(1,128)} %reshape.109.asked_ref, bf16[8,192,256]{2,1,0:T(8,128)(2,1)} %copy-done, f32[256,256]{1,0:T(8,128)} %get-tuple-element.20.local_ref), custom_call_target="tpu_custom_call" | custom-call | tf_op jit(solution)/shard_map/settle_sums/pallas_call | solution.py:380
  106.9 0.9 broadcast_in_dim.15
  107.8 18.1 %all_to_all.25 = bf16[8,128,256]{2,1,0:T(8,128)(2,1)S(1)} all-to-all(bf16[8,128,256]{2,1,0:T(8,128)(2,1)S(1)} %broadcast_in_dim.15), channel_id=1, replica_groups={{0,2,4,6,8,10,12,14},{1,3,5,7,9,11,13,15},{16,18,20,22,24,26,28,30},{17..., dimensions={0} | all-to-all | bytes 1048576 | tf_op jit(solution)/shard_map/all_to_all | solution.py:466
  125.8 8.5 %edge_result.1 = bf16[5120,256]{1,0:T(8,128)(2,1)} custom-call(bf16[10,256,512]{2,1,0:T(8,128)(2,1)} %get-tuple-element.22.grad_ref, bf16[5120,256]{1,0:T(8,128)(2,1)} %cot_ref.3, bf16[768,256]{1,0:T(8,128)(2,1)} %w_in_ref.3), custom_call_target="tpu_custom_call" | custom-call | flops 671088640 | bytes 7864320 | tf_op jit(solution)/shard_map/edge_result/pallas_call | solution.py:331
  134.5 0.8 slice.51
  136.2 0.9 slice.48
  (22 shorter events, 6.7 us)
Async XLA Ops:
  18.1 26.8 %all-to-all-start.1 = ((bf16[16,32,256]{2,1,0:T(8,128)(2,1)}), bf16[16,32,256]{2,1,0:T(8,128)(2,1)S(1)}, u32[]{:S(2)}, u32[]{:S(2)}) async-start(bf16[16,32,256]{2,1,0:T(8,128)(2,1)} %bitcast.40), calls=%async_computation.1 | async-start | bytes 524288 | tf_op jit(solution)/shard_map/all_to_all | solution.py:421
  44.9 0.7 copy-start.1
  72.3 2.1 %collective-permute-start = (bf16[8,160,256]{2,1,0:T(8,128)(2,1)S(1)}, bf16[8,160,256]{2,1,0:T(8,128)(2,1)S(1)}, u32[]{:S(2)}, u32[]{:S(2)}) collective-permute-start(bf16[8,160,256]{2,1,0:T(8,128)(2,1)S(1)} %get-tuple-element.28), channel_id=1, source_target_pairs={{0,1},{1,0},{2,3},{3,2},{4,5},{5,4},{6,7},{7,6},{8,9},{9,8},{10,11... | collective-permute-start | bytes 1966088 | tf_op jit(solution)/shard_map/ppermute | solution.py:457
  74.4 0.8 copy-start.2
  77.5 26.3 %all-to-all-start.2 = ((bf16[8,192,256]{2,1,0:T(8,128)(2,1)}), bf16[8,192,256]{2,1,0:T(8,128)(2,1)S(1)}, u32[]{:S(2)}, u32[]{:S(2)}) async-start(bf16[8,192,256]{2,1,0:T(8,128)(2,1)} %join_cores.1), calls=%async_computation.2 | async-start | bytes 1572864 | tf_op jit(solution)/shard_map/all_to_all | solution.py:459
  103.8 0.9 copy-start
  125.8 8.5 %collective-permute-start.1 = (bf16[8,128,256]{2,1,0:T(8,128)(2,1)S(1)}, bf16[8,128,256]{2,1,0:T(8,128)(2,1)S(1)}, u32[]{:S(2)}, u32[]{:S(2)}) collective-permute-start(bf16[8,128,256]{2,1,0:T(8,128)(2,1)S(1)} %all_to_all.25), channel_id=1, source_target_pairs={{0,1},{1,0},{2,3},{3,2},{4,5},{5,4},{6,7},{7,6},{8,9},{9,8},{10,11... | collective-permute-start | bytes 1572872 | tf_op jit(solution)/shard_map/ppermute | solution.py:474

commit v2 on v1

--- a/solution.py
+++ b/solution.py
@@ -40,22 +40,35 @@
 
 
 def serve_kernel(asked_ref, node_ref, rows_ref):
-    picks = onehot_rows(node_ref.shape[0], asked_ref[...])
-    rows_ref[...] = dot(picks, node_ref[...], 0, 0).astype(BF)
-
-
-def serve(asked_row, node_lat):
+    cap = asked_ref.shape[1]
+    node = node_ref[...]
+    for d in range(asked_ref.shape[0]):
+        picks = onehot_rows(node.shape[0], asked_ref[d : d + 1, :])
+        rows_ref[d * cap : (d + 1) * cap, :] = dot(picks, node, 0, 0).astype(BF)
+
+
+def serve(asked, node_lat):
     return pl.pallas_call(
         serve_kernel,
-        out_shape=jax.ShapeDtypeStruct((asked_row.shape[1], node_lat.shape[1]), BF),
+        out_shape=jax.ShapeDtypeStruct((asked.size, node_lat.shape[1]), BF),
         in_specs=[vmem(), vmem()],
         out_specs=vmem(),
         name="serve_rows",
-    )(asked_row, node_lat)
+    )(asked, node_lat)
 
 
 def prepare_kernel(
-    edge_ref, cot_ref, recv_ref, slot_ref, node_ref, w_in_t_ref, part_ref, cot_t_ref, hot_ref, node_part
+    edge_ref,
+    cot_ref,
+    recv_ref,
+    slot_ref,
+    node_ref,
+    w_in_ref,
+    part_ref,
+    cot_t_ref,
+    hot_ref,
+    node_part,
+    w_edge_t,
 ):
     latent = edge_ref.shape[1]
     nodes = node_ref.shape[0]
@@ -63,20 +76,19 @@
 
     @pl.when(pl.program_id(0) == 0)
     def _():
-        node_part[...] = dot(w_in_t_ref[:, 2 * latent :], node_ref[...], 1, 1).astype(BF)
+        node_part[...] = dot(w_in_ref[2 * latent :, :], node_ref[...], 0, 1).astype(BF)
+        w_edge_t[...] = w_in_ref[:latent, :].T
 
     recv_hot = onehot_rows(nodes, recv_ref[0])
     hot_ref[0, :nodes, :] = recv_hot
     hot_ref[0, nodes:, :] = onehot_rows(slots, slot_ref[0])
-    part_ref[0] = (
-        dot(w_in_t_ref[:, :latent], edge_ref[...], 1, 1) + dot(node_part[...], recv_hot, 1, 0)
-    ).astype(BF)
+    part_ref[0] = dot(w_edge_t[...], edge_ref[...], 1, 1) + dot(node_part[...], recv_hot, 1, 0)
     cot_t_ref[0] = cot_ref[...].T
 
 
-def prepare(edge_lat, edge_cot, recv_rows, slot_rows, node_lat, w_edge_in_t, slots):
+def prepare(edge_lat, edge_cot, recv_rows, slot_rows, node_lat, w_edge_in, slots):
     edges, latent = edge_lat.shape
-    hidden = w_edge_in_t.shape[0]
+    hidden = w_edge_in.shape[1]
     nodes = node_lat.shape[0]
     chunks = edges // CHUNK
     rows = pl.BlockSpec((CHUNK, latent), lambda i: (i, 0))
@@ -89,19 +101,19 @@
         prepare_kernel,
         grid=(chunks,),
         out_shape=[
-            jax.ShapeDtypeStruct((chunks, hidden, CHUNK), BF),
+            jax.ShapeDtypeStruct((chunks, hidden, CHUNK), F32),
             jax.ShapeDtypeStruct((chunks, latent, CHUNK), BF),
             jax.ShapeDtypeStruct((chunks, nodes + slots, CHUNK), BF),
         ],
-        in_specs=[rows, rows, index, index, whole(node_lat.shape), whole(w_edge_in_t.shape)],
+        in_specs=[rows, rows, index, index, whole(node_lat.shape), whole(w_edge_in.shape)],
         out_specs=[out(hidden), out(latent), out(nodes + slots)],
-        scratch_shapes=[pltpu.VMEM((hidden, nodes), BF)],
+        scratch_shapes=[pltpu.VMEM((hidden, nodes), BF), pltpu.VMEM((hidden, latent), BF)],
         compiler_params=pltpu.CompilerParams(vmem_limit_bytes=VMEM_LIMIT),
         cost_estimate=pl.CostEstimate(
             flops=4 * edges * latent * hidden, bytes_accessed=8 * edges * latent, transcendentals=0
         ),
         name="prepare_edges",
-    )(edge_lat, edge_cot, recv_rows, slot_rows, node_lat, w_edge_in_t)
+    )(edge_lat, edge_cot, recv_rows, slot_rows, node_lat, w_edge_in)
 
 
 def layer_kernel(
@@ -116,18 +128,15 @@
     node_ref,
     node_cot_ref,
     w_in_ref,
-    w_in_t_ref,
     w_out_ref,
-    w_out_t_ref,
     gain_edge_ref,
     w_node_in_ref,
-    w_node_in_t_ref,
     w_node_out_ref,
-    w_node_out_t_ref,
     gain_node_ref,
     grad_pre_hbm,
     node_local_ref,
-    pack_ref,
+    keep_hbm,
+    send_hbm,
     part,
     cot,
     hot,
@@ -145,13 +154,17 @@
     gain_acc,
     grad_summed,
     weight_pack,
+    w_out_t,
+    gain_column,
+    pack,
     sems,
     out_sems,
+    pack_sems,
 ):
     chunks, latent, width = part.shape
     nodes = node_ref.shape[0]
     slots = fetched_ref.shape[0]
-    bands = pack_ref.shape[1] * 2
+    bands = pack.shape[1] * 2
     cap = slots // bands
 
     def incoming(c):
@@ -173,7 +186,9 @@
         for copy in incoming_later(c):
             copy.start()
 
-    send_part[...] = dot(w_in_t_ref[:, latent : 2 * latent], fetched_ref[...], 1, 1).astype(BF)
+    send_part[...] = dot(w_in_ref[latent : 2 * latent, :], fetched_ref[...], 0, 1).astype(BF)
+    w_out_t[...] = w_out_ref[...].T
+    gain_column[...] = jnp.broadcast_to(gain_edge_ref[...], (128, latent)).T
     summed_acc[...] = jnp.zeros_like(summed_acc)
     w_in_acc[...] = jnp.zeros_like(w_in_acc)
     w_out_acc[...] = jnp.zeros_like(w_out_acc)
@@ -184,12 +199,12 @@
     def _(c):
         for copy in incoming(c):
             copy.wait()
-        pre = part[c].astype(F32) + dot(send_part[...], hot[c, nodes:, :], 1, 0)
+        pre = part[c] + dot(send_part[...], hot[c, nodes:, :], 1, 0)
         hid, slo = swish_and_slope(pre)
         hid = hid.astype(BF)
         hidden[c] = hid
         slope[c] = slo.astype(BF)
-        out = dot(w_out_t_ref[...], hid, 1, 0)
+        out = dot(w_out_t[...], hid, 1, 0)
         centred = out - jnp.mean(out, axis=0, keepdims=True)
         inv = lax.rsqrt(jnp.mean(centred * centred, axis=0, keepdims=True) + epsilon)
         inv = inv * valid_ref[c]
@@ -199,13 +214,13 @@
         summed_acc[...] += dot(norm, hot[c, :nodes, :], 1, 1)
 
     node = node_ref[...]
-    summed = (summed_acc[...] * gain_edge_ref[...]).astype(BF)
-    pre_node = dot(w_node_in_t_ref[:, :latent], node, 1, 1) + dot(
-        w_node_in_t_ref[:, latent:], summed, 1, 0
+    summed = (summed_acc[...] * gain_column[:, :1]).astype(BF)
+    pre_node = dot(w_node_in_ref[:latent, :], node, 0, 1) + dot(
+        w_node_in_ref[latent:, :], summed, 0, 0
     )
     hid_node, slope_node = swish_and_slope(pre_node)
     hid_node = hid_node.astype(BF)
-    out_node = dot(w_node_out_t_ref[...], hid_node, 1, 0)
+    out_node = dot(w_node_out_ref[...], hid_node, 0, 0)
     centred = out_node - jnp.mean(out_node, axis=0, keepdims=True)
     inv_node = lax.rsqrt(jnp.mean(centred * centred, axis=0, keepdims=True) + epsilon)
     norm_node = centred * inv_node
@@ -213,7 +228,7 @@
     cot_node = node_base.T
     product = cot_node * norm_node
     gain_node_grad = jnp.sum(product.T, axis=0, keepdims=True)
-    dy = cot_node * gain_node_ref[...]
+    dy = cot_node * jnp.broadcast_to(gain_node_ref[...], (128, latent)).T[:, :1]
     grad_out_node = (
         inv_node
         * (
@@ -238,7 +253,7 @@
         norm = normed[c].astype(F32)
         product = grad_update * norm
         gain_acc[...] += product
-        gain = gain_edge_ref[...]
+        gain = gain_column[:, :1]
         dy = grad_update * gain
         mean_dy = jnp.mean(dy, axis=0, keepdims=True)
         mean_product = jnp.mean(product * gain, axis=0, keepdims=True)
@@ -265,11 +280,21 @@
     slot_grads = dot(slot_sum, w_in_ref[latent : 2 * latent, :], 0, 1).astype(BF)
     core = core_ref[0]
     for d in range(bands):
-        side = core if d % 2 == 0 else 1 - core
-        pack_ref[side, d // 2, :cap, :] = slot_grads[d * cap : (d + 1) * cap, :]
-        pack_ref[side, d // 2, cap:, :] = weight_pack[
-            d * piece_rows : (d + 1) * piece_rows, :
-        ].astype(BF)
+        pack[d % 2, d // 2, :cap, :] = slot_grads[d * cap : (d + 1) * cap, :]
+        pack[d % 2, d // 2, cap:, :] = weight_pack[d * piece_rows : (d + 1) * piece_rows, :].astype(
+            BF
+        )
+    for own in range(2):
+
+        @pl.when(core == own)
+        def _():
+            keep = pltpu.make_async_copy(pack.at[own], keep_hbm, pack_sems.at[0])
+            send = pltpu.make_async_copy(pack.at[1 - own], send_hbm, pack_sems.at[1])
+            send.start()
+            keep.start()
+            send.wait()
+            keep.wait()
+
     for c in range(chunks):
         pltpu.make_async_copy(grad_pre.at[c], grad_pre_hbm.at[c], out_sems.at[c]).wait()
 
@@ -288,12 +313,13 @@
         out_shape=[
             jax.ShapeDtypeStruct((chunks, hidden, width), BF),
             jax.ShapeDtypeStruct((nodes, latent), F32),
-            jax.ShapeDtypeStruct((2, bands // 2, cap + piece_rows, latent), BF),
+            jax.ShapeDtypeStruct((bands // 2, cap + piece_rows, latent), BF),
+            jax.ShapeDtypeStruct((bands // 2, cap + piece_rows, latent), BF),
         ],
-        in_specs=[pl.BlockSpec(memory_space=pltpu.SMEM)] + [hbm] * 4 + [vmem()] * 14,
-        out_specs=[hbm, vmem(), vmem()],
+        in_specs=[pl.BlockSpec(memory_space=pltpu.SMEM)] + [hbm] * 4 + [vmem()] * 10,
+        out_specs=[hbm, vmem(), hbm, hbm],
         scratch_shapes=[
-            pltpu.VMEM((chunks, hidden, width), BF),
+            pltpu.VMEM((chunks, hidden, width), F32),
             pltpu.VMEM((chunks, latent, width), BF),
             pltpu.VMEM((chunks, nodes + slots, width), BF),
             pltpu.VMEM((chunks, width, latent), BF),
@@ -310,8 +336,12 @@
             pltpu.VMEM((latent, width), F32),
             pltpu.VMEM((latent, nodes), BF),
             pltpu.VMEM((piece_rows * bands, latent), F32),
+            pltpu.VMEM((latent, hidden), BF),
+            pltpu.VMEM((latent, 128), F32),
+            pltpu.VMEM((2, bands // 2, cap + piece_rows, latent), BF),
             pltpu.SemaphoreType.DMA((4, chunks)),
             pltpu.SemaphoreType.DMA((chunks,)),
+            pltpu.SemaphoreType.DMA((2,)),
         ],
         compiler_params=pltpu.CompilerParams(vmem_limit_bytes=VMEM_LIMIT),
         name="layer_backward",
@@ -367,26 +397,61 @@
     )(keep, got)
 
 
-def settle_kernel(cap, asked_ref, back_ref, local_ref, node_grad_ref, piece_ref):
+def settle_kernel(cap, core_ref, asked_ref, back_ref, local_ref, node_grad_ref, piece_ref):
     chips, height, latent = back_ref.shape
     rows = back_ref[:, : 2 * cap, :].reshape(chips * 2 * cap, latent)
-    picks = onehot_rows(local_ref.shape[0], asked_ref[...])
+    core = core_ref[0]
+    lists = []
+    for chip in range(chips):
+        for turn in range(2):
+            at = 2 * chip + (core if turn == 0 else 1 - core)
+            lists.append(asked_ref[pl.ds(at, 1), :])
+    picks = onehot_rows(local_ref.shape[0], jnp.concatenate(lists, axis=1))
     node_grad_ref[...] = local_ref[...] + dot(picks, rows, 1, 0)
-    piece_ref[...] = jnp.sum(back_ref[:, 2 * cap :, :].astype(F32), axis=0).astype(BF)
-
-
-def settle(asked_row, back, node_local, cap):
+    piece = jnp.sum(back_ref[:, 2 * cap :, :].astype(F32), axis=0).astype(BF)
+    for chip in range(chips):
+        piece_ref[chip] = piece
+
+
+def settle(core, asked, back, node_local, cap):
     chips, height, latent = back.shape
     return pl.pallas_call(
         functools.partial(settle_kernel, cap),
         out_shape=[
             jax.ShapeDtypeStruct(node_local.shape, F32),
-            jax.ShapeDtypeStruct((height - 2 * cap, latent), BF),
+            jax.ShapeDtypeStruct((chips, height - 2 * cap, latent), BF),
         ],
-        in_specs=[vmem()] * 3,
+        in_specs=[pl.BlockSpec(memory_space=pltpu.SMEM)] + [vmem()] * 3,
         out_specs=[vmem()] * 2,
         name="settle_sums",
-    )(asked_row, back, node_local)
+    )(core, asked, back, node_local)
+
+
+def assemble_kernel(core_ref, mine_ref, theirs_ref, *refs):
+    outs, rows = refs[:-1], refs[-1]
+    chips, height, latent = mine_ref.shape
+    core = core_ref[0]
+    for chip in range(chips):
+        for ref, side in ((mine_ref, core), (theirs_ref, 1 - core)):
+            start = pl.multiple_of((2 * chip + side) * height, height)
+            rows[pl.ds(start, height), :] = ref[chip].astype(F32)
+    at = 0
+    for out in outs:
+        out[...] = rows[at : at + out.shape[0], :]
+        at += out.shape[0]
+
+
+def assemble(core, mine, theirs, latent):
+    chips, height, width = mine.shape
+    heights = (3 * latent, latent, 2 * latent, latent, 1, 1)
+    return pl.pallas_call(
+        assemble_kernel,
+        out_shape=[jax.ShapeDtypeStruct((rows, width), F32) for rows in heights],
+        in_specs=[pl.BlockSpec(memory_space=pltpu.SMEM), vmem(), vmem()],
+        out_specs=[vmem()] * len(heights),
+        scratch_shapes=[pltpu.VMEM((2 * chips * height, width), F32)],
+        name="assemble_sums",
+    )(core, mine, theirs)
 
 
 def per_device(
@@ -408,7 +473,7 @@
     bands = lax.axis_size("band")
     chips = bands // 2
     me = lax.axis_index("band")
-    core = me % 2
+    core = (me % 2).reshape(1).astype(jnp.int32)
     latent = node_lat.shape[1]
     cap = fetch_idx.shape[2]
     slots = bands * cap
@@ -417,7 +482,7 @@
     same_core = [[2 * i + c for i in range(chips)] for c in range(2)]
 
     asked = lax.all_to_all(fetch_idx[0], "band", split_axis=0, concat_axis=0, tiled=True)
-    rows = serve(asked.reshape(1, slots), node_lat)
+    rows = serve(asked, node_lat)
     fetched = lax.all_to_all(
         rows.reshape(bands, cap, latent), "band", split_axis=0, concat_axis=0, tiled=True
     ).reshape(slots, latent)
@@ -427,22 +492,18 @@
     recv_rows = edge_recv.reshape(chunks, 1, CHUNK)
     slot_rows = edge_slot.reshape(chunks, 1, CHUNK)
     part, cot_t, hot = prepare(
-        edge_lat, edge_cot, recv_rows, slot_rows, node_lat, w_edge_in.T, slots
+        edge_lat, edge_cot, recv_rows, slot_rows, node_lat, w_edge_in, slots
     )
     weights = (
         w_edge_in,
-        w_edge_in.T,
         w_edge_out,
-        w_edge_out.T,
-        gain_edge[:, None],
+        gain_edge[None, :],
         w_node_in,
-        w_node_in.T,
         w_node_out,
-        w_node_out.T,
-        gain_node[:, None],
-    )
-    grad_pre, node_local, pack = layer(
-        core.reshape(1).astype(jnp.int32),
+        gain_node[None, :],
+    )
+    grad_pre, node_local, keep, send = layer(
+        core,
         part,
         cot_t,
         hot,
@@ -454,37 +515,28 @@
         weights,
         bands,
     )
-    got = lax.ppermute(pack[1], "band", other_core)
-    joined = join(pack[0], got, cap)
+    got = lax.ppermute(send, "band", other_core)
+    joined = join(keep, got, cap)
     back = lax.all_to_all(
         joined, "band", split_axis=0, concat_axis=0, tiled=True, axis_index_groups=same_core
     )
     edge_grad = edge_result(grad_pre, edge_cot, w_edge_in)
-    asked_pairs = asked.reshape(chips, 2, cap)
-    asked_pairs = jnp.where(core == 0, asked_pairs, asked_pairs[:, ::-1, :])
-    node_grad, piece = settle(asked_pairs.reshape(1, slots), back, node_local, cap)
+    back, edge_grad = lax.optimization_barrier((back, edge_grad))
+    node_grad, piece = settle(core, asked, back, node_local, cap)
     mine = lax.all_to_all(
-        jnp.broadcast_to(piece[None], (chips,) + piece.shape),
-        "band",
-        split_axis=0,
-        concat_axis=0,
-        tiled=True,
-        axis_index_groups=same_core,
+        piece, "band", split_axis=0, concat_axis=0, tiled=True, axis_index_groups=same_core
     )
     theirs = lax.ppermute(mine, "band", other_core)
-    both = jnp.where(
-        core == 0, jnp.stack([mine, theirs], axis=1), jnp.stack([theirs, mine], axis=1)
-    ).reshape(-1, latent)
-    both = both.astype(F32)
+    sums = assemble(core, mine, theirs, latent)
     return (
         node_grad,
         edge_grad,
-        both[: 3 * latent],
-        both[3 * latent : 4 * latent],
-        both[7 * latent],
-        both[4 * latent : 6 * latent],
-        both[6 * latent : 7 * latent],
-        both[7 * latent + 1],
+        sums[0],
+        sums[1],
+        sums[4].reshape(-1),
+        sums[2],
+        sums[3],
+        sums[5].reshape(-1),
     )
 
 

time: 139 us -> 119 us (0.86)
  local copies, waits for them, and re-layouts: 20.7 us -> 3.89 us
  waiting for transfers between devices: 21.6 us -> 15.9 us
  Pallas kernels: 50.5 us -> 54.3 us
    all_to_all x1, waiting for transfers between devices: 19.8 us -> 11.9 us  [per_device(): lax.all_to_all(joined, 'band', split_axis=0, concat_axis=0, tiled=True, a...]
    unnamed x11, local copies, waits for them, and re-layouts: 9.96 us -> 3.73 us
    broadcast_in_dim x3 -> x0, local copies, waits for them, and re-layouts: 3.82 us -> none  [the longest x1 1.48 us: per_device(): gain_edge[:, None]]
    slice x4 -> x0, local copies, waits for them, and re-layouts: 3.16 us -> none  [the longest x1 0.93 us: per_device(): both[:3 * latent]]
    pallas_call x1 -> x2, Pallas kernels: 1.9 us -> 4.72 us  [the longest x1 2.58 us: assemble(): pl.pallas_call(assemble_kernel, out_shape=[jax.ShapeDtypeStruct((rows, wi...]
    squeeze x1 -> x0, local copies, waits for them, and re-layouts: 2.21 us -> none  [per_device(): got = lax.ppermute(pack[1], 'band', other_core)]
    ppermute x1, waiting for transfers between devices: 0.01 us -> 1.91 us  [per_device(): theirs = lax.ppermute(mine, 'band', other_core)]
  transfers between devices with their start and end apart: 4 -> 4, of which waited for: 2 -> 3; matrix products, arithmetic and copies ran while one was open for 9% -> 2% of each run, Pallas kernels for 14% -> 17%
where the time goes in v2:
time: 119 us
  Pallas kernels  54.3 us (46%)
  blocking collectives  32.1 us (27%)
  waiting for transfers between devices  15.9 us (13%)
  starting transfers between devices  9.74 us (8%)
  local copies, waits for them, and re-layouts  3.89 us (3%)
  other arithmetic  1.95 us (2%)
    pallas_call x1, Pallas kernels, layer(): pl.pallas_call(functools.partial(layer_kernel, piece_rows), out_shape=[ja...  24.8 us
    all_to_all x1, blocking collectives, per_device(): lax.all_to_all(piece, 'band', split_axis=0, concat_axis=0, tiled=True, ax...  18.3 us
    all_to_all x1, blocking collectives, per_device(): lax.all_to_all(fetch_idx[0], 'band', split_axis=0, concat_axis=0, tiled=T...  13.8 us
    all_to_all x1, waiting for transfers between devices, per_device(): lax.all_to_all(joined, 'band', split_axis=0, concat_axis=0, tiled=True, a...  11.9 us
    pallas_call x1, Pallas kernels, prepare(): pl.pallas_call(prepare_kernel, grid=(chunks,), out_shape=[jax.ShapeDtypeS...  11.6 us
    pallas_call x1, Pallas kernels, edge_result(): pl.pallas_call(edge_kernel, grid=(chunks,), out_shape=jax.ShapeDtypeStruc...  8.53 us
    all_to_all x1, starting transfers between devices, per_device(): lax.all_to_all(joined, 'band', split_axis=0, concat_axis=0, tiled=True, a...  5.86 us
    unnamed x11, local copies, waits for them, and re-layouts  3.73 us
  transfers between devices with their start and end apart: 4, of which 3 were waited for; matrix products, arithmetic and copies ran while one was open for 2% of the time, Pallas kernels for 17%

profile of v2, /device:TPU:0, one launch (start us, length us, event | category | flops | bytes accessed | tf_op | source)
XLA Modules:
  0.0 118.5 jit_solution(16542994137841175379)
XLA Ops:
  0.6 13.8 %all_to_all.26 = s32[16,1,32]{2,1,0:T(1,128)} all-to-all(s32[16,1,32]{2,1,0:T(1,128)} %bitcast.23), channel_id=1, replica_groups=mesh['grp'=2,'band'=16] {'band'}, dimensions={0} | all-to-all | bytes 4096 | tf_op jit(solution)/shard_map/all_to_all | solution.py:484
  14.5 2.1 %serve_rows.1 = bf16[512,256]{1,0:T(8,128)(2,1)} custom-call(s32[16,32]{1,0:T(8,128)} %bitcast.19, bf16[256,256]{1,0:T(8,128)(2,1)} %node_ref.5), custom_call_target="tpu_custom_call" | custom-call | tf_op jit(solution)/shard_map/serve_rows/pallas_call | solution.py:51
  16.6 3.5 %all-to-all-start.1 = ((bf16[16,32,256]{2,1,0:T(8,128)(2,1)}), bf16[16,32,256]{2,1,0:T(8,128)(2,1)S(1)}, u32[]{:S(2)}, u32[]{:S(2)}) async-start(bf16[16,32,256]{2,1,0:T(8,128)(2,1)} %bitcast.17), calls=%async_computation.1 | async-start | bytes 524288 | tf_op jit(solution)/shard_map/all_to_all | solution.py:486
  20.2 0.5 broadcast.22
  20.7 1.3 %reduce.3 = s32[40]{0:T(128)S(1)} reduce(s32[1,40]{1,0:T(1,128)} %param.27, s32[]{:T(128)} %broadcast.22), dimensions={0}, to_apply=%param.27.reduce_sub_computation.3 | reduce | bytes 324 | tf_op args[13]
  22.0 0.1 lt.39
  22.1 11.6 %prepare_edges.1 = (f32[10,256,512]{2,1,0:T(8,128)}, bf16[10,256,512]{2,1,0:T(8,128)(2,1)}, bf16[10,768,512]{2,1,0:T(8,128)(2,1)}) custom-call(bf16[5120,256]{1,0:T(8,128)(2,1)} %edge_ref.1, bf16[5120,256]{1,0:T(8,128)(2,1)} %cot_ref.3, s32[10,1,512]{2,1,0:T(1,128)} %bitcast.21, s32[10,1,512]{2,1,0:T(1,128)} %bitcast.22, bf16[256,256]{1,0:T(8,128)(2,1)} %node_ref.5, ...), custom_call_target="tpu_custom_call" | custom-call | flops 1342177280 | bytes 10485760 | tf_op jit(solution)/shard_map/prepare_edges/pallas_call | solution.py:100
  33.7 0.1 lt.40
  33.7 0.6 compare_convert_fusion.valid_ref
  34.4 0.7 copy-done.2
  35.1 24.8 %layer_backward.1 = (bf16[10,256,512]{2,1,0:T(8,128)(2,1)}, f32[256,256]{1,0:T(8,128)}, bf16[8,160,256]{2,1,0:T(8,128)(2,1)}, bf16[8,160,256]{2,1,0:T(8,128)(2,1)}) custom-call(s32[1]{0:T(128)} %bitcast.core_ref, f32[10,256,512]{2,1,0:T(8,128)} %get-tuple-element.25.part_hbm, bf16[10,256,512]{2,1,0:T(8,128)(2,1)} %get-tuple-element.26.cot_hbm, ...), custom_call_target="tpu_custom_call" | custom-call | tf_op jit(solution)/shard_map/layer_backward/pallas_call | solution.py:311
  59.9 0.3 collective-permute-start
  60.2 2.0 %collective-permute-done.got_ref = bf16[8,160,256]{2,1,0:T(8,128)(2,1)S(1)} collective-permute-done((bf16[8,160,256]{2,1,0:T(8,128)(2,1)}, bf16[8,160,256]{2,1,0:T(8,128)(2,1)S(1)}, u32[]{:S(2)}, u32[]{:S(2)}) %collective-permute-start) | collective-permute-done | bytes 655392 | tf_op jit(solution)/shard_map/ppermute | solution.py:518
  62.3 0.8 copy-done.3
  63.1 2.3 %join_cores.1 = bf16[8,192,256]{2,1,0:T(8,128)(2,1)} custom-call(bf16[8,160,256]{2,1,0:T(8,128)(2,1)} %get-tuple-element.28.pack_ref, bf16[8,160,256]{2,1,0:T(8,128)(2,1)} %copy-done.3), custom_call_target="tpu_custom_call" | custom-call | tf_op jit(solution)/shard_map/join_cores/pallas_call | solution.py:391
  65.4 5.9 %all-to-all-start.2 = ((bf16[8,192,256]{2,1,0:T(8,128)(2,1)}), bf16[8,192,256]{2,1,0:T(8,128)(2,1)S(1)}, u32[]{:S(2)}, u32[]{:S(2)}) async-start(bf16[8,192,256]{2,1,0:T(8,128)(2,1)} %join_cores.1), calls=%async_computation.2 | async-start | bytes 1572864 | tf_op jit(solution)/shard_map/all_to_all | solution.py:520
  71.3 8.5 %edge_result.1 = bf16[5120,256]{1,0:T(8,128)(2,1)} custom-call(bf16[10,256,512]{2,1,0:T(8,128)(2,1)} %get-tuple-element.30.grad_ref, bf16[5120,256]{1,0:T(8,128)(2,1)} %cot_ref.3, bf16[768,256]{1,0:T(8,128)(2,1)} %w_in_ref.5), custom_call_target="tpu_custom_call" | custom-call | flops 671088640 | bytes 7864320 | tf_op jit(solution)/shard_map/edge_result/pallas_call | solution.py:361
  79.8 11.9 %all-to-all-done.2.back_ref = bf16[8,192,256]{2,1,0:T(8,128)(2,1)S(1)} async-done(((bf16[8,192,256]{2,1,0:T(8,128)(2,1)}), bf16[8,192,256]{2,1,0:T(8,128)(2,1)S(1)}, u32[]{:S(2)}, u32[]{:S(2)}) %all-to-all-start.2) | async-done | bytes 786464 | tf_op jit(solution)/shard_map/all_to_all | solution.py:520
  91.7 0.9 copy-done
  92.6 2.4 %settle_sums.1 = (f32[256,256]{1,0:T(8,128)}, bf16[8,128,256]{2,1,0:T(8,128)(2,1)}) custom-call(s32[1]{0:T(128)} %bitcast.core_ref, s32[16,32]{1,0:T(8,128)} %bitcast.20, bf16[8,192,256]{2,1,0:T(8,128)(2,1)} %copy-done, f32[256,256]{1,0:T(8,128)} %get-tuple-element.32.local_ref), custom_call_target="tpu_custom_call" | custom-call | tf_op jit(solution)/shard_map/settle_sums/pallas_call | solution.py:418
  95.0 18.3 %all_to_all.27.mine_ref = bf16[8,128,256]{2,1,0:T(8,128)(2,1)S(1)} all-to-all(bf16[8,128,256]{2,1,0:T(8,128)(2,1)} %get-tuple-element.35), channel_id=1, replica_groups={{0,2,4,6,8,10,12,14},{1,3,5,7,9,11,13,15},{16,18,20,22,24,26,28,30},{17..., dimensions={0} | all-to-all | bytes 1048576 | tf_op jit(solution)/shard_map/all_to_all | solution.py:526
  113.2 1.9 %collective-permute-done.1.theirs_ref = bf16[8,128,256]{2,1,0:T(8,128)(2,1)S(1)} collective-permute-done((bf16[8,128,256]{2,1,0:T(8,128)(2,1)S(1)}, bf16[8,128,256]{2,1,0:T(8,128)(2,1)S(1)}, u32[]{:S(2)}, u32[]{:S(2)}) %collective-permute-start.1) | collective-permute-done | bytes 524320 | tf_op jit(solution)/shard_map/ppermute | solution.py:529
  115.2 0.8 copy-done.4
  116.0 2.6 %assemble_sums.1 = (f32[768,256]{1,0:T(8,128)}, f32[256,256]{1,0:T(8,128)}, f32[512,256]{1,0:T(8,128)}, f32[256,256]{1,0:T(8,128)}, f32[1,256]{1,0:T(1,128)}, /*index=5*/f32[1,256]{1,0:T(1,128)}) custom-call(s32[1]{0:T(128)} %bitcast.core_ref, bf16[8,128,256]{2,1,0:T(8,128)(2,1)} %copy-done.1, bf16[8,128,256]{2,1,0:T(8,128)(2,1)} %copy-done.4), custom_call_target="tpu_custom_call" | custom-call | tf_op jit(solution)/shard_map/assemble_sums/pallas_call | solution.py:447
  (9 shorter events, 0.0 us)
Async XLA Ops:
  16.6 17.8 %all-to-all-start.1 = ((bf16[16,32,256]{2,1,0:T(8,128)(2,1)}), bf16[16,32,256]{2,1,0:T(8,128)(2,1)S(1)}, u32[]{:S(2)}, u32[]{:S(2)}) async-start(bf16[16,32,256]{2,1,0:T(8,128)(2,1)} %bitcast.17), calls=%async_computation.1 | async-start | bytes 524288 | tf_op jit(solution)/shard_map/all_to_all | solution.py:486
  34.4 0.7 copy-start.2
  59.9 2.4 %collective-permute-start = (bf16[8,160,256]{2,1,0:T(8,128)(2,1)}, bf16[8,160,256]{2,1,0:T(8,128)(2,1)S(1)}, u32[]{:S(2)}, u32[]{:S(2)}) collective-permute-start(bf16[8,160,256]{2,1,0:T(8,128)(2,1)} %get-tuple-element.29), channel_id=1, source_target_pairs={{0,1},{1,0},{2,3},{3,2},{4,5},{5,4},{6,7},{7,6},{8,9},{9,8},{10,11... | collective-permute-start | bytes 1966088 | tf_op jit(solution)/shard_map/ppermute | solution.py:518
  62.3 0.8 copy-start.3
  65.4 26.3 %all-to-all-start.2 = ((bf16[8,192,256]{2,1,0:T(8,128)(2,1)}), bf16[8,192,256]{2,1,0:T(8,128)(2,1)S(1)}, u32[]{:S(2)}, u32[]{:S(2)}) async-start(bf16[8,192,256]{2,1,0:T(8,128)(2,1)} %join_cores.1), calls=%async_computation.2 | async-start | bytes 1572864 | tf_op jit(solution)/shard_map/all_to_all | solution.py:520
  91.7 0.9 copy-start
  113.2 1.9 %copy-start.1 = (bf16[8,128,256]{2,1,0:T(8,128)(2,1)}, bf16[8,128,256]{2,1,0:T(8,128)(2,1)S(1)}, u32[]{:S(2)}) copy-start(bf16[8,128,256]{2,1,0:T(8,128)(2,1)S(1)} %all_to_all.27.mine_ref) | copy-start | bytes 1572868
  113.2 1.9 %collective-permute-start.1 = (bf16[8,128,256]{2,1,0:T(8,128)(2,1)S(1)}, bf16[8,128,256]{2,1,0:T(8,128)(2,1)S(1)}, u32[]{:S(2)}, u32[]{:S(2)}) collective-permute-start(bf16[8,128,256]{2,1,0:T(8,128)(2,1)S(1)} %all_to_all.27.mine_ref), channel_id=1, source_target_pairs={{0,1},{1,0},{2,3},{3,2},{4,5},{5,4},{6,7},{7,6},{8,9},{9,8},{10,11... | collective-permute-start | bytes 1572872 | tf_op jit(solution)/shard_map/ppermute | solution.py:529
  115.2 0.8 copy-start.4

commit v3 on v2

v3 whole, which is shorter than its diff:
```python
import functools

import jax
import jax.numpy as jnp
from jax import lax
from jax.experimental import pallas as pl
from jax.experimental.pallas import tpu as pltpu
from jax.sharding import PartitionSpec as P

epsilon = 1e-05
CHUNK = 1280
GROUP = 4
TAIL = 16
VMEM_LIMIT = 60 * 2**20
BF = jnp.bfloat16
F32 = jnp.float32


def dot(lhs, rhs, lhs_dim, rhs_dim):
    return lax.dot_general(
        lhs, rhs, (((lhs_dim,), (rhs_dim,)), ((), ())), preferred_element_type=F32
    )


def swish_and_slope(values):
    logistic = jax.nn.sigmoid(values)
    hidden = values * logistic
    return hidden, logistic + hidden * (1.0 - logistic)


def onehot_rows(row_count, index_row):
    rows = lax.broadcasted_iota(jnp.int16, (row_count, index_row.shape[1]), 0)
    return jnp.where(rows == index_row.astype(jnp.int16), jnp.ones((), BF), jnp.zeros((), BF))


def vmem():
    return pl.BlockSpec(memory_space=pltpu.VMEM)


def whole(shape):
    return pl.BlockSpec(shape, lambda *_: (0,) * len(shape))


def serve_kernel(place_ref, lists_ref, *refs):
    members, rows_ref = refs[:-1], refs[-1]
    groups, _, cap = lists_ref.shape
    group, member = place_ref[1], place_ref[2] % GROUP
    for k, nodes_ref in enumerate(members):
        owner = member ^ k
        wanted = jnp.concatenate(
            [lists_ref[j, pl.ds(group * GROUP + owner, 1), :] for j in range(groups)], axis=1
        )
        picks = onehot_rows(nodes_ref.shape[0], wanted)
        rows = dot(picks, nodes_ref[...], 0, 0).astype(BF)
        place = pl.ds(pl.multiple_of(owner * cap, cap), cap)
        for j in range(groups):
            rows_ref[group ^ j, place, :] = rows[j * cap : (j + 1) * cap]


def serve(place, lists, members):
    groups, _, cap = lists.shape
    return pl.pallas_call(
        serve_kernel,
        out_shape=jax.ShapeDtypeStruct((groups, GROUP * cap, members[0].shape[1]), BF),
        in_specs=[pl.BlockSpec(memory_space=pltpu.SMEM)] + [vmem()] * (1 + GROUP),
        out_specs=vmem(),
        compiler_params=pltpu.CompilerParams(vmem_limit_bytes=VMEM_LIMIT),
        name="serve_rows",
    )(place, lists, *members)


def prepare_kernel(
    edge_ref, cot_ref, recv_ref, node_ref, w_in_ref, part_ref, cot_t_ref, node_part, w_edge_t
):
    latent = edge_ref.shape[1]

    @pl.when(pl.program_id(0) == 0)
    def _():
        node_part[...] = dot(w_in_ref[2 * latent :, :], node_ref[...], 0, 1).astype(BF)
        w_edge_t[...] = w_in_ref[:latent, :].T

    recv_hot = onehot_rows(node_ref.shape[0], recv_ref[0])
    part_ref[0] = dot(w_edge_t[...], edge_ref[...], 1, 1) + dot(node_part[...], recv_hot, 1, 0)
    cot_t_ref[0] = cot_ref[...].T


def prepare(edge_lat, edge_cot, recv_rows, node_lat, w_edge_in):
    edges, latent = edge_lat.shape
    hidden = w_edge_in.shape[1]
    nodes = node_lat.shape[0]
    chunks = edges // CHUNK
    rows = pl.BlockSpec((CHUNK, latent), lambda i: (i, 0))

    def along(height):
        return pl.BlockSpec((1, height, CHUNK), lambda i: (i, 0, 0))

    return pl.pallas_call(
        prepare_kernel,
        grid=(chunks,),
        out_shape=[
            jax.ShapeDtypeStruct((chunks, hidden, CHUNK), F32),
            jax.ShapeDtypeStruct((chunks, latent, CHUNK), BF),
        ],
        in_specs=[rows, rows, along(1), whole(node_lat.shape), whole(w_edge_in.shape)],
        out_specs=[along(hidden), along(latent)],
        scratch_shapes=[pltpu.VMEM((hidden, nodes), BF), pltpu.VMEM((hidden, latent), BF)],
        compiler_params=pltpu.CompilerParams(vmem_limit_bytes=VMEM_LIMIT),
        cost_estimate=pl.CostEstimate(
            flops=4 * edges * latent * hidden, bytes_accessed=8 * edges * latent, transcendentals=0
        ),
        name="prepare_edges",
    )(edge_lat, edge_cot, recv_rows, node_lat, w_edge_in)


def layer_kernel(
    piece_rows,
    core_ref,
    part_hbm,
    cot_hbm,
    edge_hbm,
    recv_ref,
    slot_ref,
    wanted_ref,
    valid_ref,
    fetched_ref,
    node_ref,
    node_cot_ref,
    w_in_ref,
    w_out_ref,
    gain_edge_ref,
    w_node_in_ref,
    w_node_out_ref,
    gain_node_ref,
    grad_pre_hbm,
    node_local_ref,
    keep_hbm,
    send_hbm,
    part,
    cot,
    edge,
    hot,
    hidden,
    slope,
    normed,
    scale,
    grad_pre,
    send_part,
    summed_acc,
    w_in_acc,
    w_out_acc,
    ends_acc,
    gain_acc,
    grad_summed,
    weight_pack,
    w_out_t,
    gain_column,
    pack,
    sems,
    out_sems,
    pack_sems,
):
    chunks, latent, width = part.shape
    nodes = node_ref.shape[0]
    slots = fetched_ref.shape[0]
    bands = pack.shape[1] * 2
    cap = slots // bands

    def part_copy(c):
        return pltpu.make_async_copy(part_hbm.at[c], part.at[c], sems.at[0, c])

    def cot_copy(c):
        return pltpu.make_async_copy(cot_hbm.at[c], cot.at[c], sems.at[1, c])

    def edge_copy(c):
        return pltpu.make_async_copy(edge_hbm.at[c], edge.at[c], sems.at[2, c])

    for copy in (part_copy, cot_copy, edge_copy):
        for c in range(chunks):
            copy(c).start()

    send_part[...] = dot(w_in_ref[latent : 2 * latent, :], fetched_ref[...], 0, 1).astype(BF)
    w_out_t[...] = w_out_ref[...].T
    gain_column[...] = jnp.broadcast_to(gain_edge_ref[...], (128, latent)).T
    summed_acc[...] = jnp.zeros_like(summed_acc)
    for c in range(chunks):
        part_copy(c).wait()
    w_in_acc[...] = jnp.zeros_like(w_in_acc)
    w_out_acc[...] = jnp.zeros_like(w_out_acc)
    ends_acc[...] = jnp.zeros_like(ends_acc)
    gain_acc[...] = jnp.zeros_like(gain_acc)

    @pl.loop(0, chunks, unroll=True)
    def _(c):
        slot_hot = onehot_rows(slots, slot_ref[c])
        recv_hot = onehot_rows(nodes, recv_ref[c])
        hot[c, :nodes, :] = recv_hot
        hot[c, nodes:, :] = slot_hot
        pre = part[c] + dot(send_part[...], slot_hot, 1, 0)
        hid, slo = swish_and_slope(pre)
        hid = hid.astype(BF)
        hidden[c] = hid
        slope[c] = slo.astype(BF)
        out = dot(w_out_t[...], hid, 1, 0)
        centred = out - jnp.mean(out, axis=0, keepdims=True)
        inv = lax.rsqrt(jnp.mean(centred * centred, axis=0, keepdims=True) + epsilon)
        inv = inv * valid_ref[c]
        scale[c] = inv
        norm = (centred * inv).astype(BF)
        normed[c] = norm
        summed_acc[...] += dot(norm, recv_hot, 1, 1)

    for c in range(chunks):
        cot_copy(c).wait()
        edge_copy(c).wait()
    node = node_ref[...]
    summed = (summed_acc[...] * gain_column[:, :1]).astype(BF)
    pre_node = dot(w_node_in_ref[:latent, :], node, 0, 1) + dot(
        w_node_in_ref[latent:, :], summed, 0, 0
    )
    hid_node, slope_node = swish_and_slope(pre_node)
    hid_node = hid_node.astype(BF)
    out_node = dot(w_node_out_ref[...], hid_node, 0, 0)
    centred = out_node - jnp.mean(out_node, axis=0, keepdims=True)
    inv_node = lax.rsqrt(jnp.mean(centred * centred, axis=0, keepdims=True) + epsilon)
    norm_node = centred * inv_node
    node_base = node_cot_ref[...].astype(F32)
    cot_node = node_base.T
    product = cot_node * norm_node
    gain_node_grad = jnp.sum(product.T, axis=0, keepdims=True)
    dy = cot_node * jnp.broadcast_to(gain_node_ref[...], (128, latent)).T[:, :1]
    grad_out_node = (
        inv_node
        * (
            dy
            - jnp.mean(dy, axis=0, keepdims=True)
            - norm_node * jnp.mean(dy * norm_node, axis=0, keepdims=True)
        )
    ).astype(BF)
    base = 4 * latent
    weight_pack[base + 2 * latent : base + 3 * latent, :] = dot(hid_node, grad_out_node, 1, 1)
    grad_pre_node = (dot(w_node_out_ref[...], grad_out_node, 1, 0) * slope_node).astype(BF)
    weight_pack[base : base + latent, :] = dot(node, grad_pre_node, 0, 1)
    weight_pack[base + latent : base + 2 * latent, :] = dot(summed, grad_pre_node, 1, 1)
    grad_summed[...] = dot(w_node_in_ref[latent:, :], grad_pre_node, 1, 0).astype(BF)
    node_local = node_base + dot(grad_pre_node, w_node_in_ref[:latent, :], 0, 1)

    @pl.loop(0, chunks, unroll=True)
    def _(c):
        grad_update = cot[c].astype(F32) + dot(grad_summed[...], hot[c, :nodes, :], 1, 0)
        norm = normed[c].astype(F32)
        product = grad_update * norm
        gain_acc[...] += product
        gain = gain_column[:, :1]
        dy = grad_update * gain
        mean_dy = jnp.mean(dy, axis=0, keepdims=True)
        mean_product = jnp.mean(product * gain, axis=0, keepdims=True)
        grad_out = (scale[c] * (dy - mean_dy - norm * mean_product)).astype(BF)
        w_out_acc[...] += dot(hidden[c], grad_out, 1, 1)
        grad_hidden = dot(w_out_ref[...], grad_out, 1, 0)
        grad_in = (grad_hidden * slope[c].astype(F32)).astype(BF)
        grad_pre[c] = grad_in
        w_in_acc[...] += dot(grad_in, edge[c], 1, 0)
        ends_acc[...] += dot(hot[c], grad_in, 1, 1)

    for c in range(chunks):
        pltpu.make_async_copy(grad_pre.at[c], grad_pre_hbm.at[c], out_sems.at[c]).start()
    recv_sum = ends_acc[:nodes, :].astype(BF)
    slot_sum = ends_acc[nodes:, :].astype(BF)
    node_local_ref[...] = node_local + dot(recv_sum, w_in_ref[2 * latent :, :], 1, 1)
    weight_pack[:latent, :] = w_in_acc[...].T
    weight_pack[latent : 2 * latent, :] = dot(fetched_ref[...], slot_sum, 0, 0)
    weight_pack[2 * latent : 3 * latent, :] = dot(node, recv_sum, 0, 0)
    weight_pack[3 * latent : 4 * latent, :] = w_out_acc[...]
    used = base + 3 * latent
    if used < weight_pack.shape[0]:
        weight_pack[used:, :] = jnp.zeros_like(weight_pack[used:, :])
    gain_edge_grad = jnp.sum(gain_acc[...].T, axis=0, keepdims=True)
    slot_grads = dot(slot_sum, w_in_ref[latent : 2 * latent, :], 1, 1).astype(BF)
    core = core_ref[0]
    for d in range(bands):
        pack[d % 2, d // 2, :cap, :] = slot_grads[d * cap : (d + 1) * cap, :]
        body = weight_pack[d * piece_rows : (d + 1) * piece_rows, :]
        pack[d % 2, d // 2, cap : cap + piece_rows, :] = body.astype(BF)
        row = lax.broadcasted_iota(jnp.int32, (TAIL, latent), 0)
        listed = jnp.concatenate([wanted_ref[d : d + 1, :].astype(F32)] * (latent // cap), axis=1)
        column = lax.broadcasted_iota(jnp.int32, (1, latent), 1)
        listed = jnp.where(column // cap == core, listed, 0.0)
        extra = jnp.where(row == 1, listed, 0.0)
        if d < 2:
            extra = jnp.where(row == 0, gain_edge_grad if d == 0 else gain_node_grad, extra)
        pack[d % 2, d // 2, cap + piece_rows :, :] = extra.astype(BF)
    for own in range(2):

        @pl.when(core == own)
        def _():
            keep = pltpu.make_async_copy(pack.at[own], keep_hbm, pack_sems.at[0])
            send = pltpu.make_async_copy(pack.at[1 - own], send_hbm, pack_sems.at[1])
            send.start()
            keep.start()
            send.wait()
            keep.wait()

    for c in range(chunks):
        pltpu.make_async_copy(grad_pre.at[c], grad_pre_hbm.at[c], out_sems.at[c]).wait()


def layer(
    core, part, cot_t, edge_lat, recv_rows, slot_rows, wanted, valid_rows, fetched, node_lat, node_cot, weights, bands
):
    chunks, hidden, width = part.shape
    edges = edge_lat.reshape(chunks, width, -1)
    nodes, latent = node_lat.shape
    slots = fetched.shape[0]
    cap = slots // bands
    piece_rows = -(-7 * latent // (bands * 16)) * 16
    hbm = pl.BlockSpec(memory_space=pl.ANY)
    return pl.pallas_call(
        functools.partial(layer_kernel, piece_rows),
        out_shape=[
            jax.ShapeDtypeStruct((chunks, hidden, width), BF),
            jax.ShapeDtypeStruct((nodes, latent), F32),
            jax.ShapeDtypeStruct((bands // 2, cap + piece_rows + TAIL, latent), BF),
            jax.ShapeDtypeStruct((bands // 2, cap + piece_rows + TAIL, latent), BF),
        ],
        in_specs=[pl.BlockSpec(memory_space=pltpu.SMEM)] + [hbm] * 3 + [vmem()] * 13,
        out_specs=[hbm, vmem(), hbm, hbm],
        scratch_shapes=[
            pltpu.VMEM((chunks, hidden, width), F32),
            pltpu.VMEM((chunks, latent, width), BF),
            pltpu.VMEM((chunks, width, latent), BF),
            pltpu.VMEM((chunks, nodes + slots, width), BF),
            pltpu.VMEM((chunks, hidden, width), BF),
            pltpu.VMEM((chunks, hidden, width), BF),
            pltpu.VMEM((chunks, latent, width), BF),
            pltpu.VMEM((chunks, 1, width), F32),
            pltpu.VMEM((chunks, hidden, width), BF),
            pltpu.VMEM((hidden, slots), BF),
            pltpu.VMEM((latent, nodes), F32),
            pltpu.VMEM((hidden, latent), F32),
            pltpu.VMEM((hidden, latent), F32),
            pltpu.VMEM((nodes + slots, hidden), F32),
            pltpu.VMEM((latent, width), F32),
            pltpu.VMEM((latent, nodes), BF),
            pltpu.VMEM((piece_rows * bands, latent), F32),
            pltpu.VMEM((latent, hidden), BF),
            pltpu.VMEM((latent, 128), F32),
            pltpu.VMEM((2, bands // 2, cap + piece_rows + TAIL, latent), BF),
            pltpu.SemaphoreType.DMA((3, chunks)),
            pltpu.SemaphoreType.DMA((chunks,)),
            pltpu.SemaphoreType.DMA((2,)),
        ],
        compiler_params=pltpu.CompilerParams(vmem_limit_bytes=VMEM_LIMIT),
        name="layer_backward",
    )(core, part, cot_t, edges, recv_rows, slot_rows, wanted, valid_rows, fetched, node_lat, node_cot, *weights)


def edge_kernel(grad_ref, cot_ref, w_in_ref, out_ref):
    latent = cot_ref.shape[1]
    back = dot(grad_ref[0], w_in_ref[:latent, :], 0, 1)
    out_ref[...] = (cot_ref[...].astype(F32) + back).astype(BF)


def edge_result(grad_pre, edge_cot, w_edge_in):
    chunks, hidden, width = grad_pre.shape
    latent = edge_cot.shape[1]
    rows = pl.BlockSpec((width, latent), lambda i: (i, 0))
    return pl.pallas_call(
        edge_kernel,
        grid=(chunks,),
        out_shape=jax.ShapeDtypeStruct(edge_cot.shape, BF),
        in_specs=[
            pl.BlockSpec((1, hidden, width), lambda i: (i, 0, 0)),
            rows,
            whole(w_edge_in.shape),
        ],
        out_specs=rows,
        compiler_params=pltpu.CompilerParams(vmem_limit_bytes=VMEM_LIMIT),
        cost_estimate=pl.CostEstimate(
            flops=2 * chunks * width * hidden * latent,
            bytes_accessed=6 * chunks * width * latent,
            transcendentals=0,
        ),
        name="edge_result",
    )(grad_pre, edge_cot, w_edge_in)


def join_kernel(cap, pack_ref, got_ref, out_ref):
    out_ref[:, :cap, :] = pack_ref[:, :cap, :]
    out_ref[:, cap : 2 * cap, :] = got_ref[:, :cap, :]
    out_ref[:, 2 * cap :, :] = (
        pack_ref[:, cap:, :].astype(F32) + got_ref[:, cap:, :].astype(F32)
    ).astype(BF)


def join(keep, got, cap):
    chips, height, latent = keep.shape
    return pl.pallas_call(
        functools.partial(join_kernel, cap),
        out_shape=jax.ShapeDtypeStruct((chips, height + cap, latent), BF),
        in_specs=[vmem(), vmem()],
        out_specs=vmem(),
        name="join_cores",
    )(keep, got)


def settle_kernel(cap, core_ref, back_ref, local_ref, node_grad_ref, piece_ref):
    chips, height, latent = back_ref.shape
    rows = back_ref[:, : 2 * cap, :].reshape(chips * 2 * cap, latent)
    core = core_ref[0]
    listed = back_ref[:, height - TAIL + 1, :].astype(F32)
    lists = []
    for chip in range(chips):
        first, second = listed[chip : chip + 1, :cap], listed[chip : chip + 1, cap : 2 * cap]
        lists.append(jnp.where(core == 0, first, second))
        lists.append(jnp.where(core == 0, second, first))
    picks = onehot_rows(local_ref.shape[0], jnp.concatenate(lists, axis=1).astype(jnp.int32))
    node_grad_ref[...] = local_ref[...] + dot(picks, rows, 1, 0)
    piece = jnp.sum(back_ref[:, 2 * cap :, :].astype(F32), axis=0).astype(BF)
    for chip in range(chips):
        piece_ref[chip] = piece


def settle(place, back, node_local, cap):
    chips, height, latent = back.shape
    return pl.pallas_call(
        functools.partial(settle_kernel, cap),
        out_shape=[
            jax.ShapeDtypeStruct(node_local.shape, F32),
            jax.ShapeDtypeStruct((chips, height - 2 * cap, latent), BF),
        ],
        in_specs=[pl.BlockSpec(memory_space=pltpu.SMEM)] + [vmem()] * 2,
        out_specs=[vmem()] * 2,
        name="settle_sums",
    )(place, back, node_local)


def assemble_kernel(core_ref, mine_ref, theirs_ref, *refs):
    outs, rows = refs[:-1], refs[-1]
    chips, height, latent = mine_ref.shape
    body = height - TAIL
    core = core_ref[0]
    for chip in range(chips):
        for ref, side in ((mine_ref, core), (theirs_ref, 1 - core)):
            start = pl.multiple_of((2 * chip + side) * body, body)
            rows[pl.ds(start, body), :] = ref[chip, :body, :].astype(F32)
    first, second = mine_ref[0, body:, :].astype(F32), theirs_ref[0, body:, :].astype(F32)
    outs[-2][...] = jnp.where(core == 0, first, second)[:1]
    outs[-1][...] = jnp.where(core == 0, second, first)[:1]
    at = 0
    for out in outs[:-2]:
        out[...] = rows[at : at + out.shape[0], :]
        at += out.shape[0]


def assemble(place, mine, theirs, latent):
    chips, height, width = mine.shape
    heights = (3 * latent, latent, 2 * latent, latent, 1, 1)
    return pl.pallas_call(
        assemble_kernel,
        out_shape=[jax.ShapeDtypeStruct((rows, width), F32) for rows in heights],
        in_specs=[pl.BlockSpec(memory_space=pltpu.SMEM), vmem(), vmem()],
        out_specs=[vmem()] * len(heights),
        scratch_shapes=[pltpu.VMEM((2 * chips * (height - TAIL), width), F32)],
        name="assemble_sums",
    )(place, mine, theirs)


def per_device(
    node_lat,
    edge_lat,
    node_cot,
    edge_cot,
    w_edge_in,
    w_edge_out,
    gain_edge,
    w_node_in,
    w_node_out,
    gain_node,
    fetch_idx,
    edge_slot,
    edge_recv,
    block_fill,
):
    bands = lax.axis_size("band")
    chips = bands // 2
    me = lax.axis_index("band")
    place = jnp.stack([me % 2, me // GROUP, me]).astype(jnp.int32)
    latent = node_lat.shape[1]
    cap = fetch_idx.shape[2]
    slots = bands * cap
    chunks = edge_lat.shape[0] // CHUNK
    other_core = [(i, i ^ 1) for i in range(bands)]
    same_core = [[2 * i + c for i in range(chips)] for c in range(2)]

    groups = bands // GROUP
    like_placed = [[GROUP * g + i for g in range(groups)] for i in range(GROUP)]

    def swap(array, step):
        return lax.ppermute(array, "band", [(i, i ^ step) for i in range(bands)])

    across = swap(node_lat, 2)
    lists = fetch_idx
    step = GROUP
    while step < bands:
        lists = jnp.concatenate([lists, swap(lists, step)], axis=0)
        step *= 2
    members = (node_lat, swap(node_lat, 1), across, swap(across, 1))
    rows = serve(place, lists, members)
    valid = jnp.arange(128, dtype=jnp.int32)[None, :] < block_fill[0][:, None]
    valid = valid.astype(F32).reshape(chunks, 1, CHUNK)
    recv_rows = edge_recv.reshape(chunks, 1, CHUNK)
    recv_rows, rows = lax.optimization_barrier((recv_rows, rows))
    fetched = lax.all_to_all(
        rows, "band", split_axis=0, concat_axis=0, tiled=True, axis_index_groups=like_placed
    ).reshape(slots, latent)

    slot_rows = edge_slot.reshape(chunks, 1, CHUNK)
    part, cot_t = prepare(
        edge_lat, edge_cot, recv_rows, node_lat, w_edge_in
    )
    weights = (
        w_edge_in,
        w_edge_out,
        gain_edge[None, :],
        w_node_in,
        w_node_out,
        gain_node[None, :],
    )
    grad_pre, node_local, keep, send = layer(
        place,
        part,
        cot_t,
        edge_lat,
        recv_rows,
        slot_rows,
        fetch_idx[0],
        valid,
        fetched,
        node_lat,
        node_cot,
        weights,
        bands,
    )
    got = lax.ppermute(send, "band", other_core)
    joined = join(keep, got, cap)
    back = lax.all_to_all(
        joined, "band", split_axis=0, concat_axis=0, tiled=True, axis_index_groups=same_core
    )
    edge_grad = edge_result(grad_pre, edge_cot, w_edge_in)
    back, edge_grad = lax.optimization_barrier((back, edge_grad))
    node_grad, piece = settle(place, back, node_local, cap)
    mine = lax.all_to_all(
        piece, "band", split_axis=0, concat_axis=0, tiled=True, axis_index_groups=same_core
    )
    theirs = lax.ppermute(mine, "band", other_core)
    sums = assemble(place, mine, theirs, latent)
    return (
        node_grad,
        edge_grad,
        sums[0],
        sums[1],
        sums[4].reshape(-1),
        sums[2],
        sums[3],
        sums[5].reshape(-1),
    )


def solution(mesh):
    in_specs = (
        P(("grp", "band"), None),
        P(("grp", "band"), None),
        P(("grp", "band"), None),
        P(("grp", "band"), None),
        P(),
        P(),
        P(),
        P(),
        P(),
        P(),
        P("band", None, None),
        P("band"),
        P("band"),
        P("band", None),
    )
    out_specs = (
        P(("grp", "band"), None),
        P(("grp", "band"), None),
        P("grp", None),
        P("grp", None),
        P("grp"),
        P("grp", None),
        P("grp", None),
        P("grp"),
    )
    return jax.shard_map(
        per_device, mesh=mesh, in_specs=in_specs, out_specs=out_specs, check_vma=False
    )
```

time: 119 us -> 109 us (0.916)
  blocking collectives: 32.1 us -> 18.3 us
  Pallas kernels: 54.3 us -> 41 us
  waiting for transfers between devices: 15.9 us -> 22.6 us
  starting transfers between devices: 9.74 us -> 15.7 us
  other arithmetic: 1.95 us -> 4.58 us
  local copies, waits for them, and re-layouts: 3.89 us -> 5.21 us
    all_to_all x1 -> x0, blocking collectives: 13.8 us -> none  [per_device(): lax.all_to_all(fetch_idx[0], 'band', split_axis=0, concat_axis=0, tiled=T...]
    ppermute x0 -> x5, starting transfers between devices: none -> 7.2 us  [swap(): return lax.ppermute(array, 'band', [(i, i ^ step) for i in range(bands)])]
    pallas_call x1, Pallas kernels: 24.8 us -> 18.9 us  [layer(): pl.pallas_call(functools.partial(layer_kernel, piece_rows), out_shape=[ja...]
    pallas_call x1, Pallas kernels: 11.6 us -> 7.35 us  [prepare(): pl.pallas_call(prepare_kernel, grid=(chunks,), out_shape=[jax.ShapeDtypeS...]
    pallas_call x1, Pallas kernels: 8.53 us -> 5.27 us  [edge_result(): pl.pallas_call(edge_kernel, grid=(chunks,), out_shape=jax.ShapeDtypeStruc...]
    all_to_all x1, waiting for transfers between devices: 11.9 us -> 15.2 us  [per_device(): lax.all_to_all(joined, 'band', split_axis=0, concat_axis=0, tiled=True, a...]
    ppermute x0 -> x5, waiting for transfers between devices: none -> 2.29 us  [swap(): return lax.ppermute(array, 'band', [(i, i ^ step) for i in range(bands)])]
    concatenate x0 -> x2, other arithmetic: none -> 2.02 us  [per_device(): lists = jnp.concatenate([lists, swap(lists, step)], axis=0)]
  transfers between devices with their start and end apart: 4 -> 9, of which waited for: 3 -> 5; matrix products, arithmetic and copies ran while one was open for 2% -> 5% of each run, Pallas kernels for 17% -> 12%
where the time goes in v3:
time: 109 us; the launch traced here: 108 us
  Pallas kernels  41 us (38%)
  waiting for transfers between devices  22.6 us (21%)
  blocking collectives  18.3 us (17%)
  starting transfers between devices  15.7 us (14%)
  local copies, waits for them, and re-layouts  5.21 us (5%)
  other arithmetic  4.58 us (4%)
    pallas_call x1, Pallas kernels, layer(): pl.pallas_call(functools.partial(layer_kernel, piece_rows), out_shape=[ja...  18.9 us
    all_to_all x1, blocking collectives, per_device(): lax.all_to_all(piece, 'band', split_axis=0, concat_axis=0, tiled=True, ax...  18.3 us
    all_to_all x1, waiting for transfers between devices, per_device(): lax.all_to_all(joined, 'band', split_axis=0, concat_axis=0, tiled=True, a...  15.2 us
    pallas_call x1, Pallas kernels, prepare(): pl.pallas_call(prepare_kernel, grid=(chunks,), out_shape=[jax.ShapeDtypeS...  7.35 us
    ppermute x5, starting transfers between devices, swap(): return lax.ppermute(array, 'band', [(i, i ^ step) for i in range(bands)])  7.2 us
    pallas_call x1, Pallas kernels, edge_result(): pl.pallas_call(edge_kernel, grid=(chunks,), out_shape=jax.ShapeDtypeStruc...  5.27 us
    unnamed x17, local copies, waits for them, and re-layouts  5.02 us
    all_to_all x1, starting transfers between devices, per_device(): lax.all_to_all(rows, 'band', split_axis=0, concat_axis=0, tiled=True, axi...  4.32 us
  transfers between devices with their start and end apart: 9, of which 5 were waited for; matrix products, arithmetic and copies ran while one was open for 5% of the time, Pallas kernels for 12%

profile of v3, /device:TPU:0, one launch (start us, length us, event | category | flops | bytes accessed | tf_op | source)
XLA Modules:
  0.0 108.1 jit_solution(8422777873210885148)
XLA Ops:
  0.6 3.0 %collective-permute-start.3 = (bf16[256,256]{1,0:T(8,128)(2,1)}, bf16[256,256]{1,0:T(8,128)(2,1)S(1)}, u32[]{:S(2)}, u32[]{:S(2)}) collective-permute-start(bf16[256,256]{1,0:T(8,128)(2,1)} %node_ref.3), channel_id=1, source_target_pairs={{0,2},{1,3},{2,0},{3,1},{4,6},{5,7},{6,4},{7,5},{8,10},{9,11},{10,... | collective-permute-start | bytes 393224 | tf_op jit(solution)/shard_map/ppermute | solution.py:499
  3.7 1.6 %collective-permute-start = (s32[1,16,32]{2,1,0:T(8,128)}, s32[1,16,32]{2,1,0:T(8,128)S(1)}, u32[]{:S(2)}, u32[]{:S(2)}) collective-permute-start(s32[1,16,32]{2,1,0:T(8,128)} %param.24), channel_id=1, source_target_pairs={{0,4},{1,5},{2,6},{3,7},{4,0},{5,1},{6,2},{7,3},{8,12},{9,13},{10,... | collective-permute-start | bytes 6152 | tf_op jit(solution)/shard_map/ppermute | solution.py:499
  5.2 2.3 %collective-permute-done = s32[1,16,32]{2,1,0:T(8,128)S(1)} collective-permute-done((s32[1,16,32]{2,1,0:T(8,128)}, s32[1,16,32]{2,1,0:T(8,128)S(1)}, u32[]{:S(2)}, u32[]{:S(2)}) %collective-permute-start) | collective-permute-done | bytes 2080 | tf_op jit(solution)/shard_map/ppermute | solution.py:499
  7.5 0.7 pad_add_fusion.1
  8.2 2.6 %collective-permute-start.1 = (s32[2,16,32]{2,1,0:T(8,128)S(1)}, s32[2,16,32]{2,1,0:T(8,128)S(1)}, u32[]{:S(2)}, u32[]{:S(2)}) collective-permute-start(s32[2,16,32]{2,1,0:T(8,128)S(1)} %pad_add_fusion.1), channel_id=1, source_target_pairs={{0,8},{1,9},{2,10},{3,11},{4,12},{5,13},{6,14},{7,15},{8,0},{9,1},... | collective-permute-start | bytes 12296 | tf_op jit(solution)/shard_map/ppermute | solution.py:499
  12.0 1.3 %reduce.3 = s32[40]{0:T(128)S(1)} reduce(s32[1,40]{1,0:T(1,128)} %param.27, s32[]{:T(128)} %broadcast.23), dimensions={0}, to_apply=%param.27.reduce_sub_computation.3 | reduce | bytes 324 | tf_op args[13]
  13.5 1.3 %pad_add_fusion.lists_ref = s32[4,16,32]{2,1,0:T(8,128)} fusion(s32[2,16,32]{2,1,0:T(8,128)S(1)} %collective-permute-done.1, s32[1,16,32]{2,1,0:T(8,128)S(1)} %collective-permute-done, s32[1,16,32]{2,1,0:T(8,128)} %param.24), kind=kLoop, calls=%fused_computation.1 | loop fusion | flops 4096 | bytes 16384 | tf_op jit(solution)/shard_map/concatenate | solution.py:505
  16.1 2.2 %serve_rows.1 = bf16[4,128,256]{2,1,0:T(8,128)(2,1)} custom-call(s32[3]{0:T(128)} %pad_add_fusion.2.place_ref.core_ref, s32[4,16,32]{2,1,0:T(8,128)} %pad_add_fusion.lists_ref, bf16[256,256]{1,0:T(8,128)(2,1)} %node_ref.3, bf16[256,256]{1,0:T(8,128)(2,1)} %copy-done.6, bf16[256,256]{1,0:T(8,128)(2,1)} %copy-done.5, bf16[256,256]{1,0:T(8,128)(2,1)} %copy-done.7), custom_call_target="tpu_custom_call" | custom-call | tf_op jit(solution)/shard_map/serve_rows/pallas_call | solution.py:62
  18.3 4.3 %all-to-all-start = ((bf16[4,128,256]{2,1,0:T(8,128)(2,1)}), bf16[4,128,256]{2,1,0:T(8,128)(2,1)S(1)}, u32[]{:S(2)}, u32[]{:S(2)}) async-start(bf16[4,128,256]{2,1,0:T(8,128)(2,1)} %serve_rows.1), calls=%async_computation | async-start | bytes 524288 | tf_op jit(solution)/shard_map/all_to_all | solution.py:513
  23.2 7.3 %prepare_edges.1 = (f32[4,256,1280]{2,1,0:T(8,128)}, bf16[4,256,1280]{2,1,0:T(8,128)(2,1)}) custom-call(bf16[5120,256]{1,0:T(8,128)(2,1)} %edge_ref.1, bf16[5120,256]{1,0:T(8,128)(2,1)} %cot_ref.3, s32[4,1,1280]{2,1,0:T(1,128)} %bitcast.16, bf16[256,256]{1,0:T(8,128)(2,1)} %node_ref.3, bf16[768,256]{1,0:T(8,128)(2,1)} %w_in_ref.5), custom_call_target="tpu_custom_call" | custom-call | flops 1342177280 | bytes 10485760 | tf_op jit(solution)/shard_map/prepare_edges/pallas_call | solution.py:97
  30.6 0.9 all-to-all-done
  32.2 18.9 %layer_backward.1 = (bf16[4,256,1280]{2,1,0:T(8,128)(2,1)}, f32[256,256]{1,0:T(8,128)}, bf16[8,160,256]{2,1,0:T(8,128)(2,1)}, bf16[8,160,256]{2,1,0:T(8,128)(2,1)}) custom-call(s32[3]{0:T(128)} %pad_add_fusion.2.place_ref.core_ref, f32[4,256,1280]{2,1,0:T(8,128)} %get-tuple-element.27.part_hbm, bf16[4,256,1280]{2,1,0:T(8,128)(2,1)} %get-tuple-element.28.cot_hbm, ...), custom_call_target="tpu_custom_call" | custom-call | tf_op jit(solution)/shard_map/layer_backward/pallas_call | solution.py:317
  51.2 2.3 %collective-permute-done.5.got_ref = bf16[8,160,256]{2,1,0:T(8,128)(2,1)S(1)} collective-permute-done((bf16[8,160,256]{2,1,0:T(8,128)(2,1)}, bf16[8,160,256]{2,1,0:T(8,128)(2,1)S(1)}, u32[]{:S(2)}, u32[]{:S(2)}) %collective-permute-start.5) | collective-permute-done | bytes 655392 | tf_op jit(solution)/shard_map/ppermute | solution.py:544
  53.5 0.8 copy-done.3
  54.3 2.3 %join_cores.1 = bf16[8,192,256]{2,1,0:T(8,128)(2,1)} custom-call(bf16[8,160,256]{2,1,0:T(8,128)(2,1)} %get-tuple-element.30.pack_ref, bf16[8,160,256]{2,1,0:T(8,128)(2,1)} %copy-done.3), custom_call_target="tpu_custom_call" | custom-call | tf_op jit(solution)/shard_map/join_cores/pallas_call | solution.py:397
  56.6 4.1 %all-to-all-start.1 = ((bf16[8,192,256]{2,1,0:T(8,128)(2,1)}), bf16[8,192,256]{2,1,0:T(8,128)(2,1)S(1)}, u32[]{:S(2)}, u32[]{:S(2)}) async-start(bf16[8,192,256]{2,1,0:T(8,128)(2,1)} %join_cores.1), calls=%async_computation.1 | async-start | bytes 1572864 | tf_op jit(solution)/shard_map/all_to_all | solution.py:546
  60.8 5.3 %edge_result.1 = bf16[5120,256]{1,0:T(8,128)(2,1)} custom-call(bf16[4,256,1280]{2,1,0:T(8,128)(2,1)} %get-tuple-element.32.grad_ref, bf16[5120,256]{1,0:T(8,128)(2,1)} %cot_ref.3, bf16[768,256]{1,0:T(8,128)(2,1)} %w_in_ref.5), custom_call_target="tpu_custom_call" | custom-call | flops 671088640 | bytes 7864320 | tf_op jit(solution)/shard_map/edge_result/pallas_call | solution.py:367
  66.1 15.2 %all-to-all-done.1.back_ref = bf16[8,192,256]{2,1,0:T(8,128)(2,1)S(1)} async-done(((bf16[8,192,256]{2,1,0:T(8,128)(2,1)}), bf16[8,192,256]{2,1,0:T(8,128)(2,1)S(1)}, u32[]{:S(2)}, u32[]{:S(2)}) %all-to-all-start.1) | async-done | bytes 786464 | tf_op jit(solution)/shard_map/all_to_all | solution.py:546
  81.2 0.9 copy-done
  82.1 2.4 %settle_sums.1 = (f32[256,256]{1,0:T(8,128)}, bf16[8,128,256]{2,1,0:T(8,128)(2,1)}) custom-call(s32[3]{0:T(128)} %pad_add_fusion.2.place_ref.core_ref, bf16[8,192,256]{2,1,0:T(8,128)(2,1)} %copy-done, f32[256,256]{1,0:T(8,128)} %get-tuple-element.34.local_ref), custom_call_target="tpu_custom_call" | custom-call | tf_op jit(solution)/shard_map/settle_sums/pallas_call | solution.py:425
  84.6 18.3 %all_to_all.15.mine_ref = bf16[8,128,256]{2,1,0:T(8,128)(2,1)S(1)} all-to-all(bf16[8,128,256]{2,1,0:T(8,128)(2,1)} %get-tuple-element.37), channel_id=1, replica_groups={{0,2,4,6,8,10,12,14},{1,3,5,7,9,11,13,15},{16,18,20,22,24,26,28,30},{17..., dimensions={0} | all-to-all | bytes 1048576 | tf_op jit(solution)/shard_map/all_to_all | solution.py:552
  102.8 1.9 %collective-permute-done.6.theirs_ref = bf16[8,128,256]{2,1,0:T(8,128)(2,1)S(1)} collective-permute-done((bf16[8,128,256]{2,1,0:T(8,128)(2,1)S(1)}, bf16[8,128,256]{2,1,0:T(8,128)(2,1)S(1)}, u32[]{:S(2)}, u32[]{:S(2)}) %collective-permute-start.6) | collective-permute-done | bytes 524320 | tf_op jit(solution)/shard_map/ppermute | solution.py:555
  104.7 0.8 copy-done.4
  105.5 2.6 %assemble_sums.1 = (f32[768,256]{1,0:T(8,128)}, f32[256,256]{1,0:T(8,128)}, f32[512,256]{1,0:T(8,128)}, f32[256,256]{1,0:T(8,128)}, f32[1,256]{1,0:T(1,128)}, /*index=5*/f32[1,256]{1,0:T(1,128)}) custom-call(s32[3]{0:T(128)} %pad_add_fusion.2.place_ref.core_ref, bf16[8,128,256]{2,1,0:T(8,128)(2,1)} %copy-done.1, bf16[8,128,256]{2,1,0:T(8,128)(2,1)} %copy-done.4), custom_call_target="tpu_custom_call" | custom-call | tf_op jit(solution)/shard_map/assemble_sums/pallas_call | solution.py:458
  (28 shorter events, 4.0 us)
Async XLA Ops:
  0.6 10.2 %collective-permute-start.3 = (bf16[256,256]{1,0:T(8,128)(2,1)}, bf16[256,256]{1,0:T(8,128)(2,1)S(1)}, u32[]{:S(2)}, u32[]{:S(2)}) collective-permute-start(bf16[256,256]{1,0:T(8,128)(2,1)} %node_ref.3), channel_id=1, source_target_pairs={{0,2},{1,3},{2,0},{3,1},{4,6},{5,7},{6,4},{7,5},{8,10},{9,11},{10,... | collective-permute-start | bytes 393224 | tf_op jit(solution)/shard_map/ppermute | solution.py:499
  3.7 11.1 %collective-permute-start.2 = (bf16[256,256]{1,0:T(8,128)(2,1)}, bf16[256,256]{1,0:T(8,128)(2,1)S(1)}, u32[]{:S(2)}, u32[]{:S(2)}) collective-permute-start(bf16[256,256]{1,0:T(8,128)(2,1)} %node_ref.3), channel_id=1, source_target_pairs={{0,1},{1,0},{2,3},{3,2},{4,5},{5,4},{6,7},{7,6},{8,9},{9,8},{10,11... | collective-permute-start | bytes 393224 | tf_op jit(solution)/shard_map/ppermute | solution.py:499
  3.7 3.9 %collective-permute-start = (s32[1,16,32]{2,1,0:T(8,128)}, s32[1,16,32]{2,1,0:T(8,128)S(1)}, u32[]{:S(2)}, u32[]{:S(2)}) collective-permute-start(s32[1,16,32]{2,1,0:T(8,128)} %param.24), channel_id=1, source_target_pairs={{0,4},{1,5},{2,6},{3,7},{4,0},{5,1},{6,2},{7,3},{8,12},{9,13},{10,... | collective-permute-start | bytes 6152 | tf_op jit(solution)/shard_map/ppermute | solution.py:499
  8.2 5.2 %collective-permute-start.1 = (s32[2,16,32]{2,1,0:T(8,128)S(1)}, s32[2,16,32]{2,1,0:T(8,128)S(1)}, u32[]{:S(2)}, u32[]{:S(2)}) collective-permute-start(s32[2,16,32]{2,1,0:T(8,128)S(1)} %pad_add_fusion.1), channel_id=1, source_target_pairs={{0,8},{1,9},{2,10},{3,11},{4,12},{5,13},{6,14},{7,15},{8,0},{9,1},... | collective-permute-start | bytes 12296 | tf_op jit(solution)/shard_map/ppermute | solution.py:499
  10.8 4.0 %copy-start.5 = (bf16[256,256]{1,0:T(8,128)(2,1)}, bf16[256,256]{1,0:T(8,128)(2,1)S(1)}, u32[]{:S(2)}) copy-start(bf16[256,256]{1,0:T(8,128)(2,1)S(1)} %collective-permute-done.3.refs_2_) | copy-start | bytes 393220
  10.8 4.0 %collective-permute-start.4 = (bf16[256,256]{1,0:T(8,128)(2,1)S(1)}, bf16[256,256]{1,0:T(8,128)(2,1)S(1)}, u32[]{:S(2)}, u32[]{:S(2)}) collective-permute-start(bf16[256,256]{1,0:T(8,128)(2,1)S(1)} %collective-permute-done.3.refs_2_), channel_id=1, source_target_pairs={{0,1},{1,0},{2,3},{3,2},{4,5},{5,4},{6,7},{7,6},{8,9},{9,8},{10,11... | collective-permute-start | bytes 393224 | tf_op jit(solution)/shard_map/ppermute | solution.py:499
  14.8 0.7 copy-start.6
  15.5 0.7 copy-start.7
  18.3 13.2 %all-to-all-start = ((bf16[4,128,256]{2,1,0:T(8,128)(2,1)}), bf16[4,128,256]{2,1,0:T(8,128)(2,1)S(1)}, u32[]{:S(2)}, u32[]{:S(2)}) async-start(bf16[4,128,256]{2,1,0:T(8,128)(2,1)} %serve_rows.1), calls=%async_computation | async-start | bytes 524288 | tf_op jit(solution)/shard_map/all_to_all | solution.py:513
  31.5 0.7 copy-start.2
  51.1 2.4 %collective-permute-start.5 = (bf16[8,160,256]{2,1,0:T(8,128)(2,1)}, bf16[8,160,256]{2,1,0:T(8,128)(2,1)S(1)}, u32[]{:S(2)}, u32[]{:S(2)}) collective-permute-start(bf16[8,160,256]{2,1,0:T(8,128)(2,1)} %get-tuple-element.31), channel_id=1, source_target_pairs={{0,1},{1,0},{2,3},{3,2},{4,5},{5,4},{6,7},{7,6},{8,9},{9,8},{10,11... | collective-permute-start | bytes 1966088 | tf_op jit(solution)/shard_map/ppermute | solution.py:544
  53.5 0.8 copy-start.3
  56.6 24.6 %all-to-all-start.1 = ((bf16[8,192,256]{2,1,0:T(8,128)(2,1)}), bf16[8,192,256]{2,1,0:T(8,128)(2,1)S(1)}, u32[]{:S(2)}, u32[]{:S(2)}) async-start(bf16[8,192,256]{2,1,0:T(8,128)(2,1)} %join_cores.1), calls=%async_computation.1 | async-start | bytes 1572864 | tf_op jit(solution)/shard_map/all_to_all | solution.py:546
  81.2 0.9 copy-start
  102.8 1.9 %copy-start.1 = (bf16[8,128,256]{2,1,0:T(8,128)(2,1)}, bf16[8,128,256]{2,1,0:T(8,128)(2,1)S(1)}, u32[]{:S(2)}) copy-start(bf16[8,128,256]{2,1,0:T(8,128)(2,1)S(1)} %all_to_all.15.mine_ref) | copy-start | bytes 1572868
  102.8 1.9 %collective-permute-start.6 = (bf16[8,128,256]{2,1,0:T(8,128)(2,1)S(1)}, bf16[8,128,256]{2,1,0:T(8,128)(2,1)S(1)}, u32[]{:S(2)}, u32[]{:S(2)}) collective-permute-start(bf16[8,128,256]{2,1,0:T(8,128)(2,1)S(1)} %all_to_all.15.mine_ref), channel_id=1, source_target_pairs={{0,1},{1,0},{2,3},{3,2},{4,5},{5,4},{6,7},{7,6},{8,9},{9,8},{10,11... | collective-permute-start | bytes 1572872 | tf_op jit(solution)/shard_map/ppermute | solution.py:555
  104.7 0.8 copy-start.4

commit v4 on v3

--- a/solution.py
+++ b/solution.py
@@ -33,6 +33,10 @@
     return jnp.where(rows == index_row.astype(jnp.int16), jnp.ones((), BF), jnp.zeros((), BF))
 
 
+def in_vmem(array):
+    return pltpu.with_memory_space_constraint(array, pltpu.VMEM)
+
+
 def vmem():
     return pl.BlockSpec(memory_space=pltpu.VMEM)
 
@@ -41,14 +45,15 @@
     return pl.BlockSpec(shape, lambda *_: (0,) * len(shape))
 
 
-def serve_kernel(place_ref, lists_ref, *refs):
-    members, rows_ref = refs[:-1], refs[-1]
-    groups, _, cap = lists_ref.shape
+def serve_kernel(place_ref, *refs):
+    members, lists, rows_ref = refs[:GROUP], refs[GROUP:-1], refs[-1]
+    entries = [ref.at[i] for ref in lists for i in range(ref.shape[0])]
+    groups, cap = len(entries), entries[0].shape[1]
     group, member = place_ref[1], place_ref[2] % GROUP
     for k, nodes_ref in enumerate(members):
         owner = member ^ k
         wanted = jnp.concatenate(
-            [lists_ref[j, pl.ds(group * GROUP + owner, 1), :] for j in range(groups)], axis=1
+            [entry[pl.ds(group * GROUP + owner, 1), :] for entry in entries], axis=1
         )
         picks = onehot_rows(nodes_ref.shape[0], wanted)
         rows = dot(picks, nodes_ref[...], 0, 0).astype(BF)
@@ -58,15 +63,15 @@
 
 
 def serve(place, lists, members):
-    groups, _, cap = lists.shape
+    groups, cap = sum(part.shape[0] for part in lists), lists[0].shape[2]
     return pl.pallas_call(
         serve_kernel,
-        out_shape=jax.ShapeDtypeStruct((groups, GROUP * cap, members[0].shape[1]), BF),
-        in_specs=[pl.BlockSpec(memory_space=pltpu.SMEM)] + [vmem()] * (1 + GROUP),
+        out_shape=pltpu.VMEM((groups, GROUP * cap, members[0].shape[1]), BF),
+        in_specs=[pl.BlockSpec(memory_space=pltpu.SMEM)] + [vmem()] * (GROUP + len(lists)),
         out_specs=vmem(),
         compiler_params=pltpu.CompilerParams(vmem_limit_bytes=VMEM_LIMIT),
         name="serve_rows",
-    )(place, lists, *members)
+    )(place, members[0], *map(in_vmem, members[1:]), lists[0], *map(in_vmem, lists[1:]))
 
 
 def prepare_kernel(
@@ -120,9 +125,9 @@
     edge_hbm,
     recv_ref,
     slot_ref,
+    fetched_ref,
     wanted_ref,
     valid_ref,
-    fetched_ref,
     node_ref,
     node_cot_ref,
     w_in_ref,
@@ -133,8 +138,8 @@
     gain_node_ref,
     grad_pre_hbm,
     node_local_ref,
-    keep_hbm,
-    send_hbm,
+    keep_ref,
+    send_ref,
     part,
     cot,
     edge,
@@ -157,7 +162,6 @@
     pack,
     sems,
     out_sems,
-    pack_sems,
 ):
     chunks, latent, width = part.shape
     nodes = node_ref.shape[0]
@@ -178,10 +182,10 @@
         for c in range(chunks):
             copy(c).start()
 
-    send_part[...] = dot(w_in_ref[latent : 2 * latent, :], fetched_ref[...], 0, 1).astype(BF)
     w_out_t[...] = w_out_ref[...].T
     gain_column[...] = jnp.broadcast_to(gain_edge_ref[...], (128, latent)).T
     summed_acc[...] = jnp.zeros_like(summed_acc)
+    send_part[...] = dot(w_in_ref[latent : 2 * latent, :], fetched_ref[...], 0, 1).astype(BF)
     for c in range(chunks):
         part_copy(c).wait()
     w_in_acc[...] = jnp.zeros_like(w_in_acc)
@@ -293,19 +297,15 @@
 
         @pl.when(core == own)
         def _():
-            keep = pltpu.make_async_copy(pack.at[own], keep_hbm, pack_sems.at[0])
-            send = pltpu.make_async_copy(pack.at[1 - own], send_hbm, pack_sems.at[1])
-            send.start()
-            keep.start()
-            send.wait()
-            keep.wait()
+            keep_ref[...] = pack[own]
+            send_ref[...] = pack[1 - own]
 
     for c in range(chunks):
         pltpu.make_async_copy(grad_pre.at[c], grad_pre_hbm.at[c], out_sems.at[c]).wait()
 
 
 def layer(
-    core, part, cot_t, edge_lat, recv_rows, slot_rows, wanted, valid_rows, fetched, node_lat, node_cot, weights, bands
+    core, part, cot_t, edge_lat, recv_rows, slot_rows, fetched, wanted, valid_rows, node_lat, node_cot, weights, bands
 ):
     chunks, hidden, width = part.shape
     edges = edge_lat.reshape(chunks, width, -1)
@@ -319,11 +319,11 @@
         out_shape=[
             jax.ShapeDtypeStruct((chunks, hidden, width), BF),
             jax.ShapeDtypeStruct((nodes, latent), F32),
-            jax.ShapeDtypeStruct((bands // 2, cap + piece_rows + TAIL, latent), BF),
-            jax.ShapeDtypeStruct((bands // 2, cap + piece_rows + TAIL, latent), BF),
+            pltpu.VMEM((bands // 2, cap + piece_rows + TAIL, latent), BF),
+            pltpu.VMEM((bands // 2, cap + piece_rows + TAIL, latent), BF),
         ],
         in_specs=[pl.BlockSpec(memory_space=pltpu.SMEM)] + [hbm] * 3 + [vmem()] * 13,
-        out_specs=[hbm, vmem(), hbm, hbm],
+        out_specs=[hbm, vmem(), vmem(), vmem()],
         scratch_shapes=[
             pltpu.VMEM((chunks, hidden, width), F32),
             pltpu.VMEM((chunks, latent, width), BF),
@@ -347,11 +347,10 @@
             pltpu.VMEM((2, bands // 2, cap + piece_rows + TAIL, latent), BF),
             pltpu.SemaphoreType.DMA((3, chunks)),
             pltpu.SemaphoreType.DMA((chunks,)),
-            pltpu.SemaphoreType.DMA((2,)),
         ],
         compiler_params=pltpu.CompilerParams(vmem_limit_bytes=VMEM_LIMIT),
         name="layer_backward",
-    )(core, part, cot_t, edges, recv_rows, slot_rows, wanted, valid_rows, fetched, node_lat, node_cot, *weights)
+    )(core, part, cot_t, edges, recv_rows, slot_rows, in_vmem(fetched), wanted, valid_rows, node_lat, node_cot, *weights)
 
 
 def edge_kernel(grad_ref, cot_ref, w_in_ref, out_ref):
@@ -384,11 +383,11 @@
     )(grad_pre, edge_cot, w_edge_in)
 
 
-def join_kernel(cap, pack_ref, got_ref, out_ref):
-    out_ref[:, :cap, :] = pack_ref[:, :cap, :]
+def join_kernel(cap, keep_ref, got_ref, out_ref):
+    out_ref[:, :cap, :] = keep_ref[:, :cap, :]
     out_ref[:, cap : 2 * cap, :] = got_ref[:, :cap, :]
     out_ref[:, 2 * cap :, :] = (
-        pack_ref[:, cap:, :].astype(F32) + got_ref[:, cap:, :].astype(F32)
+        keep_ref[:, cap:, :].astype(F32) + got_ref[:, cap:, :].astype(F32)
     ).astype(BF)
 
 
@@ -396,14 +395,33 @@
     chips, height, latent = keep.shape
     return pl.pallas_call(
         functools.partial(join_kernel, cap),
-        out_shape=jax.ShapeDtypeStruct((chips, height + cap, latent), BF),
+        out_shape=pltpu.VMEM((chips, height + cap, latent), BF),
         in_specs=[vmem(), vmem()],
         out_specs=vmem(),
         name="join_cores",
-    )(keep, got)
-
-
-def settle_kernel(cap, core_ref, back_ref, local_ref, node_grad_ref, piece_ref):
+    )(in_vmem(keep), in_vmem(got))
+
+
+def total_kernel(sums_ref, pieces_ref):
+    chips, height, _ = pieces_ref.shape
+    first = sums_ref.shape[1] - height
+    piece = jnp.sum(sums_ref[:, first:, :].astype(F32), axis=0).astype(BF)
+    for chip in range(chips):
+        pieces_ref[chip] = piece
+
+
+def total(sums, cap):
+    chips, height, latent = sums.shape
+    return pl.pallas_call(
+        total_kernel,
+        out_shape=pltpu.VMEM((chips, height - 2 * cap, latent), BF),
+        in_specs=[vmem()],
+        out_specs=vmem(),
+        name="total_piece",
+    )(in_vmem(sums))
+
+
+def settle_kernel(cap, core_ref, back_ref, local_ref, node_grad_ref):
     chips, height, latent = back_ref.shape
     rows = back_ref[:, : 2 * cap, :].reshape(chips * 2 * cap, latent)
     core = core_ref[0]
@@ -415,54 +433,66 @@
         lists.append(jnp.where(core == 0, second, first))
     picks = onehot_rows(local_ref.shape[0], jnp.concatenate(lists, axis=1).astype(jnp.int32))
     node_grad_ref[...] = local_ref[...] + dot(picks, rows, 1, 0)
-    piece = jnp.sum(back_ref[:, 2 * cap :, :].astype(F32), axis=0).astype(BF)
-    for chip in range(chips):
-        piece_ref[chip] = piece
 
 
 def settle(place, back, node_local, cap):
-    chips, height, latent = back.shape
     return pl.pallas_call(
         functools.partial(settle_kernel, cap),
-        out_shape=[
-            jax.ShapeDtypeStruct(node_local.shape, F32),
-            jax.ShapeDtypeStruct((chips, height - 2 * cap, latent), BF),
-        ],
+        out_shape=jax.ShapeDtypeStruct(node_local.shape, F32),
         in_specs=[pl.BlockSpec(memory_space=pltpu.SMEM)] + [vmem()] * 2,
-        out_specs=[vmem()] * 2,
+        out_specs=vmem(),
         name="settle_sums",
-    )(place, back, node_local)
+    )(place, in_vmem(back), node_local)
 
 
 def assemble_kernel(core_ref, mine_ref, theirs_ref, *refs):
-    outs, rows = refs[:-1], refs[-1]
+    outs, (rows, out_sems) = refs[:-2], refs[-2:]
     chips, height, latent = mine_ref.shape
     body = height - TAIL
     core = core_ref[0]
+    starts, at = [], 0
+    for out in outs[:-2]:
+        starts.append(at)
+        at += out.shape[0]
+
+    def outgoing(k):
+        source = rows.at[pl.ds(starts[k], outs[k].shape[0])]
+        return pltpu.make_async_copy(source, outs[k], out_sems.at[k])
+
+    sent = 0
     for chip in range(chips):
-        for ref, side in ((mine_ref, core), (theirs_ref, 1 - core)):
-            start = pl.multiple_of((2 * chip + side) * body, body)
-            rows[pl.ds(start, body), :] = ref[chip, :body, :].astype(F32)
-    first, second = mine_ref[0, body:, :].astype(F32), theirs_ref[0, body:, :].astype(F32)
-    outs[-2][...] = jnp.where(core == 0, first, second)[:1]
-    outs[-1][...] = jnp.where(core == 0, second, first)[:1]
-    at = 0
-    for out in outs[:-2]:
-        out[...] = rows[at : at + out.shape[0], :]
-        at += out.shape[0]
+        for side, ref in enumerate((mine_ref, theirs_ref)):
+            place = 2 * chip + (core if side == 0 else 1 - core)
+            rows[pl.ds(pl.multiple_of(place * body, body), body), :] = ref[
+                chip, :body, :
+            ].astype(F32)
+        if chip == 0:
+            first, second = mine_ref[0, body:, :].astype(F32), theirs_ref[0, body:, :].astype(F32)
+            outs[-2][...] = jnp.where(core == 0, first, second)[:1]
+            outs[-1][...] = jnp.where(core == 0, second, first)[:1]
+        while sent < len(starts) and starts[sent] + outs[sent].shape[0] <= 2 * (chip + 1) * body:
+            outgoing(sent).start()
+            sent += 1
+    for k in range(len(starts)):
+        outgoing(k).wait()
 
 
 def assemble(place, mine, theirs, latent):
     chips, height, width = mine.shape
     heights = (3 * latent, latent, 2 * latent, latent, 1, 1)
+    hbm = pl.BlockSpec(memory_space=pl.ANY)
     return pl.pallas_call(
         assemble_kernel,
         out_shape=[jax.ShapeDtypeStruct((rows, width), F32) for rows in heights],
         in_specs=[pl.BlockSpec(memory_space=pltpu.SMEM), vmem(), vmem()],
-        out_specs=[vmem()] * len(heights),
-        scratch_shapes=[pltpu.VMEM((2 * chips * (height - TAIL), width), F32)],
+        out_specs=[hbm] * 4 + [vmem()] * 2,
+        scratch_shapes=[
+            pltpu.VMEM((2 * chips * (height - TAIL), width), F32),
+            pltpu.SemaphoreType.DMA((4,)),
+        ],
+        compiler_params=pltpu.CompilerParams(vmem_limit_bytes=VMEM_LIMIT),
         name="assemble_sums",
-    )(place, mine, theirs)
+    )(place, in_vmem(mine), in_vmem(theirs))
 
 
 def per_device(
@@ -499,24 +529,25 @@
         return lax.ppermute(array, "band", [(i, i ^ step) for i in range(bands)])
 
     across = swap(node_lat, 2)
-    lists = fetch_idx
+    lists = [fetch_idx]
     step = GROUP
     while step < bands:
-        lists = jnp.concatenate([lists, swap(lists, step)], axis=0)
+        held = lists[0] if len(lists) == 1 else jnp.concatenate(lists, axis=0)
+        lists.append(swap(held, step))
         step *= 2
     members = (node_lat, swap(node_lat, 1), across, swap(across, 1))
     rows = serve(place, lists, members)
     valid = jnp.arange(128, dtype=jnp.int32)[None, :] < block_fill[0][:, None]
     valid = valid.astype(F32).reshape(chunks, 1, CHUNK)
     recv_rows = edge_recv.reshape(chunks, 1, CHUNK)
-    recv_rows, rows = lax.optimization_barrier((recv_rows, rows))
+    w_edge_first, rows = lax.optimization_barrier((w_edge_in, rows))
     fetched = lax.all_to_all(
         rows, "band", split_axis=0, concat_axis=0, tiled=True, axis_index_groups=like_placed
     ).reshape(slots, latent)
 
     slot_rows = edge_slot.reshape(chunks, 1, CHUNK)
     part, cot_t = prepare(
-        edge_lat, edge_cot, recv_rows, node_lat, w_edge_in
+        edge_lat, edge_cot, recv_rows, node_lat, w_edge_first
     )
     weights = (
         w_edge_in,
@@ -533,9 +564,9 @@
         edge_lat,
         recv_rows,
         slot_rows,
+        fetched,
         fetch_idx[0],
         valid,
-        fetched,
         node_lat,
         node_cot,
         weights,
@@ -548,10 +579,12 @@
     )
     edge_grad = edge_result(grad_pre, edge_cot, w_edge_in)
     back, edge_grad = lax.optimization_barrier((back, edge_grad))
-    node_grad, piece = settle(place, back, node_local, cap)
+    pieces = total(back, cap)
     mine = lax.all_to_all(
-        piece, "band", split_axis=0, concat_axis=0, tiled=True, axis_index_groups=same_core
-    )
+        pieces, "band", split_axis=0, concat_axis=0, tiled=True, axis_index_groups=same_core
+    )
+    node_grad = settle(place, back, node_local, cap)
+    mine, node_grad = lax.optimization_barrier((mine, node_grad))
     theirs = lax.ppermute(mine, "band", other_core)
     sums = assemble(place, mine, theirs, latent)
     return (

time: 109 us -> 99.7 us (0.915)
  blocking collectives: 18.3 us -> 0 us
  waiting for transfers between devices: 22.6 us -> 34.7 us
  starting transfers between devices: 15.7 us -> 20.7 us
  local copies, waits for them, and re-layouts: 5.21 us -> 0.7 us
  Pallas kernels: 41 us -> 38.9 us
  other arithmetic: 4.58 us -> 3.24 us
    all_to_all x1 -> x0, blocking collectives: 18.3 us -> none  [per_device(): lax.all_to_all(piece, 'band', split_axis=0, concat_axis=0, tiled=True, ax...]
    all_to_all x0 -> x1, waiting for transfers between devices: none -> 12.7 us  [per_device(): lax.all_to_all(pieces, 'band', split_axis=0, concat_axis=0, tiled=True, a...]
    unnamed x17 -> x1, local copies, waits for them, and re-layouts: 5.02 us -> 0.51 us
    all_to_all x0 -> x1, starting transfers between devices: none -> 3.59 us  [per_device(): lax.all_to_all(pieces, 'band', split_axis=0, concat_axis=0, tiled=True, a...]
    concatenate x2 -> x1, other arithmetic: 2.02 us -> 0.7 us  [per_device(): held = lists[0] if len(lists) == 1 else jnp.concatenate(lists, axis=0)]
    all_to_all x1, starting transfers between devices: 4.15 us -> 5.44 us  [per_device(): lax.all_to_all(joined, 'band', split_axis=0, concat_axis=0, tiled=True, a...]
    pallas_call x3 -> x4, Pallas kernels: 6.91 us -> 5.87 us  [the longest x1 2.01 us: settle(): pl.pallas_call(functools.partial(settle_kernel, cap), out_shape=jax.Shape...]
  transfers between devices with their start and end apart: 9 -> 10, of which waited for: 5 -> 7; matrix products, arithmetic and copies ran while one was open for 5% -> 4% of each run, Pallas kernels for 12% -> 15%
where the time goes in v4:
time: 99.7 us; the launch traced here: 99 us
  Pallas kernels  38.9 us (39%)
  waiting for transfers between devices  34.7 us (35%)
  starting transfers between devices  20.7 us (21%)
  other arithmetic  3.24 us (3%)
    pallas_call x1, Pallas kernels, layer(): pl.pallas_call(functools.partial(layer_kernel, piece_rows), out_shape=[ja...  17.9 us
    all_to_all x1, waiting for transfers between devices, per_device(): lax.all_to_all(joined, 'band', split_axis=0, concat_axis=0, tiled=True, a...  15.2 us
    all_to_all x1, waiting for transfers between devices, per_device(): lax.all_to_all(pieces, 'band', split_axis=0, concat_axis=0, tiled=True, a...  12.7 us
    pallas_call x1, Pallas kernels, prepare(): pl.pallas_call(prepare_kernel, grid=(chunks,), out_shape=[jax.ShapeDtypeS...  7.34 us
    ppermute x5, starting transfers between devices, swap(): return lax.ppermute(array, 'band', [(i, i ^ step) for i in range(bands)])  7.27 us
    all_to_all x1, starting transfers between devices, per_device(): lax.all_to_all(joined, 'band', split_axis=0, concat_axis=0, tiled=True, a...  5.44 us
    pallas_call x1, Pallas kernels, edge_result(): pl.pallas_call(edge_kernel, grid=(chunks,), out_shape=jax.ShapeDtypeStruc...  5.27 us
    all_to_all x1, starting transfers between devices, per_device(): lax.all_to_all(rows, 'band', split_axis=0, concat_axis=0, tiled=True, axi...  4.34 us
  transfers between devices with their start and end apart: 10, of which 7 were waited for; matrix products, arithmetic and copies ran while one was open for 4% of the time, Pallas kernels for 15%

profile of v4, /device:TPU:0, one launch (start us, length us, event | category | flops | bytes accessed | tf_op | source)
XLA Modules:
  0.0 99.0 jit_solution(16012927682970511392)
XLA Ops:
  0.6 3.0 %collective-permute-start.1 = (bf16[256,256]{1,0:T(8,128)(2,1)}, bf16[256,256]{1,0:T(8,128)(2,1)S(1)}, u32[]{:S(2)}, u32[]{:S(2)}) collective-permute-start(bf16[256,256]{1,0:T(8,128)(2,1)} %node_ref.3), channel_id=1, source_target_pairs={{0,2},{1,3},{2,0},{3,1},{4,6},{5,7},{6,4},{7,5},{8,10},{9,11},{10,... | collective-permute-start | bytes 393224 | tf_op jit(solution)/shard_map/ppermute | solution.py:529
  3.7 1.6 %collective-permute-start.3 = (s32[1,16,32]{2,1,0:T(8,128)}, s32[1,16,32]{2,1,0:T(8,128)S(1)}, u32[]{:S(2)}, u32[]{:S(2)}) collective-permute-start(s32[1,16,32]{2,1,0:T(8,128)} %refs_4_.1), channel_id=1, source_target_pairs={{0,4},{1,5},{2,6},{3,7},{4,0},{5,1},{6,2},{7,3},{8,12},{9,13},{10,... | collective-permute-start | bytes 6152 | tf_op jit(solution)/shard_map/ppermute | solution.py:529
  5.2 2.1 %collective-permute-done.1.refs_2_ = bf16[256,256]{1,0:T(8,128)(2,1)S(1)} collective-permute-done((bf16[256,256]{1,0:T(8,128)(2,1)}, bf16[256,256]{1,0:T(8,128)(2,1)S(1)}, u32[]{:S(2)}, u32[]{:S(2)}) %collective-permute-start.1) | collective-permute-done | bytes 131104 | tf_op jit(solution)/shard_map/ppermute | solution.py:529
  7.5 0.7 pad_add_fusion
  8.2 2.7 %collective-permute-start.4 = (s32[2,16,32]{2,1,0:T(8,128)S(1)}, s32[2,16,32]{2,1,0:T(8,128)S(1)}, u32[]{:S(2)}, u32[]{:S(2)}) collective-permute-start(s32[2,16,32]{2,1,0:T(8,128)S(1)} %pad_add_fusion), channel_id=1, source_target_pairs={{0,8},{1,9},{2,10},{3,11},{4,12},{5,13},{6,14},{7,15},{8,0},{9,1},... | collective-permute-start | bytes 12296 | tf_op jit(solution)/shard_map/ppermute | solution.py:529
  10.9 0.6 pad_add_fusion.1.place_ref.core_ref
  12.0 1.3 %reduce.3 = s32[40]{0:T(128)S(1)} reduce(s32[1,40]{1,0:T(1,128)} %param.27, s32[]{:T(128)} %broadcast.23), dimensions={0}, to_apply=%param.27.reduce_sub_computation.3 | reduce | bytes 324 | tf_op args[13]
  13.5 2.0 %serve_rows.1 = bf16[4,128,256]{2,1,0:T(8,128)(2,1)} custom-call(s32[3]{0:T(128)} %pad_add_fusion.1.place_ref.core_ref, bf16[256,256]{1,0:T(8,128)(2,1)} %node_ref.3, bf16[256,256]{1,0:T(8,128)(2,1)S(1)} %collective-permute-done.refs_1_, bf16[256,256]{1,0:T(8,128)(2,1)S(1)} %collective-permute-done.1.refs_2_, ...), custom_call_target="tpu_custom_call" | custom-call | tf_op jit(solution)/shard_map/serve_rows/pallas_call | solution.py:67
  15.5 4.3 %all-to-all-start = ((bf16[4,128,256]{2,1,0:T(8,128)(2,1)}), bf16[4,128,256]{2,1,0:T(8,128)(2,1)S(1)}, u32[]{:S(2)}, u32[]{:S(2)}) async-start(bf16[4,128,256]{2,1,0:T(8,128)(2,1)} %serve_rows.1), calls=%async_computation | async-start | bytes 524288 | tf_op jit(solution)/shard_map/all_to_all | solution.py:544
  19.9 0.6 compare_convert_fusion.valid_ref
  20.5 7.3 %prepare_edges.1 = (f32[4,256,1280]{2,1,0:T(8,128)}, bf16[4,256,1280]{2,1,0:T(8,128)(2,1)}) custom-call(bf16[5120,256]{1,0:T(8,128)(2,1)} %edge_ref.1, bf16[5120,256]{1,0:T(8,128)(2,1)} %cot_ref.3, s32[4,1,1280]{2,1,0:T(1,128)} %bitcast.16, bf16[256,256]{1,0:T(8,128)(2,1)} %node_ref.3, bf16[768,256]{1,0:T(8,128)(2,1)} %w_in_ref.4), custom_call_target="tpu_custom_call" | custom-call | flops 1342177280 | bytes 10485760 | tf_op jit(solution)/shard_map/prepare_edges/pallas_call | solution.py:102
  27.8 0.6 all-to-all-done
  28.4 17.9 %layer_backward.1 = (bf16[4,256,1280]{2,1,0:T(8,128)(2,1)}, f32[256,256]{1,0:T(8,128)}, bf16[8,160,256]{2,1,0:T(8,128)(2,1)S(1)}, bf16[8,160,256]{2,1,0:T(8,128)(2,1)S(1)}) custom-call(s32[3]{0:T(128)} %pad_add_fusion.1.place_ref.core_ref, f32[4,256,1280]{2,1,0:T(8,128)} %get-tuple-element.27.part_hbm, bf16[4,256,1280]{2,1,0:T(8,128)(2,1)} %get-tuple-element.28.cot_hbm, ...), custom_call_target="tpu_custom_call" | custom-call | tf_op jit(solution)/shard_map/layer_backward/pallas_call | solution.py:317
  46.4 2.1 %collective-permute-done.5.got_ref = bf16[8,160,256]{2,1,0:T(8,128)(2,1)S(1)} collective-permute-done((bf16[8,160,256]{2,1,0:T(8,128)(2,1)S(1)}, bf16[8,160,256]{2,1,0:T(8,128)(2,1)S(1)}, u32[]{:S(2)}, u32[]{:S(2)}) %collective-permute-start.5) | collective-permute-done | bytes 655392 | tf_op jit(solution)/shard_map/ppermute | solution.py:575
  48.5 1.0 %join_cores.1 = bf16[8,192,256]{2,1,0:T(8,128)(2,1)} custom-call(bf16[8,160,256]{2,1,0:T(8,128)(2,1)S(1)} %get-tuple-element.30.keep_ref, bf16[8,160,256]{2,1,0:T(8,128)(2,1)S(1)} %collective-permute-done.5.got_ref), custom_call_target="tpu_custom_call" | custom-call | tf_op jit(solution)/shard_map/join_cores/pallas_call | solution.py:396
  49.5 5.4 %all-to-all-start.1 = ((bf16[8,192,256]{2,1,0:T(8,128)(2,1)}), bf16[8,192,256]{2,1,0:T(8,128)(2,1)S(1)}, u32[]{:S(2)}, u32[]{:S(2)}) async-start(bf16[8,192,256]{2,1,0:T(8,128)(2,1)} %join_cores.1), calls=%async_computation.1 | async-start | bytes 1572864 | tf_op jit(solution)/shard_map/all_to_all | solution.py:577
  55.0 5.3 %edge_result.1 = bf16[5120,256]{1,0:T(8,128)(2,1)} custom-call(bf16[4,256,1280]{2,1,0:T(8,128)(2,1)} %get-tuple-element.32.grad_ref, bf16[5120,256]{1,0:T(8,128)(2,1)} %cot_ref.3, bf16[768,256]{1,0:T(8,128)(2,1)} %w_in_ref.4), custom_call_target="tpu_custom_call" | custom-call | flops 671088640 | bytes 7864320 | tf_op jit(solution)/shard_map/edge_result/pallas_call | solution.py:366
  60.2 15.2 %all-to-all-done.1.sums_ref.back_ref = bf16[8,192,256]{2,1,0:T(8,128)(2,1)S(1)} async-done(((bf16[8,192,256]{2,1,0:T(8,128)(2,1)}), bf16[8,192,256]{2,1,0:T(8,128)(2,1)S(1)}, u32[]{:S(2)}, u32[]{:S(2)}) %all-to-all-start.1) | async-done | bytes 786464 | tf_op jit(solution)/shard_map/all_to_all | solution.py:577
  75.4 0.9 total_piece.1
  76.3 3.6 %all-to-all-start.2 = ((bf16[8,128,256]{2,1,0:T(8,128)(2,1)}), bf16[8,128,256]{2,1,0:T(8,128)(2,1)S(1)}, u32[]{:S(2)}, u32[]{:S(2)}) async-start(bf16[8,128,256]{2,1,0:T(8,128)(2,1)} %total_piece.1), calls=%async_computation.2 | async-start | bytes 1048576 | tf_op jit(solution)/shard_map/all_to_all | solution.py:583
  79.9 2.0 %settle_sums.1 = f32[256,256]{1,0:T(8,128)} custom-call(s32[3]{0:T(128)} %pad_add_fusion.1.place_ref.core_ref, bf16[8,192,256]{2,1,0:T(8,128)(2,1)S(1)} %all-to-all-done.1.sums_ref.back_ref, f32[256,256]{1,0:T(8,128)} %get-tuple-element.34.local_ref), custom_call_target="tpu_custom_call" | custom-call | tf_op jit(solution)/shard_map/settle_sums/pallas_call | solution.py:439
  81.9 12.7 %all-to-all-done.2.mine_ref = bf16[8,128,256]{2,1,0:T(8,128)(2,1)S(1)} async-done(((bf16[8,128,256]{2,1,0:T(8,128)(2,1)}), bf16[8,128,256]{2,1,0:T(8,128)(2,1)S(1)}, u32[]{:S(2)}, u32[]{:S(2)}) %all-to-all-start.2) | async-done | bytes 524320 | tf_op jit(solution)/shard_map/all_to_all | solution.py:583
  94.5 1.9 %collective-permute-done.6.theirs_ref = bf16[8,128,256]{2,1,0:T(8,128)(2,1)S(1)} collective-permute-done((bf16[8,128,256]{2,1,0:T(8,128)(2,1)S(1)}, bf16[8,128,256]{2,1,0:T(8,128)(2,1)S(1)}, u32[]{:S(2)}, u32[]{:S(2)}) %collective-permute-start.6) | collective-permute-done | bytes 524320 | tf_op jit(solution)/shard_map/ppermute | solution.py:588
  96.4 2.6 %assemble_sums.1 = (f32[768,256]{1,0:T(8,128)}, f32[256,256]{1,0:T(8,128)}, f32[512,256]{1,0:T(8,128)}, f32[256,256]{1,0:T(8,128)}, f32[1,256]{1,0:T(1,128)}, /*index=5*/f32[1,256]{1,0:T(1,128)}) custom-call(s32[3]{0:T(128)} %pad_add_fusion.1.place_ref.core_ref, bf16[8,128,256]{2,1,0:T(8,128)(2,1)S(1)} %all-to-all-done.2.mine_ref, ...), custom_call_target="tpu_custom_call" | custom-call | tf_op jit(solution)/shard_map/assemble_sums/pallas_call | solution.py:484
  (13 shorter events, 0.9 us)
Async XLA Ops:
  0.6 6.7 %collective-permute-start.1 = (bf16[256,256]{1,0:T(8,128)(2,1)}, bf16[256,256]{1,0:T(8,128)(2,1)S(1)}, u32[]{:S(2)}, u32[]{:S(2)}) collective-permute-start(bf16[256,256]{1,0:T(8,128)(2,1)} %node_ref.3), channel_id=1, source_target_pairs={{0,2},{1,3},{2,0},{3,1},{4,6},{5,7},{6,4},{7,5},{8,10},{9,11},{10,... | collective-permute-start | bytes 393224 | tf_op jit(solution)/shard_map/ppermute | solution.py:529
  3.7 9.9 %collective-permute-start = (bf16[256,256]{1,0:T(8,128)(2,1)}, bf16[256,256]{1,0:T(8,128)(2,1)S(1)}, u32[]{:S(2)}, u32[]{:S(2)}) collective-permute-start(bf16[256,256]{1,0:T(8,128)(2,1)} %node_ref.3), channel_id=1, source_target_pairs={{0,1},{1,0},{2,3},{3,2},{4,5},{5,4},{6,7},{7,6},{8,9},{9,8},{10,11... | collective-permute-start | bytes 393224 | tf_op jit(solution)/shard_map/ppermute | solution.py:529
  3.7 3.9 %collective-permute-start.3 = (s32[1,16,32]{2,1,0:T(8,128)}, s32[1,16,32]{2,1,0:T(8,128)S(1)}, u32[]{:S(2)}, u32[]{:S(2)}) collective-permute-start(s32[1,16,32]{2,1,0:T(8,128)} %refs_4_.1), channel_id=1, source_target_pairs={{0,4},{1,5},{2,6},{3,7},{4,0},{5,1},{6,2},{7,3},{8,12},{9,13},{10,... | collective-permute-start | bytes 6152 | tf_op jit(solution)/shard_map/ppermute | solution.py:529
  7.4 6.2 %collective-permute-start.2 = (bf16[256,256]{1,0:T(8,128)(2,1)S(1)}, bf16[256,256]{1,0:T(8,128)(2,1)S(1)}, u32[]{:S(2)}, u32[]{:S(2)}) collective-permute-start(bf16[256,256]{1,0:T(8,128)(2,1)S(1)} %collective-permute-done.1.refs_2_), channel_id=1, source_target_pairs={{0,1},{1,0},{2,3},{3,2},{4,5},{5,4},{6,7},{7,6},{8,9},{9,8},{10,11... | collective-permute-start | bytes 393224 | tf_op jit(solution)/shard_map/ppermute | solution.py:529
  8.2 5.3 %collective-permute-start.4 = (s32[2,16,32]{2,1,0:T(8,128)S(1)}, s32[2,16,32]{2,1,0:T(8,128)S(1)}, u32[]{:S(2)}, u32[]{:S(2)}) collective-permute-start(s32[2,16,32]{2,1,0:T(8,128)S(1)} %pad_add_fusion), channel_id=1, source_target_pairs={{0,8},{1,9},{2,10},{3,11},{4,12},{5,13},{6,14},{7,15},{8,0},{9,1},... | collective-permute-start | bytes 12296 | tf_op jit(solution)/shard_map/ppermute | solution.py:529
  15.5 12.9 %all-to-all-start = ((bf16[4,128,256]{2,1,0:T(8,128)(2,1)}), bf16[4,128,256]{2,1,0:T(8,128)(2,1)S(1)}, u32[]{:S(2)}, u32[]{:S(2)}) async-start(bf16[4,128,256]{2,1,0:T(8,128)(2,1)} %serve_rows.1), calls=%async_computation | async-start | bytes 524288 | tf_op jit(solution)/shard_map/all_to_all | solution.py:544
  46.3 2.2 %collective-permute-start.5 = (bf16[8,160,256]{2,1,0:T(8,128)(2,1)S(1)}, bf16[8,160,256]{2,1,0:T(8,128)(2,1)S(1)}, u32[]{:S(2)}, u32[]{:S(2)}) collective-permute-start(bf16[8,160,256]{2,1,0:T(8,128)(2,1)S(1)} %get-tuple-element.31), channel_id=1, source_target_pairs={{0,1},{1,0},{2,3},{3,2},{4,5},{5,4},{6,7},{7,6},{8,9},{9,8},{10,11... | collective-permute-start | bytes 1966088 | tf_op jit(solution)/shard_map/ppermute | solution.py:575
  49.5 25.9 %all-to-all-start.1 = ((bf16[8,192,256]{2,1,0:T(8,128)(2,1)}), bf16[8,192,256]{2,1,0:T(8,128)(2,1)S(1)}, u32[]{:S(2)}, u32[]{:S(2)}) async-start(bf16[8,192,256]{2,1,0:T(8,128)(2,1)} %join_cores.1), calls=%async_computation.1 | async-start | bytes 1572864 | tf_op jit(solution)/shard_map/all_to_all | solution.py:577
  76.3 18.3 %all-to-all-start.2 = ((bf16[8,128,256]{2,1,0:T(8,128)(2,1)}), bf16[8,128,256]{2,1,0:T(8,128)(2,1)S(1)}, u32[]{:S(2)}, u32[]{:S(2)}) async-start(bf16[8,128,256]{2,1,0:T(8,128)(2,1)} %total_piece.1), calls=%async_computation.2 | async-start | bytes 1048576 | tf_op jit(solution)/shard_map/all_to_all | solution.py:583
  94.5 1.9 %collective-permute-start.6 = (bf16[8,128,256]{2,1,0:T(8,128)(2,1)S(1)}, bf16[8,128,256]{2,1,0:T(8,128)(2,1)S(1)}, u32[]{:S(2)}, u32[]{:S(2)}) collective-permute-start(bf16[8,128,256]{2,1,0:T(8,128)(2,1)S(1)} %all-to-all-done.2.mine_ref), channel_id=1, source_target_pairs={{0,1},{1,0},{2,3},{3,2},{4,5},{5,4},{6,7},{7,6},{8,9},{9,8},{10,11... | collective-permute-start | bytes 1572872 | tf_op jit(solution)/shard_map/ppermute | solution.py:588

commit v5 on v4

--- a/solution.py
+++ b/solution.py
@@ -10,7 +10,7 @@
 epsilon = 1e-05
 CHUNK = 1280
 GROUP = 4
-TAIL = 16
+TAIL = 8
 VMEM_LIMIT = 60 * 2**20
 BF = jnp.bfloat16
 F32 = jnp.float32
@@ -159,14 +159,13 @@
     weight_pack,
     w_out_t,
     gain_column,
-    pack,
     sems,
     out_sems,
 ):
     chunks, latent, width = part.shape
     nodes = node_ref.shape[0]
     slots = fetched_ref.shape[0]
-    bands = pack.shape[1] * 2
+    bands = keep_ref.shape[0] * 2
     cap = slots // bands
 
     def part_copy(c):
@@ -186,15 +185,14 @@
     gain_column[...] = jnp.broadcast_to(gain_edge_ref[...], (128, latent)).T
     summed_acc[...] = jnp.zeros_like(summed_acc)
     send_part[...] = dot(w_in_ref[latent : 2 * latent, :], fetched_ref[...], 0, 1).astype(BF)
-    for c in range(chunks):
-        part_copy(c).wait()
     w_in_acc[...] = jnp.zeros_like(w_in_acc)
     w_out_acc[...] = jnp.zeros_like(w_out_acc)
     ends_acc[...] = jnp.zeros_like(ends_acc)
     gain_acc[...] = jnp.zeros_like(gain_acc)
 
-    @pl.loop(0, chunks, unroll=True)
-    def _(c):
+    for c in range(chunks):
+        for arrived in range(1) if c == 0 else range(1, chunks) if c == 1 else ():
+            part_copy(arrived).wait()
         slot_hot = onehot_rows(slots, slot_ref[c])
         recv_hot = onehot_rows(nodes, recv_ref[c])
         hot[c, :nodes, :] = recv_hot
@@ -281,24 +279,24 @@
     gain_edge_grad = jnp.sum(gain_acc[...].T, axis=0, keepdims=True)
     slot_grads = dot(slot_sum, w_in_ref[latent : 2 * latent, :], 1, 1).astype(BF)
     core = core_ref[0]
-    for d in range(bands):
-        pack[d % 2, d // 2, :cap, :] = slot_grads[d * cap : (d + 1) * cap, :]
-        body = weight_pack[d * piece_rows : (d + 1) * piece_rows, :]
-        pack[d % 2, d // 2, cap : cap + piece_rows, :] = body.astype(BF)
-        row = lax.broadcasted_iota(jnp.int32, (TAIL, latent), 0)
-        listed = jnp.concatenate([wanted_ref[d : d + 1, :].astype(F32)] * (latent // cap), axis=1)
-        column = lax.broadcasted_iota(jnp.int32, (1, latent), 1)
-        listed = jnp.where(column // cap == core, listed, 0.0)
-        extra = jnp.where(row == 1, listed, 0.0)
-        if d < 2:
-            extra = jnp.where(row == 0, gain_edge_grad if d == 0 else gain_node_grad, extra)
-        pack[d % 2, d // 2, cap + piece_rows :, :] = extra.astype(BF)
+    row = lax.broadcasted_iota(jnp.int32, (TAIL, latent), 0)
+    column = lax.broadcasted_iota(jnp.int32, (1, latent), 1)
     for own in range(2):
 
         @pl.when(core == own)
         def _():
-            keep_ref[...] = pack[own]
-            send_ref[...] = pack[1 - own]
+            for d in range(bands):
+                out = (keep_ref if d % 2 == own else send_ref).at[d // 2]
+                out[:cap, :] = slot_grads[d * cap : (d + 1) * cap, :]
+                body = weight_pack[d * piece_rows : (d + 1) * piece_rows, :]
+                out[cap : cap + piece_rows, :] = body.astype(BF)
+                listed = jnp.concatenate(
+                    [wanted_ref[d : d + 1, :].astype(F32)] * (latent // cap), axis=1
+                )
+                extra = jnp.where(row == 1, jnp.where(column // cap == own, listed, 0.0), 0.0)
+                if d < 2:
+                    extra = jnp.where(row == 0, gain_edge_grad if d == 0 else gain_node_grad, extra)
+                out[cap + piece_rows :, :] = extra.astype(BF)
 
     for c in range(chunks):
         pltpu.make_async_copy(grad_pre.at[c], grad_pre_hbm.at[c], out_sems.at[c]).wait()
@@ -344,7 +342,6 @@
             pltpu.VMEM((piece_rows * bands, latent), F32),
             pltpu.VMEM((latent, hidden), BF),
             pltpu.VMEM((latent, 128), F32),
-            pltpu.VMEM((2, bands // 2, cap + piece_rows + TAIL, latent), BF),
             pltpu.SemaphoreType.DMA((3, chunks)),
             pltpu.SemaphoreType.DMA((chunks,)),
         ],
@@ -528,13 +525,13 @@
     def swap(array, step):
         return lax.ppermute(array, "band", [(i, i ^ step) for i in range(bands)])
 
-    across = swap(node_lat, 2)
     lists = [fetch_idx]
     step = GROUP
     while step < bands:
         held = lists[0] if len(lists) == 1 else jnp.concatenate(lists, axis=0)
         lists.append(swap(held, step))
         step *= 2
+    across = swap(node_lat, 2)
     members = (node_lat, swap(node_lat, 1), across, swap(across, 1))
     rows = serve(place, lists, members)
     valid = jnp.arange(128, dtype=jnp.int32)[None, :] < block_fill[0][:, None]

time: 99.7 us -> 97.3 us (0.976)
  waiting for transfers between devices: 34.7 us -> 33.2 us
where the time goes in v5:
time: 97.3 us; the launch traced here: 96.6 us
  Pallas kernels  38 us (39%)
  waiting for transfers between devices  33.2 us (34%)
  starting transfers between devices  20.7 us (21%)
  other arithmetic  3.24 us (3%)
    pallas_call x1, Pallas kernels, layer(): pl.pallas_call(functools.partial(layer_kernel, piece_rows), out_shape=[ja...  17 us
    all_to_all x1, waiting for transfers between devices, per_device(): lax.all_to_all(joined, 'band', split_axis=0, concat_axis=0, tiled=True, a...  14.5 us
    all_to_all x1, waiting for transfers between devices, per_device(): lax.all_to_all(pieces, 'band', split_axis=0, concat_axis=0, tiled=True, a...  12 us
    pallas_call x1, Pallas kernels, prepare(): pl.pallas_call(prepare_kernel, grid=(chunks,), out_shape=[jax.ShapeDtypeS...  7.34 us
    ppermute x5, starting transfers between devices, swap(): return lax.ppermute(array, 'band', [(i, i ^ step) for i in range(bands)])  7.27 us
    all_to_all x1, starting transfers between devices, per_device(): lax.all_to_all(joined, 'band', split_axis=0, concat_axis=0, tiled=True, a...  5.47 us
    pallas_call x1, Pallas kernels, edge_result(): pl.pallas_call(edge_kernel, grid=(chunks,), out_shape=jax.ShapeDtypeStruc...  5.27 us
    all_to_all x1, starting transfers between devices, per_device(): lax.all_to_all(rows, 'band', split_axis=0, concat_axis=0, tiled=True, axi...  4.34 us
  transfers between devices with their start and end apart: 10, of which 7 were waited for; matrix products, arithmetic and copies ran while one was open for 4% of the time, Pallas kernels for 15%

profile of v5, /device:TPU:0, one launch (start us, length us, event | category | flops | bytes accessed | tf_op | source)
XLA Modules:
  0.0 96.6 jit_solution(6604114424506261847)
XLA Ops:
  0.6 3.0 %collective-permute-start.1 = (bf16[256,256]{1,0:T(8,128)(2,1)}, bf16[256,256]{1,0:T(8,128)(2,1)S(1)}, u32[]{:S(2)}, u32[]{:S(2)}) collective-permute-start(bf16[256,256]{1,0:T(8,128)(2,1)} %node_ref.3), channel_id=1, source_target_pairs={{0,2},{1,3},{2,0},{3,1},{4,6},{5,7},{6,4},{7,5},{8,10},{9,11},{10,... | collective-permute-start | bytes 393224 | tf_op jit(solution)/shard_map/ppermute | solution.py:526
  3.7 1.6 %collective-permute-start.3 = (s32[1,16,32]{2,1,0:T(8,128)}, s32[1,16,32]{2,1,0:T(8,128)S(1)}, u32[]{:S(2)}, u32[]{:S(2)}) collective-permute-start(s32[1,16,32]{2,1,0:T(8,128)} %refs_4_.1), channel_id=1, source_target_pairs={{0,4},{1,5},{2,6},{3,7},{4,0},{5,1},{6,2},{7,3},{8,12},{9,13},{10,... | collective-permute-start | bytes 6152 | tf_op jit(solution)/shard_map/ppermute | solution.py:526
  5.2 2.1 %collective-permute-done.1.refs_2_ = bf16[256,256]{1,0:T(8,128)(2,1)S(1)} collective-permute-done((bf16[256,256]{1,0:T(8,128)(2,1)}, bf16[256,256]{1,0:T(8,128)(2,1)S(1)}, u32[]{:S(2)}, u32[]{:S(2)}) %collective-permute-start.1) | collective-permute-done | bytes 131104 | tf_op jit(solution)/shard_map/ppermute | solution.py:526
  7.5 0.7 pad_add_fusion
  8.2 2.7 %collective-permute-start.4 = (s32[2,16,32]{2,1,0:T(8,128)S(1)}, s32[2,16,32]{2,1,0:T(8,128)S(1)}, u32[]{:S(2)}, u32[]{:S(2)}) collective-permute-start(s32[2,16,32]{2,1,0:T(8,128)S(1)} %pad_add_fusion), channel_id=1, source_target_pairs={{0,8},{1,9},{2,10},{3,11},{4,12},{5,13},{6,14},{7,15},{8,0},{9,1},... | collective-permute-start | bytes 12296 | tf_op jit(solution)/shard_map/ppermute | solution.py:526
  10.9 0.6 pad_add_fusion.1.place_ref.core_ref
  12.0 1.3 %reduce.3 = s32[40]{0:T(128)S(1)} reduce(s32[1,40]{1,0:T(1,128)} %param.27, s32[]{:T(128)} %broadcast.23), dimensions={0}, to_apply=%param.27.reduce_sub_computation.3 | reduce | bytes 324 | tf_op args[13]
  13.5 2.0 %serve_rows.1 = bf16[4,128,256]{2,1,0:T(8,128)(2,1)} custom-call(s32[3]{0:T(128)} %pad_add_fusion.1.place_ref.core_ref, bf16[256,256]{1,0:T(8,128)(2,1)} %node_ref.3, bf16[256,256]{1,0:T(8,128)(2,1)S(1)} %collective-permute-done.refs_1_, bf16[256,256]{1,0:T(8,128)(2,1)S(1)} %collective-permute-done.1.refs_2_, ...), custom_call_target="tpu_custom_call" | custom-call | tf_op jit(solution)/shard_map/serve_rows/pallas_call | solution.py:67
  15.5 4.3 %all-to-all-start = ((bf16[4,128,256]{2,1,0:T(8,128)(2,1)}), bf16[4,128,256]{2,1,0:T(8,128)(2,1)S(1)}, u32[]{:S(2)}, u32[]{:S(2)}) async-start(bf16[4,128,256]{2,1,0:T(8,128)(2,1)} %serve_rows.1), calls=%async_computation | async-start | bytes 524288 | tf_op jit(solution)/shard_map/all_to_all | solution.py:541
  19.9 0.6 compare_convert_fusion.valid_ref
  20.5 7.3 %prepare_edges.1 = (f32[4,256,1280]{2,1,0:T(8,128)}, bf16[4,256,1280]{2,1,0:T(8,128)(2,1)}) custom-call(bf16[5120,256]{1,0:T(8,128)(2,1)} %edge_ref.1, bf16[5120,256]{1,0:T(8,128)(2,1)} %cot_ref.3, s32[4,1,1280]{2,1,0:T(1,128)} %bitcast.16, bf16[256,256]{1,0:T(8,128)(2,1)} %node_ref.3, bf16[768,256]{1,0:T(8,128)(2,1)} %w_in_ref.4), custom_call_target="tpu_custom_call" | custom-call | flops 1342177280 | bytes 10485760 | tf_op jit(solution)/shard_map/prepare_edges/pallas_call | solution.py:102
  27.8 0.6 all-to-all-done
  28.4 17.0 %layer_backward.1 = (bf16[4,256,1280]{2,1,0:T(8,128)(2,1)}, f32[256,256]{1,0:T(8,128)}, bf16[8,152,256]{2,1,0:T(8,128)(2,1)S(1)}, bf16[8,152,256]{2,1,0:T(8,128)(2,1)S(1)}) custom-call(s32[3]{0:T(128)} %pad_add_fusion.1.place_ref.core_ref, f32[4,256,1280]{2,1,0:T(8,128)} %get-tuple-element.27.part_hbm, bf16[4,256,1280]{2,1,0:T(8,128)(2,1)} %get-tuple-element.28.cot_hbm, ...), custom_call_target="tpu_custom_call" | custom-call | tf_op jit(solution)/shard_map/layer_backward/pallas_call | solution.py:315
  45.5 2.0 %collective-permute-done.5.got_ref = bf16[8,152,256]{2,1,0:T(8,128)(2,1)S(1)} collective-permute-done((bf16[8,152,256]{2,1,0:T(8,128)(2,1)S(1)}, bf16[8,152,256]{2,1,0:T(8,128)(2,1)S(1)}, u32[]{:S(2)}, u32[]{:S(2)}) %collective-permute-start.5) | collective-permute-done | bytes 622624 | tf_op jit(solution)/shard_map/ppermute | solution.py:572
  47.6 1.0 %join_cores.1 = bf16[8,184,256]{2,1,0:T(8,128)(2,1)} custom-call(bf16[8,152,256]{2,1,0:T(8,128)(2,1)S(1)} %get-tuple-element.30.keep_ref, bf16[8,152,256]{2,1,0:T(8,128)(2,1)S(1)} %collective-permute-done.5.got_ref), custom_call_target="tpu_custom_call" | custom-call | tf_op jit(solution)/shard_map/join_cores/pallas_call | solution.py:393
  48.6 5.5 %all-to-all-start.1 = ((bf16[8,184,256]{2,1,0:T(8,128)(2,1)}), bf16[8,184,256]{2,1,0:T(8,128)(2,1)S(1)}, u32[]{:S(2)}, u32[]{:S(2)}) async-start(bf16[8,184,256]{2,1,0:T(8,128)(2,1)} %join_cores.1), calls=%async_computation.1 | async-start | bytes 1507328 | tf_op jit(solution)/shard_map/all_to_all | solution.py:574
  54.0 5.3 %edge_result.1 = bf16[5120,256]{1,0:T(8,128)(2,1)} custom-call(bf16[4,256,1280]{2,1,0:T(8,128)(2,1)} %get-tuple-element.32.grad_ref, bf16[5120,256]{1,0:T(8,128)(2,1)} %cot_ref.3, bf16[768,256]{1,0:T(8,128)(2,1)} %w_in_ref.4), custom_call_target="tpu_custom_call" | custom-call | flops 671088640 | bytes 7864320 | tf_op jit(solution)/shard_map/edge_result/pallas_call | solution.py:363
  59.3 14.5 %all-to-all-done.1.sums_ref.back_ref = bf16[8,184,256]{2,1,0:T(8,128)(2,1)S(1)} async-done(((bf16[8,184,256]{2,1,0:T(8,128)(2,1)}), bf16[8,184,256]{2,1,0:T(8,128)(2,1)S(1)}, u32[]{:S(2)}, u32[]{:S(2)}) %all-to-all-start.1) | async-done | bytes 753696 | tf_op jit(solution)/shard_map/all_to_all | solution.py:574
  73.8 0.8 total_piece.1
  74.6 3.6 %all-to-all-start.2 = ((bf16[8,120,256]{2,1,0:T(8,128)(2,1)}), bf16[8,120,256]{2,1,0:T(8,128)(2,1)S(1)}, u32[]{:S(2)}, u32[]{:S(2)}) async-start(bf16[8,120,256]{2,1,0:T(8,128)(2,1)} %total_piece.1), calls=%async_computation.2 | async-start | bytes 983040 | tf_op jit(solution)/shard_map/all_to_all | solution.py:580
  78.2 2.0 %settle_sums.1 = f32[256,256]{1,0:T(8,128)} custom-call(s32[3]{0:T(128)} %pad_add_fusion.1.place_ref.core_ref, bf16[8,184,256]{2,1,0:T(8,128)(2,1)S(1)} %all-to-all-done.1.sums_ref.back_ref, f32[256,256]{1,0:T(8,128)} %get-tuple-element.34.local_ref), custom_call_target="tpu_custom_call" | custom-call | tf_op jit(solution)/shard_map/settle_sums/pallas_call | solution.py:436
  80.2 12.0 %all-to-all-done.2.mine_ref = bf16[8,120,256]{2,1,0:T(8,128)(2,1)S(1)} async-done(((bf16[8,120,256]{2,1,0:T(8,128)(2,1)}), bf16[8,120,256]{2,1,0:T(8,128)(2,1)S(1)}, u32[]{:S(2)}, u32[]{:S(2)}) %all-to-all-start.2) | async-done | bytes 491552 | tf_op jit(solution)/shard_map/all_to_all | solution.py:580
  92.2 1.9 %collective-permute-done.6.theirs_ref = bf16[8,120,256]{2,1,0:T(8,128)(2,1)S(1)} collective-permute-done((bf16[8,120,256]{2,1,0:T(8,128)(2,1)S(1)}, bf16[8,120,256]{2,1,0:T(8,128)(2,1)S(1)}, u32[]{:S(2)}, u32[]{:S(2)}) %collective-permute-start.6) | collective-permute-done | bytes 491552 | tf_op jit(solution)/shard_map/ppermute | solution.py:585
  94.1 2.6 %assemble_sums.1 = (f32[768,256]{1,0:T(8,128)}, f32[256,256]{1,0:T(8,128)}, f32[512,256]{1,0:T(8,128)}, f32[256,256]{1,0:T(8,128)}, f32[1,256]{1,0:T(1,128)}, /*index=5*/f32[1,256]{1,0:T(1,128)}) custom-call(s32[3]{0:T(128)} %pad_add_fusion.1.place_ref.core_ref, bf16[8,120,256]{2,1,0:T(8,128)(2,1)S(1)} %all-to-all-done.2.mine_ref, ...), custom_call_target="tpu_custom_call" | custom-call | tf_op jit(solution)/shard_map/assemble_sums/pallas_call | solution.py:481
  (13 shorter events, 0.9 us)
Async XLA Ops:
  0.6 6.7 %collective-permute-start.1 = (bf16[256,256]{1,0:T(8,128)(2,1)}, bf16[256,256]{1,0:T(8,128)(2,1)S(1)}, u32[]{:S(2)}, u32[]{:S(2)}) collective-permute-start(bf16[256,256]{1,0:T(8,128)(2,1)} %node_ref.3), channel_id=1, source_target_pairs={{0,2},{1,3},{2,0},{3,1},{4,6},{5,7},{6,4},{7,5},{8,10},{9,11},{10,... | collective-permute-start | bytes 393224 | tf_op jit(solution)/shard_map/ppermute | solution.py:526
  3.7 9.9 %collective-permute-start = (bf16[256,256]{1,0:T(8,128)(2,1)}, bf16[256,256]{1,0:T(8,128)(2,1)S(1)}, u32[]{:S(2)}, u32[]{:S(2)}) collective-permute-start(bf16[256,256]{1,0:T(8,128)(2,1)} %node_ref.3), channel_id=1, source_target_pairs={{0,1},{1,0},{2,3},{3,2},{4,5},{5,4},{6,7},{7,6},{8,9},{9,8},{10,11... | collective-permute-start | bytes 393224 | tf_op jit(solution)/shard_map/ppermute | solution.py:526
  3.7 3.9 %collective-permute-start.3 = (s32[1,16,32]{2,1,0:T(8,128)}, s32[1,16,32]{2,1,0:T(8,128)S(1)}, u32[]{:S(2)}, u32[]{:S(2)}) collective-permute-start(s32[1,16,32]{2,1,0:T(8,128)} %refs_4_.1), channel_id=1, source_target_pairs={{0,4},{1,5},{2,6},{3,7},{4,0},{5,1},{6,2},{7,3},{8,12},{9,13},{10,... | collective-permute-start | bytes 6152 | tf_op jit(solution)/shard_map/ppermute | solution.py:526
  7.4 6.2 %collective-permute-start.2 = (bf16[256,256]{1,0:T(8,128)(2,1)S(1)}, bf16[256,256]{1,0:T(8,128)(2,1)S(1)}, u32[]{:S(2)}, u32[]{:S(2)}) collective-permute-start(bf16[256,256]{1,0:T(8,128)(2,1)S(1)} %collective-permute-done.1.refs_2_), channel_id=1, source_target_pairs={{0,1},{1,0},{2,3},{3,2},{4,5},{5,4},{6,7},{7,6},{8,9},{9,8},{10,11... | collective-permute-start | bytes 393224 | tf_op jit(solution)/shard_map/ppermute | solution.py:526
  8.2 5.3 %collective-permute-start.4 = (s32[2,16,32]{2,1,0:T(8,128)S(1)}, s32[2,16,32]{2,1,0:T(8,128)S(1)}, u32[]{:S(2)}, u32[]{:S(2)}) collective-permute-start(s32[2,16,32]{2,1,0:T(8,128)S(1)} %pad_add_fusion), channel_id=1, source_target_pairs={{0,8},{1,9},{2,10},{3,11},{4,12},{5,13},{6,14},{7,15},{8,0},{9,1},... | collective-permute-start | bytes 12296 | tf_op jit(solution)/shard_map/ppermute | solution.py:526
  15.5 12.9 %all-to-all-start = ((bf16[4,128,256]{2,1,0:T(8,128)(2,1)}), bf16[4,128,256]{2,1,0:T(8,128)(2,1)S(1)}, u32[]{:S(2)}, u32[]{:S(2)}) async-start(bf16[4,128,256]{2,1,0:T(8,128)(2,1)} %serve_rows.1), calls=%async_computation | async-start | bytes 524288 | tf_op jit(solution)/shard_map/all_to_all | solution.py:541
  45.4 2.1 %collective-permute-start.5 = (bf16[8,152,256]{2,1,0:T(8,128)(2,1)S(1)}, bf16[8,152,256]{2,1,0:T(8,128)(2,1)S(1)}, u32[]{:S(2)}, u32[]{:S(2)}) collective-permute-start(bf16[8,152,256]{2,1,0:T(8,128)(2,1)S(1)} %get-tuple-element.31), channel_id=1, source_target_pairs={{0,1},{1,0},{2,3},{3,2},{4,5},{5,4},{6,7},{7,6},{8,9},{9,8},{10,11... | collective-permute-start | bytes 1867784 | tf_op jit(solution)/shard_map/ppermute | solution.py:572
  48.6 25.2 %all-to-all-start.1 = ((bf16[8,184,256]{2,1,0:T(8,128)(2,1)}), bf16[8,184,256]{2,1,0:T(8,128)(2,1)S(1)}, u32[]{:S(2)}, u32[]{:S(2)}) async-start(bf16[8,184,256]{2,1,0:T(8,128)(2,1)} %join_cores.1), calls=%async_computation.1 | async-start | bytes 1507328 | tf_op jit(solution)/shard_map/all_to_all | solution.py:574
  74.6 17.6 %all-to-all-start.2 = ((bf16[8,120,256]{2,1,0:T(8,128)(2,1)}), bf16[8,120,256]{2,1,0:T(8,128)(2,1)S(1)}, u32[]{:S(2)}, u32[]{:S(2)}) async-start(bf16[8,120,256]{2,1,0:T(8,128)(2,1)} %total_piece.1), calls=%async_computation.2 | async-start | bytes 983040 | tf_op jit(solution)/shard_map/all_to_all | solution.py:580
  92.2 1.9 %collective-permute-start.6 = (bf16[8,120,256]{2,1,0:T(8,128)(2,1)S(1)}, bf16[8,120,256]{2,1,0:T(8,128)(2,1)S(1)}, u32[]{:S(2)}, u32[]{:S(2)}) collective-permute-start(bf16[8,120,256]{2,1,0:T(8,128)(2,1)S(1)} %all-to-all-done.2.mine_ref), channel_id=1, source_target_pairs={{0,1},{1,0},{2,3},{3,2},{4,5},{5,4},{6,7},{7,6},{8,9},{9,8},{10,11... | collective-permute-start | bytes 1474568 | tf_op jit(solution)/shard_map/ppermute | solution.py:585

commit v6 on v5

--- a/solution.py
+++ b/solution.py
@@ -11,7 +11,9 @@
 CHUNK = 1280
 GROUP = 4
 TAIL = 8
-VMEM_LIMIT = 60 * 2**20
+VMEM_LIMIT = 20 * 2**20
+LAYER_VMEM_LIMIT = 48 * 2**20
+STORED_SLOTS = 1024
 BF = jnp.bfloat16
 F32 = jnp.float32
 
@@ -35,6 +37,10 @@
 
 def in_vmem(array):
     return pltpu.with_memory_space_constraint(array, pltpu.VMEM)
+
+
+def in_hbm(array):
+    return pltpu.with_memory_space_constraint(array, pltpu.HBM)
 
 
 def vmem():
@@ -71,7 +77,7 @@
         out_specs=vmem(),
         compiler_params=pltpu.CompilerParams(vmem_limit_bytes=VMEM_LIMIT),
         name="serve_rows",
-    )(place, members[0], *map(in_vmem, members[1:]), lists[0], *map(in_vmem, lists[1:]))
+    )(place, in_hbm(members[0]), *map(in_vmem, members[1:]), in_hbm(lists[0]), *map(in_vmem, lists[1:]))
 
 
 def prepare_kernel(
@@ -103,8 +109,8 @@
         prepare_kernel,
         grid=(chunks,),
         out_shape=[
-            jax.ShapeDtypeStruct((chunks, hidden, CHUNK), F32),
-            jax.ShapeDtypeStruct((chunks, latent, CHUNK), BF),
+            pltpu.HBM((chunks, hidden, CHUNK), F32),
+            pltpu.HBM((chunks, latent, CHUNK), BF),
         ],
         in_specs=[rows, rows, along(1), whole(node_lat.shape), whole(w_edge_in.shape)],
         out_specs=[along(hidden), along(latent)],
@@ -114,7 +120,7 @@
             flops=4 * edges * latent * hidden, bytes_accessed=8 * edges * latent, transcendentals=0
         ),
         name="prepare_edges",
-    )(edge_lat, edge_cot, recv_rows, node_lat, w_edge_in)
+    )(in_hbm(edge_lat), in_hbm(edge_cot), in_hbm(recv_rows), in_hbm(node_lat), in_hbm(w_edge_in))
 
 
 def layer_kernel(
@@ -165,6 +171,7 @@
     chunks, latent, width = part.shape
     nodes = node_ref.shape[0]
     slots = fetched_ref.shape[0]
+    stored = slots <= STORED_SLOTS
     bands = keep_ref.shape[0] * 2
     cap = slots // bands
 
@@ -196,7 +203,8 @@
         slot_hot = onehot_rows(slots, slot_ref[c])
         recv_hot = onehot_rows(nodes, recv_ref[c])
         hot[c, :nodes, :] = recv_hot
-        hot[c, nodes:, :] = slot_hot
+        if stored:
+            hot[c, nodes:, :] = slot_hot
         pre = part[c] + dot(send_part[...], slot_hot, 1, 0)
         hid, slo = swish_and_slope(pre)
         hid = hid.astype(BF)
@@ -262,7 +270,11 @@
         grad_in = (grad_hidden * slope[c].astype(F32)).astype(BF)
         grad_pre[c] = grad_in
         w_in_acc[...] += dot(grad_in, edge[c], 1, 0)
-        ends_acc[...] += dot(hot[c], grad_in, 1, 1)
+        if stored:
+            ends_acc[...] += dot(hot[c], grad_in, 1, 1)
+        else:
+            ends_acc[:nodes, :] += dot(hot[c], grad_in, 1, 1)
+            ends_acc[nodes:, :] += dot(onehot_rows(slots, slot_ref[c]), grad_in, 1, 1)
 
     for c in range(chunks):
         pltpu.make_async_copy(grad_pre.at[c], grad_pre_hbm.at[c], out_sems.at[c]).start()
@@ -315,7 +327,7 @@
     return pl.pallas_call(
         functools.partial(layer_kernel, piece_rows),
         out_shape=[
-            jax.ShapeDtypeStruct((chunks, hidden, width), BF),
+            pltpu.HBM((chunks, hidden, width), BF),
             jax.ShapeDtypeStruct((nodes, latent), F32),
             pltpu.VMEM((bands // 2, cap + piece_rows + TAIL, latent), BF),
             pltpu.VMEM((bands // 2, cap + piece_rows + TAIL, latent), BF),
@@ -326,7 +338,7 @@
             pltpu.VMEM((chunks, hidden, width), F32),
             pltpu.VMEM((chunks, latent, width), BF),
             pltpu.VMEM((chunks, width, latent), BF),
-            pltpu.VMEM((chunks, nodes + slots, width), BF),
+            pltpu.VMEM((chunks, nodes + (slots if slots <= STORED_SLOTS else 0), width), BF),
             pltpu.VMEM((chunks, hidden, width), BF),
             pltpu.VMEM((chunks, hidden, width), BF),
             pltpu.VMEM((chunks, latent, width), BF),
@@ -345,9 +357,9 @@
             pltpu.SemaphoreType.DMA((3, chunks)),
             pltpu.SemaphoreType.DMA((chunks,)),
         ],
-        compiler_params=pltpu.CompilerParams(vmem_limit_bytes=VMEM_LIMIT),
+        compiler_params=pltpu.CompilerParams(vmem_limit_bytes=LAYER_VMEM_LIMIT),
         name="layer_backward",
-    )(core, part, cot_t, edges, recv_rows, slot_rows, in_vmem(fetched), wanted, valid_rows, node_lat, node_cot, *weights)
+    )(core, in_hbm(part), in_hbm(cot_t), in_hbm(edges), recv_rows, slot_rows, in_vmem(fetched), wanted, valid_rows, node_lat, node_cot, *weights)
 
 
 def edge_kernel(grad_ref, cot_ref, w_in_ref, out_ref):
@@ -377,7 +389,7 @@
             transcendentals=0,
         ),
         name="edge_result",
-    )(grad_pre, edge_cot, w_edge_in)
+    )(in_hbm(grad_pre), in_hbm(edge_cot), w_edge_in)
 
 
 def join_kernel(cap, keep_ref, got_ref, out_ref):

time: 97.3 us -> 96.2 us (0.989)
  Pallas kernels: 38 us -> 36.5 us
  other arithmetic: 3.24 us -> 2.12 us
    pallas_call x2, Pallas kernels: 24.3 us -> 23.1 us  [the longest x1 15.7 us: layer(): pl.pallas_call(functools.partial(layer_kernel, piece_rows), out_shape=[pl...]
  transfers between devices with their start and end apart: 10 -> 10, of which waited for: 7 -> 7; matrix products, arithmetic and copies ran while one was open for 4% -> 3% of each run, Pallas kernels for 15% -> 15%
where the time goes in v6:
time: 96.2 us; the launch traced here: 95.5 us
  Pallas kernels  36.5 us (38%)
  waiting for transfers between devices  33.5 us (35%)
  starting transfers between devices  21 us (22%)
  other arithmetic  2.12 us (2%)
  local copies, waits for them, and re-layouts  1.47 us (2%)
    pallas_call x1, Pallas kernels, layer(): pl.pallas_call(functools.partial(layer_kernel, piece_rows), out_shape=[pl...  15.7 us
    all_to_all x1, waiting for transfers between devices, per_device(): lax.all_to_all(joined, 'band', split_axis=0, concat_axis=0, tiled=True, a...  14.6 us
    all_to_all x1, waiting for transfers between devices, per_device(): lax.all_to_all(pieces, 'band', split_axis=0, concat_axis=0, tiled=True, a...  12 us
    pallas_call x1, Pallas kernels, prepare(): pl.pallas_call(prepare_kernel, grid=(chunks,), out_shape=[pltpu.HBM((chun...  7.46 us
    ppermute x5, starting transfers between devices, swap(): return lax.ppermute(array, 'band', [(i, i ^ step) for i in range(bands)])  7.27 us
    all_to_all x1, starting transfers between devices, per_device(): lax.all_to_all(joined, 'band', split_axis=0, concat_axis=0, tiled=True, a...  5.3 us
    pallas_call x1, Pallas kernels, edge_result(): pl.pallas_call(edge_kernel, grid=(chunks,), out_shape=jax.ShapeDtypeStruc...  5.15 us
    all_to_all x1, starting transfers between devices, per_device(): lax.all_to_all(rows, 'band', split_axis=0, concat_axis=0, tiled=True, axi...  4.85 us
  transfers between devices with their start and end apart: 10, of which 7 were waited for; matrix products, arithmetic and copies ran while one was open for 3% of the time, Pallas kernels for 15%

profile of v6, /device:TPU:0, one launch (start us, length us, event | category | flops | bytes accessed | tf_op | source)
XLA Modules:
  0.0 95.5 jit_solution(5014057022763068913)
XLA Ops:
  0.6 3.0 %collective-permute-start.1 = (bf16[256,256]{1,0:T(8,128)(2,1)}, bf16[256,256]{1,0:T(8,128)(2,1)S(1)}, u32[]{:S(2)}, u32[]{:S(2)}) collective-permute-start(bf16[256,256]{1,0:T(8,128)(2,1)} %node_ref.3), channel_id=1, source_target_pairs={{0,2},{1,3},{2,0},{3,1},{4,6},{5,7},{6,4},{7,5},{8,10},{9,11},{10,... | collective-permute-start | bytes 393224 | tf_op jit(solution)/shard_map/ppermute | solution.py:538
  3.7 1.6 %collective-permute-start.3 = (s32[1,16,32]{2,1,0:T(8,128)}, s32[1,16,32]{2,1,0:T(8,128)S(1)}, u32[]{:S(2)}, u32[]{:S(2)}) collective-permute-start(s32[1,16,32]{2,1,0:T(8,128)} %refs_4_.1), channel_id=1, source_target_pairs={{0,4},{1,5},{2,6},{3,7},{4,0},{5,1},{6,2},{7,3},{8,12},{9,13},{10,... | collective-permute-start | bytes 6152 | tf_op jit(solution)/shard_map/ppermute | solution.py:538
  5.2 2.1 %collective-permute-done.1.refs_2_ = bf16[256,256]{1,0:T(8,128)(2,1)S(1)} collective-permute-done((bf16[256,256]{1,0:T(8,128)(2,1)}, bf16[256,256]{1,0:T(8,128)(2,1)S(1)}, u32[]{:S(2)}, u32[]{:S(2)}) %collective-permute-start.1) | collective-permute-done | bytes 131104 | tf_op jit(solution)/shard_map/ppermute | solution.py:538
  7.5 0.7 pad_add_fusion
  8.2 2.7 %collective-permute-start.4 = (s32[2,16,32]{2,1,0:T(8,128)S(1)}, s32[2,16,32]{2,1,0:T(8,128)S(1)}, u32[]{:S(2)}, u32[]{:S(2)}) collective-permute-start(s32[2,16,32]{2,1,0:T(8,128)S(1)} %pad_add_fusion), channel_id=1, source_target_pairs={{0,8},{1,9},{2,10},{3,11},{4,12},{5,13},{6,14},{7,15},{8,0},{9,1},... | collective-permute-start | bytes 12296 | tf_op jit(solution)/shard_map/ppermute | solution.py:538
  11.0 0.5 broadcast.23
  11.5 1.3 %reduce.3 = s32[40]{0:T(128)S(1)} reduce(s32[1,40]{1,0:T(1,128)} %param.27, s32[]{:T(128)} %broadcast.23), dimensions={0}, to_apply=%param.27.reduce_sub_computation.3 | reduce | bytes 324 | tf_op args[13]
  13.0 2.0 %serve_rows.1 = bf16[4,128,256]{2,1,0:T(8,128)(2,1)} custom-call(s32[3]{0:T(128)S(1)} %pad_add_fusion.1.place_ref.core_ref, bf16[256,256]{1,0:T(8,128)(2,1)} %node_ref.3, bf16[256,256]{1,0:T(8,128)(2,1)S(1)} %collective-permute-done.refs_1_, bf16[256,256]{1,0:T(8,128)(2,1)S(1)} %collective-permute-done.1.refs_2_, ...), custom_call_target="tpu_custom_call" | custom-call | tf_op jit(solution)/shard_map/serve_rows/pallas_call | solution.py:73
  15.0 4.9 %all-to-all-start = ((bf16[4,128,256]{2,1,0:T(8,128)(2,1)}), bf16[4,128,256]{2,1,0:T(8,128)(2,1)S(1)}, u32[]{:S(2)}, u32[]{:S(2)}) async-start(bf16[4,128,256]{2,1,0:T(8,128)(2,1)} %serve_rows.1), calls=%async_computation | async-start | bytes 524288 | tf_op jit(solution)/shard_map/all_to_all | solution.py:553
  20.0 7.5 %prepare_edges.1 = (f32[4,256,1280]{2,1,0:T(8,128)}, bf16[4,256,1280]{2,1,0:T(8,128)(2,1)}) custom-call(bf16[5120,256]{1,0:T(8,128)(2,1)} %edge_ref.1, bf16[5120,256]{1,0:T(8,128)(2,1)} %cot_ref.3, s32[4,1,1280]{2,1,0:T(1,128)} %bitcast.15, bf16[256,256]{1,0:T(8,128)(2,1)} %node_ref.3, bf16[768,256]{1,0:T(8,128)(2,1)} %w_in_ref.4), custom_call_target="tpu_custom_call" | custom-call | flops 1342177280 | bytes 10485760 | tf_op jit(solution)/shard_map/prepare_edges/pallas_call | solution.py:108
  27.5 0.8 all-to-all-done
  28.3 15.7 %layer_backward.1 = (bf16[4,256,1280]{2,1,0:T(8,128)(2,1)}, f32[256,256]{1,0:T(8,128)S(1)}, bf16[8,152,256]{2,1,0:T(8,128)(2,1)S(1)}, bf16[8,152,256]{2,1,0:T(8,128)(2,1)S(1)}) custom-call(s32[3]{0:T(128)S(1)} %pad_add_fusion.1.place_ref.core_ref, f32[4,256,1280]{2,1,0:T(8,128)} %get-tuple-element.27.part_hbm, ...), custom_call_target="tpu_custom_call" | custom-call | tf_op jit(solution)/shard_map/layer_backward/pallas_call | solution.py:327
  44.0 0.7 copy-done.3
  44.7 2.0 %collective-permute-done.5.got_ref = bf16[8,152,256]{2,1,0:T(8,128)(2,1)S(1)} collective-permute-done((bf16[8,152,256]{2,1,0:T(8,128)(2,1)S(1)}, bf16[8,152,256]{2,1,0:T(8,128)(2,1)S(1)}, u32[]{:S(2)}, u32[]{:S(2)}) %collective-permute-start.5) | collective-permute-done | bytes 622624 | tf_op jit(solution)/shard_map/ppermute | solution.py:584
  46.8 1.0 %join_cores.1 = bf16[8,184,256]{2,1,0:T(8,128)(2,1)} custom-call(bf16[8,152,256]{2,1,0:T(8,128)(2,1)S(1)} %get-tuple-element.30.keep_ref, bf16[8,152,256]{2,1,0:T(8,128)(2,1)S(1)} %collective-permute-done.5.got_ref), custom_call_target="tpu_custom_call" | custom-call | tf_op jit(solution)/shard_map/join_cores/pallas_call | solution.py:405
  47.8 5.3 %all-to-all-start.1 = ((bf16[8,184,256]{2,1,0:T(8,128)(2,1)}), bf16[8,184,256]{2,1,0:T(8,128)(2,1)S(1)}, u32[]{:S(2)}, u32[]{:S(2)}) async-start(bf16[8,184,256]{2,1,0:T(8,128)(2,1)} %join_cores.1), calls=%async_computation.1 | async-start | bytes 1507328 | tf_op jit(solution)/shard_map/all_to_all | solution.py:586
  53.1 5.2 %edge_result.1 = bf16[5120,256]{1,0:T(8,128)(2,1)} custom-call(bf16[4,256,1280]{2,1,0:T(8,128)(2,1)} %get-tuple-element.32.grad_ref, bf16[5120,256]{1,0:T(8,128)(2,1)} %cot_ref.3, bf16[768,256]{1,0:T(8,128)(2,1)S(1)} %copy-done), custom_call_target="tpu_custom_call" | custom-call | flops 671088640 | bytes 7864320 | tf_op jit(solution)/shard_map/edge_result/pallas_call | solution.py:375
  58.2 14.6 %all-to-all-done.1.sums_ref.back_ref = bf16[8,184,256]{2,1,0:T(8,128)(2,1)S(1)} async-done(((bf16[8,184,256]{2,1,0:T(8,128)(2,1)}), bf16[8,184,256]{2,1,0:T(8,128)(2,1)S(1)}, u32[]{:S(2)}, u32[]{:S(2)}) %all-to-all-start.1) | async-done | bytes 753696 | tf_op jit(solution)/shard_map/all_to_all | solution.py:586
  72.8 0.8 total_piece.1
  73.7 3.6 %all-to-all-start.2 = ((bf16[8,120,256]{2,1,0:T(8,128)(2,1)}), bf16[8,120,256]{2,1,0:T(8,128)(2,1)S(1)}, u32[]{:S(2)}, u32[]{:S(2)}) async-start(bf16[8,120,256]{2,1,0:T(8,128)(2,1)} %total_piece.1), calls=%async_computation.2 | async-start | bytes 983040 | tf_op jit(solution)/shard_map/all_to_all | solution.py:592
  77.3 2.0 %settle_sums.1 = f32[256,256]{1,0:T(8,128)} custom-call(s32[3]{0:T(128)} %copy-done.10, bf16[8,184,256]{2,1,0:T(8,128)(2,1)S(1)} %all-to-all-done.1.sums_ref.back_ref, f32[256,256]{1,0:T(8,128)} %copy-done.3), custom_call_target="tpu_custom_call" | custom-call | tf_op jit(solution)/shard_map/settle_sums/pallas_call | solution.py:448
  79.3 12.0 %all-to-all-done.2.mine_ref = bf16[8,120,256]{2,1,0:T(8,128)(2,1)S(1)} async-done(((bf16[8,120,256]{2,1,0:T(8,128)(2,1)}), bf16[8,120,256]{2,1,0:T(8,128)(2,1)S(1)}, u32[]{:S(2)}, u32[]{:S(2)}) %all-to-all-start.2) | async-done | bytes 491552 | tf_op jit(solution)/shard_map/all_to_all | solution.py:592
  91.2 1.9 %collective-permute-done.6.theirs_ref = bf16[8,120,256]{2,1,0:T(8,128)(2,1)S(1)} collective-permute-done((bf16[8,120,256]{2,1,0:T(8,128)(2,1)S(1)}, bf16[8,120,256]{2,1,0:T(8,128)(2,1)S(1)}, u32[]{:S(2)}, u32[]{:S(2)}) %collective-permute-start.6) | collective-permute-done | bytes 491552 | tf_op jit(solution)/shard_map/ppermute | solution.py:597
  93.1 2.4 %assemble_sums.1 = (f32[768,256]{1,0:T(8,128)}, f32[256,256]{1,0:T(8,128)}, f32[512,256]{1,0:T(8,128)}, f32[256,256]{1,0:T(8,128)}, f32[1,256]{1,0:T(1,128)}, /*index=5*/f32[1,256]{1,0:T(1,128)}) custom-call(s32[3]{0:T(128)S(1)} %copy-done.11, bf16[8,120,256]{2,1,0:T(8,128)(2,1)S(1)} %all-to-all-done.2.mine_ref, ...), custom_call_target="tpu_custom_call" | custom-call | tf_op jit(solution)/shard_map/assemble_sums/pallas_call | solution.py:493
  (41 shorter events, 0.5 us)
Async XLA Ops:
  0.6 6.7 %collective-permute-start.1 = (bf16[256,256]{1,0:T(8,128)(2,1)}, bf16[256,256]{1,0:T(8,128)(2,1)S(1)}, u32[]{:S(2)}, u32[]{:S(2)}) collective-permute-start(bf16[256,256]{1,0:T(8,128)(2,1)} %node_ref.3), channel_id=1, source_target_pairs={{0,2},{1,3},{2,0},{3,1},{4,6},{5,7},{6,4},{7,5},{8,10},{9,11},{10,... | collective-permute-start | bytes 393224 | tf_op jit(solution)/shard_map/ppermute | solution.py:538
  3.7 9.3 %collective-permute-start = (bf16[256,256]{1,0:T(8,128)(2,1)}, bf16[256,256]{1,0:T(8,128)(2,1)S(1)}, u32[]{:S(2)}, u32[]{:S(2)}) collective-permute-start(bf16[256,256]{1,0:T(8,128)(2,1)} %node_ref.3), channel_id=1, source_target_pairs={{0,1},{1,0},{2,3},{3,2},{4,5},{5,4},{6,7},{7,6},{8,9},{9,8},{10,11... | collective-permute-start | bytes 393224 | tf_op jit(solution)/shard_map/ppermute | solution.py:538
  3.7 3.9 %collective-permute-start.3 = (s32[1,16,32]{2,1,0:T(8,128)}, s32[1,16,32]{2,1,0:T(8,128)S(1)}, u32[]{:S(2)}, u32[]{:S(2)}) collective-permute-start(s32[1,16,32]{2,1,0:T(8,128)} %refs_4_.1), channel_id=1, source_target_pairs={{0,4},{1,5},{2,6},{3,7},{4,0},{5,1},{6,2},{7,3},{8,12},{9,13},{10,... | collective-permute-start | bytes 6152 | tf_op jit(solution)/shard_map/ppermute | solution.py:538
  7.4 5.6 %collective-permute-start.2 = (bf16[256,256]{1,0:T(8,128)(2,1)S(1)}, bf16[256,256]{1,0:T(8,128)(2,1)S(1)}, u32[]{:S(2)}, u32[]{:S(2)}) collective-permute-start(bf16[256,256]{1,0:T(8,128)(2,1)S(1)} %collective-permute-done.1.refs_2_), channel_id=1, source_target_pairs={{0,1},{1,0},{2,3},{3,2},{4,5},{5,4},{6,7},{7,6},{8,9},{9,8},{10,11... | collective-permute-start | bytes 393224 | tf_op jit(solution)/shard_map/ppermute | solution.py:538
  8.2 4.8 %collective-permute-start.4 = (s32[2,16,32]{2,1,0:T(8,128)S(1)}, s32[2,16,32]{2,1,0:T(8,128)S(1)}, u32[]{:S(2)}, u32[]{:S(2)}) collective-permute-start(s32[2,16,32]{2,1,0:T(8,128)S(1)} %pad_add_fusion), channel_id=1, source_target_pairs={{0,8},{1,9},{2,10},{3,11},{4,12},{5,13},{6,14},{7,15},{8,0},{9,1},... | collective-permute-start | bytes 12296 | tf_op jit(solution)/shard_map/ppermute | solution.py:538
  11.0 17.3 %copy-start.10 = (s32[3]{0:T(128)}, s32[3]{0:T(128)S(1)}, u32[]{:S(2)}) copy-start(s32[3]{0:T(128)S(1)} %pad_add_fusion.1.place_ref.core_ref) | copy-start | bytes 40
  15.0 13.2 %all-to-all-start = ((bf16[4,128,256]{2,1,0:T(8,128)(2,1)}), bf16[4,128,256]{2,1,0:T(8,128)(2,1)S(1)}, u32[]{:S(2)}, u32[]{:S(2)}) async-start(bf16[4,128,256]{2,1,0:T(8,128)(2,1)} %serve_rows.1), calls=%async_computation | async-start | bytes 524288 | tf_op jit(solution)/shard_map/all_to_all | solution.py:553
  19.9 8.4 %copy-start = (bf16[768,256]{1,0:T(8,128)(2,1)S(1)}, bf16[768,256]{1,0:T(8,128)(2,1)}, u32[]{:S(2)}) copy-start(bf16[768,256]{1,0:T(8,128)(2,1)} %w_in_ref.4) | copy-start | bytes 1179652
  19.9 8.4 %copy-start.1 = (bf16[256,256]{1,0:T(8,128)(2,1)S(1)}, bf16[256,256]{1,0:T(8,128)(2,1)}, u32[]{:S(2)}) copy-start(bf16[256,256]{1,0:T(8,128)(2,1)} %node_ref.3) | copy-start | bytes 393220
  19.9 8.4 %copy-start.2 = (bf16[512,256]{1,0:T(8,128)(2,1)S(1)}, bf16[512,256]{1,0:T(8,128)(2,1)}, u32[]{:S(2)}) copy-start(bf16[512,256]{1,0:T(8,128)(2,1)} %w_node_in_ref.1) | copy-start | bytes 786436
  19.9 8.4 %copy-start.4 = (bf16[256,256]{1,0:T(8,128)(2,1)S(1)}, bf16[256,256]{1,0:T(8,128)(2,1)}, u32[]{:S(2)}) copy-start(bf16[256,256]{1,0:T(8,128)(2,1)} %node_cot_ref.1) | copy-start | bytes 393220
  19.9 8.4 %copy-start.5 = (bf16[256,256]{1,0:T(8,128)(2,1)S(1)}, bf16[256,256]{1,0:T(8,128)(2,1)}, u32[]{:S(2)}) copy-start(bf16[256,256]{1,0:T(8,128)(2,1)} %w_out_ref.1) | copy-start | bytes 393220
  19.9 8.4 %copy-start.6 = (bf16[256,256]{1,0:T(8,128)(2,1)S(1)}, bf16[256,256]{1,0:T(8,128)(2,1)}, u32[]{:S(2)}) copy-start(bf16[256,256]{1,0:T(8,128)(2,1)} %w_node_out_ref.1) | copy-start | bytes 393220
  19.9 8.3 %copy-start.7 = (s32[5120]{0:T(1024)S(1)}, s32[5120]{0:T(1024)}, u32[]{:S(2)}) copy-start(s32[5120]{0:T(1024)} %param.26) | copy-start | bytes 61444
  20.0 8.3 %copy-start.8 = (s32[1,16,32]{2,1,0:T(8,128)S(1)}, s32[1,16,32]{2,1,0:T(8,128)}, u32[]{:S(2)}) copy-start(s32[1,16,32]{2,1,0:T(8,128)} %refs_4_.1) | copy-start | bytes 6148
  20.0 8.3 %copy-start.9 = (s32[5120]{0:T(1024)S(1)}, s32[5120]{0:T(1024)}, u32[]{:S(2)}) copy-start(s32[5120]{0:T(1024)} %param.25) | copy-start | bytes 61444
  20.0 8.3 %copy-start.12 = (f32[256]{0:T(256)S(1)}, f32[256]{0:T(256)}, u32[]{:S(2)}) copy-start(f32[256]{0:T(256)} %param.20) | copy-start | bytes 3076
  20.0 8.3 %copy-start.13 = (f32[256]{0:T(256)S(1)}, f32[256]{0:T(256)}, u32[]{:S(2)}) copy-start(f32[256]{0:T(256)} %param.23) | copy-start | bytes 3076
  44.0 0.7 copy-start.3
  44.7 2.1 %collective-permute-start.5 = (bf16[8,152,256]{2,1,0:T(8,128)(2,1)S(1)}, bf16[8,152,256]{2,1,0:T(8,128)(2,1)S(1)}, u32[]{:S(2)}, u32[]{:S(2)}) collective-permute-start(bf16[8,152,256]{2,1,0:T(8,128)(2,1)S(1)} %get-tuple-element.31), channel_id=1, source_target_pairs={{0,1},{1,0},{2,3},{3,2},{4,5},{5,4},{6,7},{7,6},{8,9},{9,8},{10,11... | collective-permute-start | bytes 1867784 | tf_op jit(solution)/shard_map/ppermute | solution.py:584
  47.8 25.1 %all-to-all-start.1 = ((bf16[8,184,256]{2,1,0:T(8,128)(2,1)}), bf16[8,184,256]{2,1,0:T(8,128)(2,1)S(1)}, u32[]{:S(2)}, u32[]{:S(2)}) async-start(bf16[8,184,256]{2,1,0:T(8,128)(2,1)} %join_cores.1), calls=%async_computation.1 | async-start | bytes 1507328 | tf_op jit(solution)/shard_map/all_to_all | solution.py:586
  58.2 34.9 %copy-start.11 = (s32[3]{0:T(128)S(1)}, s32[3]{0:T(128)}, u32[]{:S(2)}) copy-start(s32[3]{0:T(128)} %copy-done.10) | copy-start | bytes 40
  73.7 17.6 %all-to-all-start.2 = ((bf16[8,120,256]{2,1,0:T(8,128)(2,1)}), bf16[8,120,256]{2,1,0:T(8,128)(2,1)S(1)}, u32[]{:S(2)}, u32[]{:S(2)}) async-start(bf16[8,120,256]{2,1,0:T(8,128)(2,1)} %total_piece.1), calls=%async_computation.2 | async-start | bytes 983040 | tf_op jit(solution)/shard_map/all_to_all | solution.py:592
  91.2 1.9 %collective-permute-start.6 = (bf16[8,120,256]{2,1,0:T(8,128)(2,1)S(1)}, bf16[8,120,256]{2,1,0:T(8,128)(2,1)S(1)}, u32[]{:S(2)}, u32[]{:S(2)}) collective-permute-start(bf16[8,120,256]{2,1,0:T(8,128)(2,1)S(1)} %all-to-all-done.2.mine_ref), channel_id=1, source_target_pairs={{0,1},{1,0},{2,3},{3,2},{4,5},{5,4},{6,7},{7,6},{8,9},{9,8},{10,11... | collective-permute-start | bytes 1474568 | tf_op jit(solution)/shard_map/ppermute | solution.py:597

commit v7 on v6

--- a/solution.py
+++ b/solution.py
@@ -328,7 +328,7 @@
         functools.partial(layer_kernel, piece_rows),
         out_shape=[
             pltpu.HBM((chunks, hidden, width), BF),
-            jax.ShapeDtypeStruct((nodes, latent), F32),
+            pltpu.VMEM((nodes, latent), F32),
             pltpu.VMEM((bands // 2, cap + piece_rows + TAIL, latent), BF),
             pltpu.VMEM((bands // 2, cap + piece_rows + TAIL, latent), BF),
         ],
@@ -451,7 +451,7 @@
         in_specs=[pl.BlockSpec(memory_space=pltpu.SMEM)] + [vmem()] * 2,
         out_specs=vmem(),
         name="settle_sums",
-    )(place, in_vmem(back), node_local)
+    )(place, in_vmem(back), in_vmem(node_local))
 
 
 def assemble_kernel(core_ref, mine_ref, theirs_ref, *refs):

time: 96.2 us -> 95.5 us (level)
  no operation moved by 1% of the time
where the time goes in v7:
time: 95.5 us; the launch traced here: 94.9 us
  Pallas kernels  36.2 us (38%)
  waiting for transfers between devices  33.8 us (35%)
  starting transfers between devices  21.1 us (22%)
  other arithmetic  2.12 us (2%)
    pallas_call x1, Pallas kernels, layer(): pl.pallas_call(functools.partial(layer_kernel, piece_rows), out_shape=[pl...  15.7 us
    all_to_all x1, waiting for transfers between devices, per_device(): lax.all_to_all(joined, 'band', split_axis=0, concat_axis=0, tiled=True, a...  14.6 us
    all_to_all x1, waiting for transfers between devices, per_device(): lax.all_to_all(pieces, 'band', split_axis=0, concat_axis=0, tiled=True, a...  12.3 us
    pallas_call x1, Pallas kernels, prepare(): pl.pallas_call(prepare_kernel, grid=(chunks,), out_shape=[pltpu.HBM((chun...  7.46 us
    ppermute x5, starting transfers between devices, swap(): return lax.ppermute(array, 'band', [(i, i ^ step) for i in range(bands)])  7.27 us
    all_to_all x1, starting transfers between devices, per_device(): lax.all_to_all(joined, 'band', split_axis=0, concat_axis=0, tiled=True, a...  5.31 us
    pallas_call x1, Pallas kernels, edge_result(): pl.pallas_call(edge_kernel, grid=(chunks,), out_shape=jax.ShapeDtypeStruc...  5.15 us
    all_to_all x1, starting transfers between devices, per_device(): lax.all_to_all(rows, 'band', split_axis=0, concat_axis=0, tiled=True, axi...  4.85 us
  transfers between devices with their start and end apart: 10, of which 7 were waited for; matrix products, arithmetic and copies ran while one was open for 3% of the time, Pallas kernels for 15%

profile of v7, /device:TPU:0, one launch (start us, length us, event | category | flops | bytes accessed | tf_op | source)
XLA Modules:
  0.0 94.9 jit_solution(4386761407581540541)
XLA Ops:
  0.6 3.0 %collective-permute-start.1 = (bf16[256,256]{1,0:T(8,128)(2,1)}, bf16[256,256]{1,0:T(8,128)(2,1)S(1)}, u32[]{:S(2)}, u32[]{:S(2)}) collective-permute-start(bf16[256,256]{1,0:T(8,128)(2,1)} %node_ref.3), channel_id=1, source_target_pairs={{0,2},{1,3},{2,0},{3,1},{4,6},{5,7},{6,4},{7,5},{8,10},{9,11},{10,... | collective-permute-start | bytes 393224 | tf_op jit(solution)/shard_map/ppermute | solution.py:538
  3.7 1.6 %collective-permute-start.3 = (s32[1,16,32]{2,1,0:T(8,128)}, s32[1,16,32]{2,1,0:T(8,128)S(1)}, u32[]{:S(2)}, u32[]{:S(2)}) collective-permute-start(s32[1,16,32]{2,1,0:T(8,128)} %refs_4_.1), channel_id=1, source_target_pairs={{0,4},{1,5},{2,6},{3,7},{4,0},{5,1},{6,2},{7,3},{8,12},{9,13},{10,... | collective-permute-start | bytes 6152 | tf_op jit(solution)/shard_map/ppermute | solution.py:538
  5.2 2.1 %collective-permute-done.1.refs_2_ = bf16[256,256]{1,0:T(8,128)(2,1)S(1)} collective-permute-done((bf16[256,256]{1,0:T(8,128)(2,1)}, bf16[256,256]{1,0:T(8,128)(2,1)S(1)}, u32[]{:S(2)}, u32[]{:S(2)}) %collective-permute-start.1) | collective-permute-done | bytes 131104 | tf_op jit(solution)/shard_map/ppermute | solution.py:538
  7.4 0.2 collective-permute-done.3.refs_5_
  7.5 0.7 pad_add_fusion
  8.2 2.7 %collective-permute-start.4 = (s32[2,16,32]{2,1,0:T(8,128)S(1)}, s32[2,16,32]{2,1,0:T(8,128)S(1)}, u32[]{:S(2)}, u32[]{:S(2)}) collective-permute-start(s32[2,16,32]{2,1,0:T(8,128)S(1)} %pad_add_fusion), channel_id=1, source_target_pairs={{0,8},{1,9},{2,10},{3,11},{4,12},{5,13},{6,14},{7,15},{8,0},{9,1},... | collective-permute-start | bytes 12296 | tf_op jit(solution)/shard_map/ppermute | solution.py:538
  11.0 0.5 broadcast.23
  11.5 1.3 %reduce.3 = s32[40]{0:T(128)S(1)} reduce(s32[1,40]{1,0:T(1,128)} %param.27, s32[]{:T(128)} %broadcast.23), dimensions={0}, to_apply=%param.27.reduce_sub_computation.3 | reduce | bytes 324 | tf_op args[13]
  13.0 2.0 %serve_rows.1 = bf16[4,128,256]{2,1,0:T(8,128)(2,1)} custom-call(s32[3]{0:T(128)S(1)} %pad_add_fusion.1.place_ref.core_ref, bf16[256,256]{1,0:T(8,128)(2,1)} %node_ref.3, bf16[256,256]{1,0:T(8,128)(2,1)S(1)} %collective-permute-done.refs_1_, bf16[256,256]{1,0:T(8,128)(2,1)S(1)} %collective-permute-done.1.refs_2_, ...), custom_call_target="tpu_custom_call" | custom-call | tf_op jit(solution)/shard_map/serve_rows/pallas_call | solution.py:73
  15.0 4.9 %all-to-all-start = ((bf16[4,128,256]{2,1,0:T(8,128)(2,1)}), bf16[4,128,256]{2,1,0:T(8,128)(2,1)S(1)}, u32[]{:S(2)}, u32[]{:S(2)}) async-start(bf16[4,128,256]{2,1,0:T(8,128)(2,1)} %serve_rows.1), calls=%async_computation | async-start | bytes 524288 | tf_op jit(solution)/shard_map/all_to_all | solution.py:553
  20.0 7.5 %prepare_edges.1 = (f32[4,256,1280]{2,1,0:T(8,128)}, bf16[4,256,1280]{2,1,0:T(8,128)(2,1)}) custom-call(bf16[5120,256]{1,0:T(8,128)(2,1)} %edge_ref.1, bf16[5120,256]{1,0:T(8,128)(2,1)} %cot_ref.3, s32[4,1,1280]{2,1,0:T(1,128)} %bitcast.15, bf16[256,256]{1,0:T(8,128)(2,1)} %node_ref.3, bf16[768,256]{1,0:T(8,128)(2,1)} %w_in_ref.4), custom_call_target="tpu_custom_call" | custom-call | flops 1342177280 | bytes 10485760 | tf_op jit(solution)/shard_map/prepare_edges/pallas_call | solution.py:108
  27.5 0.8 all-to-all-done
  28.3 15.7 %layer_backward.1 = (bf16[4,256,1280]{2,1,0:T(8,128)(2,1)}, f32[256,256]{1,0:T(8,128)S(1)}, bf16[8,152,256]{2,1,0:T(8,128)(2,1)S(1)}, bf16[8,152,256]{2,1,0:T(8,128)(2,1)S(1)}) custom-call(s32[3]{0:T(128)S(1)} %pad_add_fusion.1.place_ref.core_ref, f32[4,256,1280]{2,1,0:T(8,128)} %get-tuple-element.27.part_hbm, ...), custom_call_target="tpu_custom_call" | custom-call | tf_op jit(solution)/shard_map/layer_backward/pallas_call | solution.py:327
  44.1 2.0 %collective-permute-done.5.got_ref = bf16[8,152,256]{2,1,0:T(8,128)(2,1)S(1)} collective-permute-done((bf16[8,152,256]{2,1,0:T(8,128)(2,1)S(1)}, bf16[8,152,256]{2,1,0:T(8,128)(2,1)S(1)}, u32[]{:S(2)}, u32[]{:S(2)}) %collective-permute-start.5) | collective-permute-done | bytes 622624 | tf_op jit(solution)/shard_map/ppermute | solution.py:584
  46.1 1.0 %join_cores.1 = bf16[8,184,256]{2,1,0:T(8,128)(2,1)} custom-call(bf16[8,152,256]{2,1,0:T(8,128)(2,1)S(1)} %get-tuple-element.30.keep_ref, bf16[8,152,256]{2,1,0:T(8,128)(2,1)S(1)} %collective-permute-done.5.got_ref), custom_call_target="tpu_custom_call" | custom-call | tf_op jit(solution)/shard_map/join_cores/pallas_call | solution.py:405
  47.1 5.3 %all-to-all-start.1 = ((bf16[8,184,256]{2,1,0:T(8,128)(2,1)}), bf16[8,184,256]{2,1,0:T(8,128)(2,1)S(1)}, u32[]{:S(2)}, u32[]{:S(2)}) async-start(bf16[8,184,256]{2,1,0:T(8,128)(2,1)} %join_cores.1), calls=%async_computation.1 | async-start | bytes 1507328 | tf_op jit(solution)/shard_map/all_to_all | solution.py:586
  52.4 5.2 %edge_result.1 = bf16[5120,256]{1,0:T(8,128)(2,1)} custom-call(bf16[4,256,1280]{2,1,0:T(8,128)(2,1)} %get-tuple-element.32.grad_ref, bf16[5120,256]{1,0:T(8,128)(2,1)} %cot_ref.3, bf16[768,256]{1,0:T(8,128)(2,1)S(1)} %copy-done), custom_call_target="tpu_custom_call" | custom-call | flops 671088640 | bytes 7864320 | tf_op jit(solution)/shard_map/edge_result/pallas_call | solution.py:375
  57.6 14.6 %all-to-all-done.1.sums_ref.back_ref = bf16[8,184,256]{2,1,0:T(8,128)(2,1)S(1)} async-done(((bf16[8,184,256]{2,1,0:T(8,128)(2,1)}), bf16[8,184,256]{2,1,0:T(8,128)(2,1)S(1)}, u32[]{:S(2)}, u32[]{:S(2)}) %all-to-all-start.1) | async-done | bytes 753696 | tf_op jit(solution)/shard_map/all_to_all | solution.py:586
  72.2 0.8 total_piece.1
  73.0 3.6 %all-to-all-start.2 = ((bf16[8,120,256]{2,1,0:T(8,128)(2,1)}), bf16[8,120,256]{2,1,0:T(8,128)(2,1)S(1)}, u32[]{:S(2)}, u32[]{:S(2)}) async-start(bf16[8,120,256]{2,1,0:T(8,128)(2,1)} %total_piece.1), calls=%async_computation.2 | async-start | bytes 983040 | tf_op jit(solution)/shard_map/all_to_all | solution.py:592
  76.6 1.7 %settle_sums.1 = f32[256,256]{1,0:T(8,128)} custom-call(s32[3]{0:T(128)} %copy-done.9, bf16[8,184,256]{2,1,0:T(8,128)(2,1)S(1)} %all-to-all-done.1.sums_ref.back_ref, f32[256,256]{1,0:T(8,128)S(1)} %get-tuple-element.34.local_ref), custom_call_target="tpu_custom_call" | custom-call | tf_op jit(solution)/shard_map/settle_sums/pallas_call | solution.py:448
  78.3 12.3 %all-to-all-done.2.mine_ref = bf16[8,120,256]{2,1,0:T(8,128)(2,1)S(1)} async-done(((bf16[8,120,256]{2,1,0:T(8,128)(2,1)}), bf16[8,120,256]{2,1,0:T(8,128)(2,1)S(1)}, u32[]{:S(2)}, u32[]{:S(2)}) %all-to-all-start.2) | async-done | bytes 491552 | tf_op jit(solution)/shard_map/all_to_all | solution.py:592
  90.6 1.9 %collective-permute-done.6.theirs_ref = bf16[8,120,256]{2,1,0:T(8,128)(2,1)S(1)} collective-permute-done((bf16[8,120,256]{2,1,0:T(8,128)(2,1)S(1)}, bf16[8,120,256]{2,1,0:T(8,128)(2,1)S(1)}, u32[]{:S(2)}, u32[]{:S(2)}) %collective-permute-start.6) | collective-permute-done | bytes 491552 | tf_op jit(solution)/shard_map/ppermute | solution.py:597
  92.5 2.4 %assemble_sums.1 = (f32[768,256]{1,0:T(8,128)}, f32[256,256]{1,0:T(8,128)}, f32[512,256]{1,0:T(8,128)}, f32[256,256]{1,0:T(8,128)}, f32[1,256]{1,0:T(1,128)}, /*index=5*/f32[1,256]{1,0:T(1,128)}) custom-call(s32[3]{0:T(128)S(1)} %copy-done.10, bf16[8,120,256]{2,1,0:T(8,128)(2,1)S(1)} %all-to-all-done.2.mine_ref, ...), custom_call_target="tpu_custom_call" | custom-call | tf_op jit(solution)/shard_map/assemble_sums/pallas_call | solution.py:493
  (39 shorter events, 0.4 us)
Async XLA Ops:
  0.6 6.7 %collective-permute-start.1 = (bf16[256,256]{1,0:T(8,128)(2,1)}, bf16[256,256]{1,0:T(8,128)(2,1)S(1)}, u32[]{:S(2)}, u32[]{:S(2)}) collective-permute-start(bf16[256,256]{1,0:T(8,128)(2,1)} %node_ref.3), channel_id=1, source_target_pairs={{0,2},{1,3},{2,0},{3,1},{4,6},{5,7},{6,4},{7,5},{8,10},{9,11},{10,... | collective-permute-start | bytes 393224 | tf_op jit(solution)/shard_map/ppermute | solution.py:538
  3.7 9.3 %collective-permute-start = (bf16[256,256]{1,0:T(8,128)(2,1)}, bf16[256,256]{1,0:T(8,128)(2,1)S(1)}, u32[]{:S(2)}, u32[]{:S(2)}) collective-permute-start(bf16[256,256]{1,0:T(8,128)(2,1)} %node_ref.3), channel_id=1, source_target_pairs={{0,1},{1,0},{2,3},{3,2},{4,5},{5,4},{6,7},{7,6},{8,9},{9,8},{10,11... | collective-permute-start | bytes 393224 | tf_op jit(solution)/shard_map/ppermute | solution.py:538
  3.7 3.9 %collective-permute-start.3 = (s32[1,16,32]{2,1,0:T(8,128)}, s32[1,16,32]{2,1,0:T(8,128)S(1)}, u32[]{:S(2)}, u32[]{:S(2)}) collective-permute-start(s32[1,16,32]{2,1,0:T(8,128)} %refs_4_.1), channel_id=1, source_target_pairs={{0,4},{1,5},{2,6},{3,7},{4,0},{5,1},{6,2},{7,3},{8,12},{9,13},{10,... | collective-permute-start | bytes 6152 | tf_op jit(solution)/shard_map/ppermute | solution.py:538
  7.4 5.6 %collective-permute-start.2 = (bf16[256,256]{1,0:T(8,128)(2,1)S(1)}, bf16[256,256]{1,0:T(8,128)(2,1)S(1)}, u32[]{:S(2)}, u32[]{:S(2)}) collective-permute-start(bf16[256,256]{1,0:T(8,128)(2,1)S(1)} %collective-permute-done.1.refs_2_), channel_id=1, source_target_pairs={{0,1},{1,0},{2,3},{3,2},{4,5},{5,4},{6,7},{7,6},{8,9},{9,8},{10,11... | collective-permute-start | bytes 393224 | tf_op jit(solution)/shard_map/ppermute | solution.py:538
  8.2 4.8 %collective-permute-start.4 = (s32[2,16,32]{2,1,0:T(8,128)S(1)}, s32[2,16,32]{2,1,0:T(8,128)S(1)}, u32[]{:S(2)}, u32[]{:S(2)}) collective-permute-start(s32[2,16,32]{2,1,0:T(8,128)S(1)} %pad_add_fusion), channel_id=1, source_target_pairs={{0,8},{1,9},{2,10},{3,11},{4,12},{5,13},{6,14},{7,15},{8,0},{9,1},... | collective-permute-start | bytes 12296 | tf_op jit(solution)/shard_map/ppermute | solution.py:538
  11.0 17.3 %copy-start.9 = (s32[3]{0:T(128)}, s32[3]{0:T(128)S(1)}, u32[]{:S(2)}) copy-start(s32[3]{0:T(128)S(1)} %pad_add_fusion.1.place_ref.core_ref) | copy-start | bytes 40
  15.0 13.2 %all-to-all-start = ((bf16[4,128,256]{2,1,0:T(8,128)(2,1)}), bf16[4,128,256]{2,1,0:T(8,128)(2,1)S(1)}, u32[]{:S(2)}, u32[]{:S(2)}) async-start(bf16[4,128,256]{2,1,0:T(8,128)(2,1)} %serve_rows.1), calls=%async_computation | async-start | bytes 524288 | tf_op jit(solution)/shard_map/all_to_all | solution.py:553
  19.9 8.4 %copy-start = (bf16[768,256]{1,0:T(8,128)(2,1)S(1)}, bf16[768,256]{1,0:T(8,128)(2,1)}, u32[]{:S(2)}) copy-start(bf16[768,256]{1,0:T(8,128)(2,1)} %w_in_ref.4) | copy-start | bytes 1179652
  19.9 8.4 %copy-start.1 = (bf16[256,256]{1,0:T(8,128)(2,1)S(1)}, bf16[256,256]{1,0:T(8,128)(2,1)}, u32[]{:S(2)}) copy-start(bf16[256,256]{1,0:T(8,128)(2,1)} %node_ref.3) | copy-start | bytes 393220
  19.9 8.4 %copy-start.2 = (bf16[512,256]{1,0:T(8,128)(2,1)S(1)}, bf16[512,256]{1,0:T(8,128)(2,1)}, u32[]{:S(2)}) copy-start(bf16[512,256]{1,0:T(8,128)(2,1)} %w_node_in_ref.1) | copy-start | bytes 786436
  19.9 8.4 %copy-start.3 = (bf16[256,256]{1,0:T(8,128)(2,1)S(1)}, bf16[256,256]{1,0:T(8,128)(2,1)}, u32[]{:S(2)}) copy-start(bf16[256,256]{1,0:T(8,128)(2,1)} %node_cot_ref.1) | copy-start | bytes 393220
  19.9 8.4 %copy-start.4 = (bf16[256,256]{1,0:T(8,128)(2,1)S(1)}, bf16[256,256]{1,0:T(8,128)(2,1)}, u32[]{:S(2)}) copy-start(bf16[256,256]{1,0:T(8,128)(2,1)} %w_out_ref.1) | copy-start | bytes 393220
  19.9 8.4 %copy-start.5 = (bf16[256,256]{1,0:T(8,128)(2,1)S(1)}, bf16[256,256]{1,0:T(8,128)(2,1)}, u32[]{:S(2)}) copy-start(bf16[256,256]{1,0:T(8,128)(2,1)} %w_node_out_ref.1) | copy-start | bytes 393220
  19.9 8.3 %copy-start.6 = (s32[5120]{0:T(1024)S(1)}, s32[5120]{0:T(1024)}, u32[]{:S(2)}) copy-start(s32[5120]{0:T(1024)} %param.26) | copy-start | bytes 61444
  20.0 8.3 %copy-start.7 = (s32[1,16,32]{2,1,0:T(8,128)S(1)}, s32[1,16,32]{2,1,0:T(8,128)}, u32[]{:S(2)}) copy-start(s32[1,16,32]{2,1,0:T(8,128)} %refs_4_.1) | copy-start | bytes 6148
  20.0 8.3 %copy-start.8 = (s32[5120]{0:T(1024)S(1)}, s32[5120]{0:T(1024)}, u32[]{:S(2)}) copy-start(s32[5120]{0:T(1024)} %param.25) | copy-start | bytes 61444
  20.0 8.3 %copy-start.11 = (f32[256]{0:T(256)S(1)}, f32[256]{0:T(256)}, u32[]{:S(2)}) copy-start(f32[256]{0:T(256)} %param.20) | copy-start | bytes 3076
  20.0 8.3 %copy-start.12 = (f32[256]{0:T(256)S(1)}, f32[256]{0:T(256)}, u32[]{:S(2)}) copy-start(f32[256]{0:T(256)} %param.23) | copy-start | bytes 3076
  44.0 2.1 %collective-permute-start.5 = (bf16[8,152,256]{2,1,0:T(8,128)(2,1)S(1)}, bf16[8,152,256]{2,1,0:T(8,128)(2,1)S(1)}, u32[]{:S(2)}, u32[]{:S(2)}) collective-permute-start(bf16[8,152,256]{2,1,0:T(8,128)(2,1)S(1)} %get-tuple-element.31), channel_id=1, source_target_pairs={{0,1},{1,0},{2,3},{3,2},{4,5},{5,4},{6,7},{7,6},{8,9},{9,8},{10,11... | collective-permute-start | bytes 1867784 | tf_op jit(solution)/shard_map/ppermute | solution.py:584
  47.1 25.1 %all-to-all-start.1 = ((bf16[8,184,256]{2,1,0:T(8,128)(2,1)}), bf16[8,184,256]{2,1,0:T(8,128)(2,1)S(1)}, u32[]{:S(2)}, u32[]{:S(2)}) async-start(bf16[8,184,256]{2,1,0:T(8,128)(2,1)} %join_cores.1), calls=%async_computation.1 | async-start | bytes 1507328 | tf_op jit(solution)/shard_map/all_to_all | solution.py:586
  57.6 34.9 %copy-start.10 = (s32[3]{0:T(128)S(1)}, s32[3]{0:T(128)}, u32[]{:S(2)}) copy-start(s32[3]{0:T(128)} %copy-done.9) | copy-start | bytes 40
  73.0 17.6 %all-to-all-start.2 = ((bf16[8,120,256]{2,1,0:T(8,128)(2,1)}), bf16[8,120,256]{2,1,0:T(8,128)(2,1)S(1)}, u32[]{:S(2)}, u32[]{:S(2)}) async-start(bf16[8,120,256]{2,1,0:T(8,128)(2,1)} %total_piece.1), calls=%async_computation.2 | async-start | bytes 983040 | tf_op jit(solution)/shard_map/all_to_all | solution.py:592
  90.6 1.9 %collective-permute-start.6 = (bf16[8,120,256]{2,1,0:T(8,128)(2,1)S(1)}, bf16[8,120,256]{2,1,0:T(8,128)(2,1)S(1)}, u32[]{:S(2)}, u32[]{:S(2)}) collective-permute-start(bf16[8,120,256]{2,1,0:T(8,128)(2,1)S(1)} %all-to-all-done.2.mine_ref), channel_id=1, source_target_pairs={{0,1},{1,0},{2,3},{3,2},{4,5},{5,4},{6,7},{7,6},{8,9},{9,8},{10,11... | collective-permute-start | bytes 1474568 | tf_op jit(solution)/shard_map/ppermute | solution.py:597
